TPU v7x, 32 devices: a whole 2x2x4 slice. The times are simulated.
32 devices in a mesh: chrom: 2 (over x), samp: 16 (over z, y, core).
Axes of the slice: x: 2, y: 2, z: 4, core: 2. Of those that a mesh axis runs over, the one named last changes fastest.
Arguments:
- genotypes: int32 [6144, 6144], P('samp', 'chrom'), may hold values from 0 to 2, as said below
- frequency: float32 [6144], P('chrom'), may hold values from 0.05 to 0.5, as said below
- widths: int32 [8], replicated, may hold values from 1 to 1536, 6144 in all
- ridge_term: float32 [1], replicated, may hold values from 0.5 to 1.5
- direction: float32 [6144, 64], P('samp'), may hold values from -6 to 6
Outputs:
- loco_out: float32 [8, 6144, 64], P('chrom', 'samp')
Inputs may be any that keep to these rules, and one draw needn't show every extreme that they name: Each variant's allele frequency is a whole number of thousandths. `genotypes`: each dosage, apart from samples 0 and 1 at variant 0 (set to 2 and 0), is the sum of two independent draws that are 1 with the variant's allele frequency and 0 otherwise. The 8 widths sum to 6144.
All inputs are finite; a program needn't handle non-finite values.
Results may differ from a plain program's by a relative error of at most 0.004.
Values may be sent and summed in bfloat16 or wider, within the bound.
No kernel may reach another device: no remote copies, remote signals or barrier semaphores. Data moves between devices by JAX's collectives and lax.ppermute only.
A program may use at most 64 MiB of HBM per device.

v0:
```python
import jax
import jax.numpy as jnp
from jax import lax
from jax.sharding import PartitionSpec as P


def on_device(genotypes, frequency, widths, ridge_term, direction):
    local_vars = genotypes.shape[1]
    sample_rows = genotypes.shape[0]
    sections_all = widths.shape[0]
    rhs_count = direction.shape[1]
    doubled = 2.0 * frequency
    standard = (
        (genotypes.astype(jnp.float32) - doubled) * lax.rsqrt(doubled * (1.0 - frequency))
    ).astype(jnp.bfloat16)
    vector = direction.astype(jnp.bfloat16)
    first_var = lax.axis_index("chrom") * local_vars
    section_ends = jnp.cumsum(widths)
    var_index = first_var + jnp.arange(local_vars, dtype=jnp.int32)
    section = jnp.sum((var_index[:, None] >= section_ends[None, :]).astype(jnp.int32), axis=1)
    onehot = (section[:, None] == jnp.arange(sections_all, dtype=jnp.int32)[None, :]).astype(
        jnp.bfloat16
    )
    contract = (((0,), (0,)), ((), ()))
    crossed = lax.psum(
        lax.dot_general(standard, vector, contract, preferred_element_type=jnp.float32), "samp"
    )
    shared = crossed.astype(jnp.bfloat16)
    spread = (shared[:, None, :] * onehot[:, :, None]).reshape(local_vars, sections_all * rhs_count)
    partial_value = jnp.dot(standard, spread, preferred_element_type=jnp.float32)
    per_device = sections_all // lax.axis_size("chrom")
    first_section = lax.axis_index("chrom") * per_device
    by_section = partial_value.reshape(sample_rows, sections_all, rhs_count)
    summed = lax.psum(by_section, "chrom")
    all_total = jnp.sum(summed, axis=1)
    own_sums = lax.dynamic_slice_in_dim(summed, first_section, per_device, 1)
    variant_total = local_vars * lax.axis_size("chrom")
    own_widths = lax.dynamic_slice_in_dim(widths, first_section, per_device, 0)
    divisor = (variant_total - own_widths).astype(jnp.float32)
    result = (
        ridge_term[0] * direction[:, None, :]
        + (all_total[:, None, :] - own_sums) / divisor[None, :, None]
    )
    return jnp.transpose(result, (1, 0, 2))


def solution(mesh):
    return jax.shard_map(
        on_device,
        mesh=mesh,
        in_specs=(P("samp", "chrom"), P("chrom"), P(), P(), P("samp", None)),
        out_specs=P("chrom", "samp", None),
        check_vma=False,
    )
```

profile of v0, /device:TPU:0, one launch (start us, length us, event | category | flops | bytes accessed | tf_op | source)
XLA Modules:
  0.0 128.9 jit_solution(11766750784579875503)
XLA Ops:
  6.5 0.0 copy-start.1
  6.5 0.0 all-reduce.3.cloned.1.call-start
  6.5 0.7 broadcast_multiply_fusion.1
  7.3 3.2 %fusion.6 = f32[3072,64]{0,1:T(8,128)S(1)} fusion(s32[384,3072]{1,0:T(8,128)} %param.5, f32[3072]{0:T(1024)S(1)} %get-tuple-element.6, f32[3072]{0:T(1024)S(1)} %get-tuple-element.5, f32[384,64]{0,1:T(8,128)} %param.9), kind=kOutput, calls=%fused_computation.7 | convolution fusion | flops 155738112 | bytes 5627904 | tf_op jit(solution)/shard_map/dot_general | solution.py:26
  10.5 71.3 %all-reduce.4 = bf16[3072,64]{0,1:T(8,128)(2,1)S(1)} all-reduce(f32[3072,64]{0,1:T(8,128)S(1)} %fusion.6), channel_id=1, replica_groups=mesh['chrom'=2,'samp'=16] {'samp'}, use_global_device_ids=true, to_apply=%region_0.0 | all-reduce | flops 196608 | bytes 1179648 | tf_op jit(solution)/shard_map/psum | solution.py:25
  81.8 0.0 copy-done.1
  81.8 0.2 reduce-window.8
  82.0 0.1 convert_reduce_fusion
  82.1 0.0 copy-start
  82.1 5.1 %fusion = f32[384,8,64]{0,2,1:T(8,128)} fusion(bf16[3072,8]{0,1:T(8,128)(2,1)S(1)} %fusion.7, bf16[3072,64]{0,1:T(8,128)(2,1)S(1)} %all-reduce.4, s32[384,3072]{1,0:T(8,128)} %param.5, f32[3072]{0:T(1024)S(1)} %get-tuple-element.6, f32[3072]{0:T(1024)S(1)} %get-tuple-element.5), kind=kOutput, calls=%fused_computation.1 | convolution fusion | flops 1218969600 | bytes 5971968 | tf_op jit(solution)/shard_map/dot_general | solution.py:30
  87.2 0.0 all-reduce.3.cloned.1.call-update
  87.9 0.1 subtract_convert_fusion
  88.0 0.0 copy-done
  88.0 31.0 %all-reduce.3.cloned.1.call-done = f32[384,8,64]{0,2,1:T(8,128)} async-done(((f32[384,8,64]{0,2,1:T(8,128)}), f32[384,8,64]{0,2,1:T(8,128)}) %all-reduce.3.cloned.1.call-update) | async-done | bytes 786448 | tf_op jit(solution)/shard_map/psum | solution.py:34
  119.0 1.2 reduce_sum.19
  120.2 1.9 %add_bitcast_fusion = f32[4,384,64]{1,2,0:T(8,128)} fusion(f32[384,8,64]{0,2,1:T(8,128)} %all-reduce.3.cloned.1.call-done, s32[]{:T(128)S(6)} %select_n.4, f32[4]{0:T(128)S(1)} %subtract_convert_fusion, f32[384,64]{0,1:T(8,128)S(1)} %reduce_sum.19, f32[384,64]{0,1:T(8,128)S(1)} %broadcast_multiply_fusion), kind=kLoop, calls=%fused_computation.8 | loop fusion | flops 294912 | bytes 983060 | tf_op jit(solution)/shard_map/transpose | solution.py:44
  (3 shorter events, 0.0 us)
Async XLA Ops:
  6.5 75.3 %copy-start.1 = (s32[8]{0:T(128)S(1)}, s32[8]{0:T(128)}, u32[]{:S(2)}) copy-start(s32[8]{0:T(128)} %param.7) | copy-start | bytes 100
  6.5 112.4 %all-reduce.3.cloned.1.call-start = ((), (), s32[]{:S(2)}) async-start(), calls=%async_computation | async-start | bytes 1572864 | tf_op jit(solution)/shard_map/psum | solution.py:34
  82.1 5.9 %copy-start = (f32[384,64]{0,1:T(8,128)S(1)}, f32[384,64]{0,1:T(8,128)}, u32[]{:S(2)}) copy-start(f32[384,64]{0,1:T(8,128)} %param.9) | copy-start | bytes 294916
Sparse Core Ops, SparseCore 0:
  87.4 31.5 all-reduce.2
where the time goes:
time: 129 us
  blocking collectives  71.3 us (55%)
  waiting for transfers between devices  31 us (24%)
  between operations  14.1 us (11%)
  matrix products  8.28 us (6%)
  other arithmetic  4.16 us (3%)
    psum x1, blocking collectives, on_device(): lax.psum(lax.dot_general(standard, vector, contract, preferred_element_ty...  71.3 us
    psum x1, waiting for transfers between devices, on_device(): summed = lax.psum(by_section, 'chrom')  31 us
    dot_general x1, matrix products, on_device(): jnp.dot(standard, spread, preferred_element_type=jnp.float32)  5.1 us
    dot_general x1, matrix products, on_device(): lax.dot_general(standard, vector, contract, preferred_element_type=jnp.fl...  3.18 us
  transfers between devices with their start and end apart: 1, of which 1 were waited for; matrix products, arithmetic and copies ran while one was open for 0% of the time, Pallas kernels for 0%

commit v1 on v0

v1 whole, which is shorter than its diff:
```python
import functools

import jax
import jax.numpy as jnp
from jax import lax
from jax.experimental import pallas as pl
from jax.experimental.pallas import tpu as pltpu
from jax.sharding import PartitionSpec as P

VMEM_LIMIT = 24 * 1024 * 1024


def core_and_bits():
    samp = lax.axis_index("samp")
    core = samp % 2
    return core, jnp.where(core == 0, (samp // 2) % 2, (samp // 4) % 2), jnp.where(core == 0, (samp // 4) % 2, (samp // 2) % 2)


def cross_kernel(blocks, geno_hbm, freq_ref, dir_ref, stand_ref, keep_ref, send_ref, geno, sems):
    width = geno_hbm.shape[1] // blocks
    copies = []
    for i in range(blocks):
        columns = pl.ds(i * width, width)
        copies.append(pltpu.make_async_copy(geno_hbm.at[:, columns], geno.at[:, columns], sems.at[i]))
        copies[-1].start()
    half = dir_ref.shape[0] // 2
    first = lax.axis_index("samp") % 2 == 0
    vector = dir_ref[...].astype(jnp.bfloat16)
    for i in range(blocks):
        columns = pl.ds(i * width, width)
        doubled = 2.0 * freq_ref[:, columns]
        scale = lax.rsqrt(doubled * (1.0 - freq_ref[:, columns]))
        copies[i].wait()
        standard = ((geno[:, columns].astype(jnp.float32) - doubled) * scale).astype(jnp.bfloat16)
        stand_ref[:, columns] = standard
        crossed = jnp.dot(vector, standard, preferred_element_type=jnp.float32)
        keep_ref[:, columns] = jnp.where(first, crossed[:half], crossed[half:])
        send_ref[:, columns] = jnp.where(first, crossed[half:], crossed[:half]).astype(jnp.bfloat16)


def section_kernel(others, widths_ref, stand_ref, *refs):
    *pieces, out_ref = refs
    variants = stand_ref.shape[1]
    sections = widths_ref.shape[0]
    chrom = lax.axis_index("chrom")
    half = (chrom // (lax.axis_size("chrom") // 2)) % 2
    first_section = (1 - half if others else half) * (sections // 2)
    first_var = chrom * variants
    var = first_var + lax.broadcasted_iota(jnp.int32, (1, variants), 1)
    start = jnp.int32(0)
    for c in range(sections // 2):
        start = start + jnp.where(first_section > 0, widths_ref[c], 0)
    shared = jnp.concatenate([p[...] for p in pieces], axis=0)
    spread = []
    for c in range(sections // 2):
        end = start + widths_ref[first_section + c]
        outside = jnp.where((var < start) | (var >= end), 1.0, 0.0).astype(jnp.bfloat16)
        spread.append(shared * outside)
        start = end
    product = lax.dot_general(
        jnp.concatenate(spread, axis=0), stand_ref[...], (((1,), (1,)), ((), ())), preferred_element_type=jnp.float32
    )
    out_ref[...] = product.reshape(out_ref.shape).astype(out_ref.dtype)


def finish_kernel(total, widths_ref, ridge_ref, dir_ref, own_ref, got_ref, out_ref):
    per_device, rhs, _ = out_ref.shape
    first_section = lax.axis_index("chrom") * per_device
    core, mine, sibling = core_and_bits()
    quarter = rhs // 4
    half = rhs // 2
    rows = [
        core * half + mine * quarter,
        core * half + (1 - mine) * quarter,
        (1 - core) * half + sibling * quarter,
        (1 - core) * half + (1 - sibling) * quarter,
    ]
    for p in range(4):
        at = pl.ds(pl.multiple_of(rows[p], quarter), quarter)
        ridged = ridge_ref[0] * dir_ref[at, :]
        here = pl.ds(p * quarter, quarter)
        for c in range(per_device):
            divisor = (total - widths_ref[first_section + c]).astype(jnp.float32)
            rest = own_ref[c, here, :] + got_ref[c, here, :].astype(jnp.float32)
            out_ref[c, at, :] = ridged + rest / divisor


def on_device(genotypes, frequency, widths, ridge_term, direction):
    rows, variants = genotypes.shape
    rhs = direction.shape[1]
    sections = widths.shape[0]
    n_samp, n_chrom = lax.axis_size("samp"), lax.axis_size("chrom")
    per_device = sections // n_chrom
    half, quarter = rhs // 2, rhs // 4
    vmem = pl.BlockSpec(memory_space=pltpu.VMEM)
    smem = pl.BlockSpec(memory_space=pltpu.SMEM)
    params = pltpu.CompilerParams(vmem_limit_bytes=VMEM_LIMIT)
    dir_t = direction.T

    blocks = max(1, variants // 512)
    standard, keep, send = pl.pallas_call(
        functools.partial(cross_kernel, blocks),
        out_shape=(
            jax.ShapeDtypeStruct((rows, variants), jnp.bfloat16),
            jax.ShapeDtypeStruct((half, variants), jnp.float32),
            jax.ShapeDtypeStruct((half, variants), jnp.bfloat16),
        ),
        in_specs=[pl.BlockSpec(memory_space=pl.ANY), vmem, vmem],
        out_specs=(vmem, vmem, vmem),
        scratch_shapes=[pltpu.VMEM((rows, variants), jnp.int32), pltpu.SemaphoreType.DMA((blocks,))],
        compiler_params=params,
        name="cross",
    )(genotypes, frequency.reshape(1, variants), dir_t)

    def swap(x, even, odd):
        return lax.ppermute(x, "samp", [(i, i ^ (odd if i % 2 else even)) for i in range(n_samp)])

    core, mine, _ = core_and_bits()
    sums = keep + swap(send, 1, 1)
    at = lambda b: lax.dynamic_slice_in_dim(sums, b * quarter, quarter, 0)
    mine_sum = at(mine) + swap(at(1 - mine).astype(jnp.bfloat16), 2, 4)
    mine_sum = mine_sum + swap(mine_sum.astype(jnp.bfloat16), 4, 2)
    bit = 8
    while bit < n_samp:
        mine_sum = mine_sum + swap(mine_sum.astype(jnp.bfloat16), bit, bit)
        bit *= 2
    first = mine_sum.astype(jnp.bfloat16)
    second = swap(first, 2, 4)
    pieces = (first, second, swap(first, 1, 1), swap(second, 1, 1))

    def products(others, dtype):
        return pl.pallas_call(
            functools.partial(section_kernel, others),
            out_shape=jax.ShapeDtypeStruct((sections // 2, rhs, rows), dtype),
            in_specs=[smem, vmem] + [vmem] * 4,
            out_specs=vmem,
            compiler_params=params,
            cost_estimate=pl.CostEstimate(
                flops=rows * variants * rhs * sections, bytes_accessed=rows * variants * 2, transcendentals=0
            ),
            name="others" if others else "own",
        )(widths, standard, *pieces)

    def swap_chrom(x, bit):
        return lax.ppermute(x, "chrom", [(i, i ^ bit) for i in range(n_chrom)])

    bit = n_chrom // 2
    got = swap_chrom(products(True, jnp.bfloat16), bit)
    own = products(False, jnp.float32)
    while bit > 1:
        own = own + got
        bit //= 2
        count = own.shape[0] // 2
        side = (lax.axis_index("chrom") // bit) % 2
        got = swap_chrom(lax.dynamic_slice_in_dim(own, (1 - side) * count, count, 0).astype(jnp.bfloat16), bit)
        own = lax.dynamic_slice_in_dim(own, side * count, count, 0)

    out = pl.pallas_call(
        functools.partial(finish_kernel, variants * n_chrom),
        out_shape=jax.ShapeDtypeStruct((per_device, rhs, rows), jnp.float32),
        in_specs=[smem, smem, vmem, vmem, vmem],
        out_specs=vmem,
        compiler_params=params,
        name="finish",
    )(widths, ridge_term, dir_t, own, got)
    return jnp.transpose(out, (0, 2, 1))


def solution(mesh):
    return jax.shard_map(
        on_device,
        mesh=mesh,
        in_specs=(P("samp", "chrom"), P("chrom"), P(), P(), P("samp", None)),
        out_specs=P("chrom", "samp", None),
        check_vma=False,
    )
```

time: 129 us -> 40.1 us (0.31)
  blocking collectives: 71.3 us -> 0 us
  waiting for transfers between devices: 31 us -> 15.9 us
  between operations: 14.1 us -> 0.71 us
  starting transfers between devices: 0.01 us -> 12.5 us
  matrix products: 8.28 us -> 0 us
  Pallas kernels: 0 us -> 6.55 us
  other arithmetic: 4.16 us -> 0.15 us
  local copies, waits for them, and re-layouts: 0.01 us -> 3.98 us
    psum x1 -> x0, blocking collectives: 71.3 us -> none  [on_device(): lax.psum(lax.dot_general(standard, vector, contract, preferred_element_ty...]
    psum x1 -> x0, waiting for transfers between devices: 31 us -> none  [on_device(): summed = lax.psum(by_section, 'chrom')]
    ppermute x0 -> x8, waiting for transfers between devices: none -> 15.9 us  [the longest x7 12.9 us: swap(): lax.ppermute(x, 'samp', [(i, i ^ (odd if i % 2 else even)) for i in range...]
    ppermute x0 -> x8, starting transfers between devices: none -> 12.5 us  [the longest x7 10.6 us: swap(): lax.ppermute(x, 'samp', [(i, i ^ (odd if i % 2 else even)) for i in range...]
    dot_general x2 -> x0, matrix products: 8.28 us -> none  [the longest x1 5.1 us: on_device(): jnp.dot(standard, spread, preferred_element_type=jnp.float32)]
    pallas_call x0 -> x4, Pallas kernels: none -> 6.55 us  [the longest x2 3.07 us: products(): pl.pallas_call(functools.partial(section_kernel, others), out_shape=jax.S...]
    unnamed x4 -> x10, local copies, waits for them, and re-layouts: 0.01 us -> 3.96 us
    transpose x1 -> x0, other arithmetic: 1.86 us -> none  [on_device(): return jnp.transpose(result, (1, 0, 2))]
  transfers between devices with their start and end apart: 1 -> 8, of which waited for: 1 -> 7; matrix products, arithmetic and copies ran while one was open for 0% -> 0% of each run, Pallas kernels for 0% -> 4%
where the time goes in v1:
time: 40.1 us; the launch traced here: 39.9 us
  waiting for transfers between devices  15.9 us (40%)
  starting transfers between devices  12.5 us (31%)
  Pallas kernels  6.55 us (16%)
  local copies, waits for them, and re-layouts  3.98 us (10%)
  between operations  0.71 us (2%)
    ppermute x7, waiting for transfers between devices, swap(): lax.ppermute(x, 'samp', [(i, i ^ (odd if i % 2 else even)) for i in range...  12.9 us
    ppermute x7, starting transfers between devices, swap(): lax.ppermute(x, 'samp', [(i, i ^ (odd if i % 2 else even)) for i in range...  10.6 us
    unnamed x10, local copies, waits for them, and re-layouts  3.96 us
    pallas_call x2, Pallas kernels, products(): pl.pallas_call(functools.partial(section_kernel, others), out_shape=jax.S...  3.07 us
    ppermute x1, waiting for transfers between devices, swap_chrom(): return lax.ppermute(x, 'chrom', [(i, i ^ bit) for i in range(n_chrom)])  3.03 us
    pallas_call x1, Pallas kernels, on_device(): pl.pallas_call(functools.partial(cross_kernel, blocks), out_shape=(jax.Sh...  2.1 us
    ppermute x1, starting transfers between devices, swap_chrom(): return lax.ppermute(x, 'chrom', [(i, i ^ bit) for i in range(n_chrom)])  1.89 us
    pallas_call x1, Pallas kernels, on_device(): pl.pallas_call(functools.partial(finish_kernel, variants * n_chrom), out_...  1.37 us
  transfers between devices with their start and end apart: 8, of which 7 were waited for; matrix products, arithmetic and copies ran while one was open for 0% of the time, Pallas kernels for 4%

profile of v1, /device:TPU:0, one launch (start us, length us, event | category | flops | bytes accessed | tf_op | source)
XLA Modules:
  0.0 39.9 jit_solution(882127587588076935)
XLA Ops:
  0.0 0.0 copy-start.4
  0.0 0.0 copy-start
  0.0 2.3 %copy-done = s32[384,3072]{1,0:T(8,128)S(1)} copy-done((s32[384,3072]{1,0:T(8,128)S(1)}, s32[384,3072]{1,0:T(8,128)}, u32[]{:S(2)}) %copy-start) | copy-done | bytes 4718616
  2.4 0.0 copy-start.1
  2.4 0.9 %copy-done.1 = f32[384,64]{0,1:T(8,128)S(1)} copy-done((f32[384,64]{0,1:T(8,128)S(1)}, f32[384,64]{0,1:T(8,128)}, u32[]{:S(2)}) %copy-start.1) | copy-done | bytes 98328
  3.2 0.0 copy-start.3
  3.2 0.7 %copy-done.3 = f32[3072]{0:T(1024)S(1)} copy-done((f32[3072]{0:T(1024)S(1)}, f32[3072]{0:T(1024)}, u32[]{:S(2)}) %copy-start.3) | copy-done | bytes 12312
  4.0 2.1 %cross.1 = (bf16[384,3072]{1,0:T(8,128)(2,1)S(1)}, f32[32,3072]{1,0:T(8,128)S(1)}, bf16[32,3072]{1,0:T(8,128)(2,1)S(1)}) custom-call(s32[384,3072]{1,0:T(8,128)S(1)} %copy-done, f32[1,3072]{1,0:T(1,128)S(1)} %bitcast.5, f32[64,384]{1,0:T(8,128)S(1)} %bitcast.3), custom_call_target="tpu_custom_call" | custom-call | tf_op jit(solution)/shard_map/cross/pallas_call | solution.py:101
  6.1 0.0 copy-start.2
  6.1 0.5 %collective-permute-start = (bf16[32,3072]{1,0:T(8,128)(2,1)S(1)}, bf16[32,3072]{1,0:T(8,128)(2,1)S(1)}, u32[]{:S(2)}, u32[]{:S(2)}) collective-permute-start(bf16[32,3072]{1,0:T(8,128)(2,1)S(1)} %get-tuple-element.10), channel_id=1, source_target_pairs={{0,1},{1,0},{2,3},{3,2},{4,5},{5,4},{6,7},{7,6},{8,9},{9,8},{10,11... | collective-permute-start | bytes 589832 | tf_op jit(solution)/shard_map/ppermute | solution.py:116
  6.6 1.1 %collective-permute-done = bf16[32,3072]{1,0:T(8,128)(2,1)S(1)} collective-permute-done((bf16[32,3072]{1,0:T(8,128)(2,1)S(1)}, bf16[32,3072]{1,0:T(8,128)(2,1)S(1)}, u32[]{:S(2)}, u32[]{:S(2)}) %collective-permute-start) | collective-permute-done | bytes 196640 | tf_op jit(solution)/shard_map/ppermute | solution.py:116
  7.7 3.0 %collective-permute-start.1 = (bf16[16,3072]{1,0:T(8,128)(2,1)S(1)}, bf16[16,3072]{1,0:T(8,128)(2,1)S(1)}, u32[]{:S(2)}, u32[]{:S(2)}) collective-permute-start(bf16[16,3072]{1,0:T(8,128)(2,1)S(1)} %dynamic-slice_convert_fusion), channel_id=1, source_target_pairs={{0,2},{1,5},{2,0},{3,7},{4,6},{5,1},{6,4},{7,3},{8,10},{9,13},{10,... | collective-permute-start | bytes 294920 | tf_op jit(solution)/shard_map/ppermute | solution.py:116
  10.7 2.6 %collective-permute-done.1 = bf16[16,3072]{1,0:T(8,128)(2,1)S(1)} collective-permute-done((bf16[16,3072]{1,0:T(8,128)(2,1)S(1)}, bf16[16,3072]{1,0:T(8,128)(2,1)S(1)}, u32[]{:S(2)}, u32[]{:S(2)}) %collective-permute-start.1) | collective-permute-done | bytes 98336 | tf_op jit(solution)/shard_map/ppermute | solution.py:116
  13.3 2.1 %collective-permute-start.2 = (bf16[16,3072]{1,0:T(8,128)(2,1)S(1)}, bf16[16,3072]{1,0:T(8,128)(2,1)S(1)}, u32[]{:S(2)}, u32[]{:S(2)}) collective-permute-start(bf16[16,3072]{1,0:T(8,128)(2,1)S(1)} %fusion.1), channel_id=1, source_target_pairs={{0,4},{1,3},{2,6},{3,1},{4,0},{5,7},{6,2},{7,5},{8,12},{9,11},{10,... | collective-permute-start | bytes 294920 | tf_op jit(solution)/shard_map/ppermute | solution.py:116
  15.5 2.6 %collective-permute-done.2 = bf16[16,3072]{1,0:T(8,128)(2,1)S(1)} collective-permute-done((bf16[16,3072]{1,0:T(8,128)(2,1)S(1)}, bf16[16,3072]{1,0:T(8,128)(2,1)S(1)}, u32[]{:S(2)}, u32[]{:S(2)}) %collective-permute-start.2) | collective-permute-done | bytes 98336 | tf_op jit(solution)/shard_map/ppermute | solution.py:116
  18.1 3.1 %collective-permute-start.3 = (bf16[16,3072]{1,0:T(8,128)(2,1)S(1)}, bf16[16,3072]{1,0:T(8,128)(2,1)S(1)}, u32[]{:S(2)}, u32[]{:S(2)}) collective-permute-start(bf16[16,3072]{1,0:T(8,128)(2,1)S(1)} %fusion), channel_id=1, source_target_pairs={{0,8},{1,9},{2,10},{3,11},{4,12},{5,13},{6,14},{7,15},{8,0},{9,1},... | collective-permute-start | bytes 294920 | tf_op jit(solution)/shard_map/ppermute | solution.py:116
  21.2 2.6 %collective-permute-done.3 = bf16[16,3072]{1,0:T(8,128)(2,1)S(1)} collective-permute-done((bf16[16,3072]{1,0:T(8,128)(2,1)S(1)}, bf16[16,3072]{1,0:T(8,128)(2,1)S(1)}, u32[]{:S(2)}, u32[]{:S(2)}) %collective-permute-start.3) | collective-permute-done | bytes 98336 | tf_op jit(solution)/shard_map/ppermute | solution.py:116
  23.8 0.1 add_convert_fusion.refs_0_
  23.8 1.9 %collective-permute-start.4 = (bf16[16,3072]{1,0:T(8,128)(2,1)S(1)}, bf16[16,3072]{1,0:T(8,128)(2,1)S(1)}, u32[]{:S(2)}, u32[]{:S(2)}) collective-permute-start(bf16[16,3072]{1,0:T(8,128)(2,1)S(1)} %add_convert_fusion.refs_0_), channel_id=1, source_target_pairs={{0,2},{1,5},{2,0},{3,7},{4,6},{5,1},{6,4},{7,3},{8,10},{9,13},{10,... | collective-permute-start | bytes 294920 | tf_op jit(solution)/shard_map/ppermute | solution.py:116
  25.8 0.0 collective-permute-start.5
  25.8 2.8 %collective-permute-done.4.refs_1_ = bf16[16,3072]{1,0:T(8,128)(2,1)S(1)} collective-permute-done((bf16[16,3072]{1,0:T(8,128)(2,1)S(1)}, bf16[16,3072]{1,0:T(8,128)(2,1)S(1)}, u32[]{:S(2)}, u32[]{:S(2)}) %collective-permute-start.4) | collective-permute-done | bytes 98336 | tf_op jit(solution)/shard_map/ppermute | solution.py:116
  28.5 0.0 collective-permute-start.6
  28.5 0.0 collective-permute-done.5.refs_2_
  28.5 1.3 %collective-permute-done.6.refs_3_ = bf16[16,3072]{1,0:T(8,128)(2,1)S(1)} collective-permute-done((bf16[16,3072]{1,0:T(8,128)(2,1)S(1)}, bf16[16,3072]{1,0:T(8,128)(2,1)S(1)}, u32[]{:S(2)}, u32[]{:S(2)}) %collective-permute-start.6) | collective-permute-done | bytes 98336 | tf_op jit(solution)/shard_map/ppermute | solution.py:116
  29.8 0.0 copy-done.4
  29.8 1.5 %others.1 = bf16[4,64,384]{2,1,0:T(8,128)(2,1)S(1)} custom-call(s32[8]{0:T(128)S(1)} %copy-done.4, bf16[384,3072]{1,0:T(8,128)(2,1)S(1)} %get-tuple-element.8.stand_ref, bf16[16,3072]{1,0:T(8,128)(2,1)S(1)} %add_convert_fusion.refs_0_, bf16[16,3072]{1,0:T(8,128)(2,1)S(1)} %collective-permute-done.4.refs_1_, ...), custom_call_target="tpu_custom_call" | custom-call | flops 603979776 | bytes 2359296 | tf_op jit(solution)/shard_map/others/pallas_call | solution.py:132
  31.4 1.9 %collective-permute-start.7 = (bf16[4,64,384]{2,1,0:T(8,128)(2,1)S(1)}, bf16[4,64,384]{2,1,0:T(8,128)(2,1)S(1)}, u32[]{:S(2)}, u32[]{:S(2)}) collective-permute-start(bf16[4,64,384]{2,1,0:T(8,128)(2,1)S(1)} %others.1), channel_id=1, source_target_pairs={{0,16},{16,0},{1,17},{17,1},{2,18},{18,2},{3,19},{19,3},{4,20},{20... | collective-permute-start | bytes 589832 | tf_op jit(solution)/shard_map/ppermute | solution.py:145
  33.9 1.5 %own.1.own_ref = f32[4,64,384]{2,1,0:T(8,128)S(1)} custom-call(s32[8]{0:T(128)S(1)} %copy-done.4, bf16[384,3072]{1,0:T(8,128)(2,1)S(1)} %get-tuple-element.8.stand_ref, bf16[16,3072]{1,0:T(8,128)(2,1)S(1)} %add_convert_fusion.refs_0_, bf16[16,3072]{1,0:T(8,128)(2,1)S(1)} %collective-permute-done.4.refs_1_, ...), custom_call_target="tpu_custom_call" | custom-call | flops 603979776 | bytes 2359296 | tf_op jit(solution)/shard_map/own/pallas_call | solution.py:132
  35.5 3.0 %collective-permute-done.7.got_ref = bf16[4,64,384]{2,1,0:T(8,128)(2,1)S(1)} collective-permute-done((bf16[4,64,384]{2,1,0:T(8,128)(2,1)S(1)}, bf16[4,64,384]{2,1,0:T(8,128)(2,1)S(1)}, u32[]{:S(2)}, u32[]{:S(2)}) %collective-permute-start.7) | collective-permute-done | bytes 196640 | tf_op jit(solution)/shard_map/ppermute | solution.py:145
  38.5 0.0 copy-done.2
  38.5 1.4 %finish.1 = f32[4,64,384]{2,1,0:T(8,128)} custom-call(s32[8]{0:T(128)S(1)} %copy-done.4, f32[1]{0:T(128)S(6)} %copy.6.ridge_ref, f32[64,384]{1,0:T(8,128)S(1)} %bitcast.4, f32[4,64,384]{2,1,0:T(8,128)S(1)} %own.1.own_ref, bf16[4,64,384]{2,1,0:T(8,128)(2,1)S(1)} %collective-permute-done.7.got_ref), custom_call_target="tpu_custom_call" | custom-call | tf_op jit(solution)/shard_map/finish/pallas_call | solution.py:158
  (4 shorter events, 0.1 us)
Async XLA Ops:
  0.0 29.8 %copy-start.4 = (s32[8]{0:T(128)S(1)}, s32[8]{0:T(128)}, u32[]{:S(2)}) copy-start(s32[8]{0:T(128)} %widths_ref.5) | copy-start | bytes 100
  0.0 2.4 %copy-start = (s32[384,3072]{1,0:T(8,128)S(1)}, s32[384,3072]{1,0:T(8,128)}, u32[]{:S(2)}) copy-start(s32[384,3072]{1,0:T(8,128)} %geno_hbm.1) | copy-start | bytes 14155780
  2.4 0.9 %copy-start.1 = (f32[384,64]{0,1:T(8,128)S(1)}, f32[384,64]{0,1:T(8,128)}, u32[]{:S(2)}) copy-start(f32[384,64]{0,1:T(8,128)} %param.9) | copy-start | bytes 294916
  3.2 0.7 %copy-start.3 = (f32[3072]{0:T(1024)S(1)}, f32[3072]{0:T(1024)}, u32[]{:S(2)}) copy-start(f32[3072]{0:T(1024)} %param.6) | copy-start | bytes 36868
  6.1 32.4 %copy-start.2 = (f32[384,64]{0,1:T(8,128)S(1)}, f32[384,64]{0,1:T(8,128)}, u32[]{:S(2)}) copy-start(f32[384,64]{0,1:T(8,128)} %param.9) | copy-start | bytes 294916
  6.1 1.6 %collective-permute-start = (bf16[32,3072]{1,0:T(8,128)(2,1)S(1)}, bf16[32,3072]{1,0:T(8,128)(2,1)S(1)}, u32[]{:S(2)}, u32[]{:S(2)}) collective-permute-start(bf16[32,3072]{1,0:T(8,128)(2,1)S(1)} %get-tuple-element.10), channel_id=1, source_target_pairs={{0,1},{1,0},{2,3},{3,2},{4,5},{5,4},{6,7},{7,6},{8,9},{9,8},{10,11... | collective-permute-start | bytes 589832 | tf_op jit(solution)/shard_map/ppermute | solution.py:116
  7.7 5.5 %collective-permute-start.1 = (bf16[16,3072]{1,0:T(8,128)(2,1)S(1)}, bf16[16,3072]{1,0:T(8,128)(2,1)S(1)}, u32[]{:S(2)}, u32[]{:S(2)}) collective-permute-start(bf16[16,3072]{1,0:T(8,128)(2,1)S(1)} %dynamic-slice_convert_fusion), channel_id=1, source_target_pairs={{0,2},{1,5},{2,0},{3,7},{4,6},{5,1},{6,4},{7,3},{8,10},{9,13},{10,... | collective-permute-start | bytes 294920 | tf_op jit(solution)/shard_map/ppermute | solution.py:116
  13.3 4.7 %collective-permute-start.2 = (bf16[16,3072]{1,0:T(8,128)(2,1)S(1)}, bf16[16,3072]{1,0:T(8,128)(2,1)S(1)}, u32[]{:S(2)}, u32[]{:S(2)}) collective-permute-start(bf16[16,3072]{1,0:T(8,128)(2,1)S(1)} %fusion.1), channel_id=1, source_target_pairs={{0,4},{1,3},{2,6},{3,1},{4,0},{5,7},{6,2},{7,5},{8,12},{9,11},{10,... | collective-permute-start | bytes 294920 | tf_op jit(solution)/shard_map/ppermute | solution.py:116
  18.1 5.7 %collective-permute-start.3 = (bf16[16,3072]{1,0:T(8,128)(2,1)S(1)}, bf16[16,3072]{1,0:T(8,128)(2,1)S(1)}, u32[]{:S(2)}, u32[]{:S(2)}) collective-permute-start(bf16[16,3072]{1,0:T(8,128)(2,1)S(1)} %fusion), channel_id=1, source_target_pairs={{0,8},{1,9},{2,10},{3,11},{4,12},{5,13},{6,14},{7,15},{8,0},{9,1},... | collective-permute-start | bytes 294920 | tf_op jit(solution)/shard_map/ppermute | solution.py:116
  23.8 4.7 %collective-permute-start.4 = (bf16[16,3072]{1,0:T(8,128)(2,1)S(1)}, bf16[16,3072]{1,0:T(8,128)(2,1)S(1)}, u32[]{:S(2)}, u32[]{:S(2)}) collective-permute-start(bf16[16,3072]{1,0:T(8,128)(2,1)S(1)} %add_convert_fusion.refs_0_), channel_id=1, source_target_pairs={{0,2},{1,5},{2,0},{3,7},{4,6},{5,1},{6,4},{7,3},{8,10},{9,13},{10,... | collective-permute-start | bytes 294920 | tf_op jit(solution)/shard_map/ppermute | solution.py:116
  25.8 2.8 %collective-permute-start.5 = (bf16[16,3072]{1,0:T(8,128)(2,1)S(1)}, bf16[16,3072]{1,0:T(8,128)(2,1)S(1)}, u32[]{:S(2)}, u32[]{:S(2)}) collective-permute-start(bf16[16,3072]{1,0:T(8,128)(2,1)S(1)} %add_convert_fusion.refs_0_), channel_id=1, source_target_pairs={{0,1},{1,0},{2,3},{3,2},{4,5},{5,4},{6,7},{7,6},{8,9},{9,8},{10,11... | collective-permute-start | bytes 294920 | tf_op jit(solution)/shard_map/ppermute | solution.py:116
  28.5 1.3 %collective-permute-start.6 = (bf16[16,3072]{1,0:T(8,128)(2,1)S(1)}, bf16[16,3072]{1,0:T(8,128)(2,1)S(1)}, u32[]{:S(2)}, u32[]{:S(2)}) collective-permute-start(bf16[16,3072]{1,0:T(8,128)(2,1)S(1)} %collective-permute-done.4.refs_1_), channel_id=1, source_target_pairs={{0,1},{1,0},{2,3},{3,2},{4,5},{5,4},{6,7},{7,6},{8,9},{9,8},{10,11... | collective-permute-start | bytes 294920 | tf_op jit(solution)/shard_map/ppermute | solution.py:116
  31.4 7.1 %collective-permute-start.7 = (bf16[4,64,384]{2,1,0:T(8,128)(2,1)S(1)}, bf16[4,64,384]{2,1,0:T(8,128)(2,1)S(1)}, u32[]{:S(2)}, u32[]{:S(2)}) collective-permute-start(bf16[4,64,384]{2,1,0:T(8,128)(2,1)S(1)} %others.1), channel_id=1, source_target_pairs={{0,16},{16,0},{1,17},{17,1},{2,18},{18,2},{3,19},{19,3},{4,20},{20... | collective-permute-start | bytes 589832 | tf_op jit(solution)/shard_map/ppermute | solution.py:145

commit v2 on v1

v2 whole, which is shorter than its diff:
```python
import functools

import jax
import jax.numpy as jnp
from jax import lax
from jax.experimental import pallas as pl
from jax.experimental.pallas import tpu as pltpu
from jax.sharding import PartitionSpec as P

VMEM_LIMIT = 24 * 1024 * 1024
BLOCK = 512


def core_and_bits():
    samp = lax.axis_index("samp")
    core, y, z = samp % 2, (samp // 2) % 2, (samp // 4) % 2
    return core, jnp.where(core == 0, y, z), jnp.where(core == 0, z, y)


def cross_kernel(blocks, geno_hbm, freq_hbm, dir_hbm, stand_ref, keep_ref, send_ref, geno, freq_ref, dir_ref, sems):
    width = geno_hbm.shape[1] // blocks
    small = [
        pltpu.make_async_copy(freq_hbm, freq_ref, sems.at[blocks]),
        pltpu.make_async_copy(dir_hbm, dir_ref, sems.at[blocks + 1]),
    ]
    for copy in small:
        copy.start()
    copies = []
    for i in range(blocks):
        columns = pl.ds(i * width, width)
        copies.append(pltpu.make_async_copy(geno_hbm.at[:, columns], geno.at[:, columns], sems.at[i]))
        copies[-1].start()
    half = dir_ref.shape[0] // 2
    first = lax.axis_index("samp") % 2 == 0
    for copy in small:
        copy.wait()
    vector = dir_ref[...].astype(jnp.bfloat16)
    for i in range(blocks):
        columns = pl.ds(i * width, width)
        doubled = 2.0 * freq_ref[:, columns]
        scale = lax.rsqrt(doubled * (1.0 - freq_ref[:, columns]))
        copies[i].wait()
        standard = ((geno[:, columns].astype(jnp.float32) - doubled) * scale).astype(jnp.bfloat16)
        stand_ref[:, columns] = standard
        crossed = jnp.dot(vector, standard, preferred_element_type=jnp.float32)
        keep_ref[:, columns] = jnp.where(first, crossed[:half], crossed[half:])
        send_ref[:, columns] = jnp.where(first, crossed[half:], crossed[:half]).astype(jnp.bfloat16)


def piece_rows(rhs):
    core, mine, sibling = core_and_bits()
    half, quarter = rhs // 2, rhs // 4
    return [
        core * half + mine * quarter,
        (1 - core) * half + sibling * quarter,
        core * half + (1 - mine) * quarter,
        (1 - core) * half + (1 - sibling) * quarter,
    ]


def prepare_kernel(total, widths_ref, ridge_ref, dir_ref, others_ref, own_ref, inverse_ref, ridged_ref):
    sections = widths_ref.shape[0]
    _, rows, variants = own_ref.shape
    per_device = inverse_ref.shape[0]
    rhs = dir_ref.shape[0]
    chrom = lax.axis_index("chrom")
    side = (chrom // (lax.axis_size("chrom") // 2)) % 2
    var = chrom * variants + lax.broadcasted_iota(jnp.int32, (1, variants), 1)
    start = jnp.int32(0)
    for c in range(sections):
        end = start + widths_ref[c]
        outside = jnp.where((var < start) | (var >= end), 1.0, 0.0)
        outside = jnp.broadcast_to(outside, (rows, variants)).astype(jnp.bfloat16)
        here = side == (0 if c < sections // 2 else 1)

        @pl.when(here)
        def _():
            own_ref[c % (sections // 2)] = outside

        @pl.when(jnp.logical_not(here))
        def _():
            others_ref[c % (sections // 2)] = outside

        start = end
    for c in range(per_device):
        divisor = (total - widths_ref[chrom * per_device + c]).astype(jnp.float32)
        inverse_ref[c] = 1.0 / jnp.full(inverse_ref.shape[1:], divisor, jnp.float32)
    for p, row in enumerate(piece_rows(rhs)):
        quarter = rhs // 4
        ridged_ref[pl.ds(p * quarter, quarter), :] = ridge_ref[0] * dir_ref[pl.ds(pl.multiple_of(row, quarter), quarter), :]


def section_kernel(outside_ref, stand_ref, *refs):
    *pieces, out_ref = refs
    count = outside_ref.shape[0]
    spread = [p[...] * outside_ref[c] for c in range(count) for p in pieces]
    product = lax.dot_general(
        jnp.concatenate(spread, axis=0), stand_ref[...], (((1,), (1,)), ((), ())), preferred_element_type=jnp.float32
    )
    out_ref[...] = product.reshape(out_ref.shape).astype(out_ref.dtype)


def finish_kernel(inverse_ref, ridged_ref, *refs):
    owns, gots, out_ref = refs[:2], refs[2:4], refs[4]
    per_device, rhs, _ = out_ref.shape
    quarter = rhs // 4
    for p, row in enumerate(piece_rows(rhs)):
        at = pl.ds(pl.multiple_of(row, quarter), quarter)
        ridged = ridged_ref[pl.ds(p * quarter, quarter), :]
        here = pl.ds((p % 2) * quarter, quarter)
        for c in range(per_device):
            rest = owns[p // 2][c, here, :] + gots[p // 2][c, here, :].astype(jnp.float32)
            out_ref[c, at, :] = ridged + rest * inverse_ref[c]


def on_device(genotypes, frequency, widths, ridge_term, direction):
    rows, variants = genotypes.shape
    rhs = direction.shape[1]
    sections = widths.shape[0]
    n_samp, n_chrom = lax.axis_size("samp"), lax.axis_size("chrom")
    per_device = sections // n_chrom
    half, quarter = rhs // 2, rhs // 4
    vmem = pl.BlockSpec(memory_space=pltpu.VMEM)
    smem = pl.BlockSpec(memory_space=pltpu.SMEM)
    params = pltpu.CompilerParams(vmem_limit_bytes=VMEM_LIMIT)
    dir_t = direction.T

    blocks = max(1, variants // BLOCK)
    operands = (genotypes, frequency.reshape(1, variants), dir_t)
    standard, keep, send = pl.pallas_call(
        functools.partial(cross_kernel, blocks),
        out_shape=(
            jax.ShapeDtypeStruct((rows, variants), jnp.bfloat16),
            jax.ShapeDtypeStruct((half, variants), jnp.float32),
            jax.ShapeDtypeStruct((half, variants), jnp.bfloat16),
        ),
        in_specs=[pl.BlockSpec(memory_space=pl.ANY)] * 3,
        out_specs=(vmem, vmem, vmem),
        scratch_shapes=[
            pltpu.VMEM((rows, variants), jnp.int32),
            pltpu.VMEM((1, variants), jnp.float32),
            pltpu.VMEM((rhs, rows), jnp.float32),
            pltpu.SemaphoreType.DMA((blocks + 2,)),
        ],
        compiler_params=params,
        name="cross",
    )(*(pltpu.with_memory_space_constraint(a, pltpu.HBM) for a in operands))

    mask = jax.ShapeDtypeStruct((sections // 2, quarter, variants), jnp.bfloat16)
    outside_others, outside_own, inverse, ridged = pl.pallas_call(
        functools.partial(prepare_kernel, variants * n_chrom),
        out_shape=(
            mask,
            mask,
            jax.ShapeDtypeStruct((per_device, quarter, rows), jnp.float32),
            jax.ShapeDtypeStruct((rhs, rows), jnp.float32),
        ),
        in_specs=[smem, smem, vmem],
        out_specs=(vmem,) * 4,
        compiler_params=params,
        name="prepare",
    )(widths, ridge_term, dir_t)

    def swap(x, even, odd):
        return lax.ppermute(x, "samp", [(i, i ^ (odd if i % 2 else even)) for i in range(n_samp)])

    _, mine, _ = core_and_bits()
    sums = keep + swap(send, 1, 1)
    at = lambda b: lax.dynamic_slice_in_dim(sums, b * quarter, quarter, 0)
    mine_sum = at(mine) + swap(at(1 - mine).astype(jnp.bfloat16), 2, 4)
    mine_sum, outside_others, outside_own, inverse, ridged = lax.optimization_barrier(
        (mine_sum, outside_others, outside_own, inverse, ridged)
    )
    rest = [1 << b for b in range(3, n_samp.bit_length() - 1)]
    even_bits, odd_bits = [4] + rest, [2] + rest
    for even, odd in zip(even_bits, odd_bits):
        mine_sum = mine_sum + swap(mine_sum.astype(jnp.bfloat16), even, odd)
    first = mine_sum.astype(jnp.bfloat16)
    second = swap(first, 2, 4)
    halves = ((first, swap(first, 1, 1)), (second, swap(second, 1, 1)))

    def products(outside, pieces, dtype, name):
        return pl.pallas_call(
            section_kernel,
            out_shape=jax.ShapeDtypeStruct((sections // 2, half, rows), dtype),
            in_specs=[vmem] * 4,
            out_specs=vmem,
            compiler_params=params,
            cost_estimate=pl.CostEstimate(
                flops=rows * variants * half * sections, bytes_accessed=rows * variants * 2, transcendentals=0
            ),
            name=name,
        )(outside, standard, *pieces)

    def swap_chrom(x, bit):
        return lax.ppermute(x, "chrom", [(i, i ^ bit) for i in range(n_chrom)])

    bit = n_chrom // 2
    gots = [swap_chrom(products(outside_others, pieces, jnp.bfloat16, "others"), bit) for pieces in halves]
    owns = [products(outside_own, pieces, jnp.float32, "own") for pieces in halves]
    while bit > 1:
        bit //= 2
        count = owns[0].shape[0] // 2
        side = (lax.axis_index("chrom") // bit) % 2
        sums = [own + got for own, got in zip(owns, gots)]
        gots = [
            swap_chrom(lax.dynamic_slice_in_dim(s, (1 - side) * count, count, 0).astype(jnp.bfloat16), bit) for s in sums
        ]
        owns = [lax.dynamic_slice_in_dim(s, side * count, count, 0) for s in sums]

    out = pl.pallas_call(
        finish_kernel,
        out_shape=jax.ShapeDtypeStruct((per_device, rhs, rows), jnp.float32),
        in_specs=[vmem] * 6,
        out_specs=vmem,
        compiler_params=params,
        name="finish",
    )(inverse, ridged, *owns, *gots)
    return jnp.transpose(out, (0, 2, 1))


def solution(mesh):
    return jax.shard_map(
        on_device,
        mesh=mesh,
        in_specs=(P("samp", "chrom"), P("chrom"), P(), P(), P("samp", None)),
        out_specs=P("chrom", "samp", None),
        check_vma=False,
    )
```

time: 40.1 us -> 34.9 us (0.87)
  local copies, waits for them, and re-layouts: 3.98 us -> 0.03 us
  waiting for transfers between devices: 15.9 us -> 12.9 us
  Pallas kernels: 6.55 us -> 7.67 us
  starting transfers between devices: 12.5 us -> 13.2 us
    unnamed x10 -> x4, local copies, waits for them, and re-layouts: 3.96 us -> 0.01 us
    ppermute x7, waiting for transfers between devices: 12.9 us -> 10.1 us  [swap(): lax.ppermute(x, 'samp', [(i, i ^ (odd if i % 2 else even)) for i in range...]
    pallas_call x1, Pallas kernels: 2.1 us -> 2.8 us  [on_device(): pl.pallas_call(functools.partial(cross_kernel, blocks), out_shape=(jax.Sh...]
    ppermute x1 -> x2, starting transfers between devices: 1.89 us -> 2.46 us  [swap_chrom(): return lax.ppermute(x, 'chrom', [(i, i ^ bit) for i in range(n_chrom)])]
    pallas_call x3 -> x6, Pallas kernels: 4.45 us -> 4.87 us  [the longest x4 3.26 us: products(): pl.pallas_call(section_kernel, out_shape=jax.ShapeDtypeStruct((sections /...]
    ppermute x1 -> x2, waiting for transfers between devices: 3.03 us -> 2.87 us  [swap_chrom(): return lax.ppermute(x, 'chrom', [(i, i ^ bit) for i in range(n_chrom)])]
  transfers between devices with their start and end apart: 8 -> 9, of which waited for: 7 -> 7; matrix products, arithmetic and copies ran while one was open for 0% -> 0% of each run, Pallas kernels for 4% -> 12%
where the time goes in v2:
time: 34.9 us; the launch traced here: 34.7 us
  starting transfers between devices  13.2 us (38%)
  waiting for transfers between devices  12.9 us (37%)
  Pallas kernels  7.67 us (22%)
  between operations  0.75 us (2%)
    ppermute x7, starting transfers between devices, swap(): lax.ppermute(x, 'samp', [(i, i ^ (odd if i % 2 else even)) for i in range...  10.7 us
    ppermute x7, waiting for transfers between devices, swap(): lax.ppermute(x, 'samp', [(i, i ^ (odd if i % 2 else even)) for i in range...  10.1 us
    pallas_call x4, Pallas kernels, products(): pl.pallas_call(section_kernel, out_shape=jax.ShapeDtypeStruct((sections /...  3.26 us
    ppermute x2, waiting for transfers between devices, swap_chrom(): return lax.ppermute(x, 'chrom', [(i, i ^ bit) for i in range(n_chrom)])  2.87 us
    pallas_call x1, Pallas kernels, on_device(): pl.pallas_call(functools.partial(cross_kernel, blocks), out_shape=(jax.Sh...  2.8 us
    ppermute x2, starting transfers between devices, swap_chrom(): return lax.ppermute(x, 'chrom', [(i, i ^ bit) for i in range(n_chrom)])  2.46 us
    pallas_call x1, Pallas kernels, on_device(): pl.pallas_call(finish_kernel, out_shape=jax.ShapeDtypeStruct((per_device,...  0.82 us
    pallas_call x1, Pallas kernels, on_device(): pl.pallas_call(functools.partial(prepare_kernel, variants * n_chrom), out...  0.78 us
  transfers between devices with their start and end apart: 9, of which 7 were waited for; matrix products, arithmetic and copies ran while one was open for 0% of the time, Pallas kernels for 12%

profile of v2, /device:TPU:0, one launch (start us, length us, event | category | flops | bytes accessed | tf_op | source)
XLA Modules:
  0.0 34.7 jit_solution(7201763699042836431)
XLA Ops:
  0.0 0.0 copy-start
  0.0 0.0 copy-start.1
  0.0 2.8 %cross.1 = (bf16[384,3072]{1,0:T(8,128)(2,1)S(1)}, f32[32,3072]{1,0:T(8,128)S(1)}, bf16[32,3072]{1,0:T(8,128)(2,1)S(1)}) custom-call(s32[384,3072]{1,0:T(8,128)} %geno_hbm.1, f32[1,3072]{1,0:T(1,128)} %bitcast.5, f32[64,384]{1,0:T(8,128)} %bitcast.3), custom_call_target="tpu_custom_call" | custom-call | tf_op jit(solution)/shard_map/cross/pallas_call | solution.py:130
  2.8 0.5 %collective-permute-start = (bf16[32,3072]{1,0:T(8,128)(2,1)S(1)}, bf16[32,3072]{1,0:T(8,128)(2,1)S(1)}, u32[]{:S(2)}, u32[]{:S(2)}) collective-permute-start(bf16[32,3072]{1,0:T(8,128)(2,1)S(1)} %get-tuple-element.18), channel_id=1, source_target_pairs={{0,1},{1,0},{2,3},{3,2},{4,5},{5,4},{6,7},{7,6},{8,9},{9,8},{10,11... | collective-permute-start | bytes 589832 | tf_op jit(solution)/shard_map/ppermute | solution.py:165
  3.3 1.1 %collective-permute-done = bf16[32,3072]{1,0:T(8,128)(2,1)S(1)} collective-permute-done((bf16[32,3072]{1,0:T(8,128)(2,1)S(1)}, bf16[32,3072]{1,0:T(8,128)(2,1)S(1)}, u32[]{:S(2)}, u32[]{:S(2)}) %collective-permute-start) | collective-permute-done | bytes 196640 | tf_op jit(solution)/shard_map/ppermute | solution.py:165
  4.5 3.0 %collective-permute-start.1 = (bf16[16,3072]{1,0:T(8,128)(2,1)S(1)}, bf16[16,3072]{1,0:T(8,128)(2,1)S(1)}, u32[]{:S(2)}, u32[]{:S(2)}) collective-permute-start(bf16[16,3072]{1,0:T(8,128)(2,1)S(1)} %dynamic-slice_convert_fusion), channel_id=1, source_target_pairs={{0,2},{1,5},{2,0},{3,7},{4,6},{5,1},{6,4},{7,3},{8,10},{9,13},{10,... | collective-permute-start | bytes 294920 | tf_op jit(solution)/shard_map/ppermute | solution.py:165
  8.1 0.0 copy-done
  8.1 0.0 copy-done.1
  8.1 0.8 %prepare.1 = (bf16[4,16,3072]{2,1,0:T(8,128)(2,1)S(1)}, bf16[4,16,3072]{2,1,0:T(8,128)(2,1)S(1)}, f32[4,16,384]{2,1,0:T(8,128)S(1)}, f32[64,384]{1,0:T(8,128)S(1)}) custom-call(s32[8]{0:T(128)S(1)} %copy-done.1, f32[1]{0:T(128)S(6)} %copy.6.ridge_ref, f32[64,384]{1,0:T(8,128)S(1)} %bitcast.4), custom_call_target="tpu_custom_call" | custom-call | tf_op jit(solution)/shard_map/prepare/pallas_call | solution.py:150
  8.9 1.1 %collective-permute-done.1 = bf16[16,3072]{1,0:T(8,128)(2,1)S(1)} collective-permute-done((bf16[16,3072]{1,0:T(8,128)(2,1)S(1)}, bf16[16,3072]{1,0:T(8,128)(2,1)S(1)}, u32[]{:S(2)}, u32[]{:S(2)}) %collective-permute-start.1) | collective-permute-done | bytes 98336 | tf_op jit(solution)/shard_map/ppermute | solution.py:165
  10.1 2.1 %collective-permute-start.2 = (bf16[16,3072]{1,0:T(8,128)(2,1)S(1)}, bf16[16,3072]{1,0:T(8,128)(2,1)S(1)}, u32[]{:S(2)}, u32[]{:S(2)}) collective-permute-start(bf16[16,3072]{1,0:T(8,128)(2,1)S(1)} %convert_element_type.27), channel_id=1, source_target_pairs={{0,4},{1,3},{2,6},{3,1},{4,0},{5,7},{6,2},{7,5},{8,12},{9,11},{10,... | collective-permute-start | bytes 294920 | tf_op jit(solution)/shard_map/ppermute | solution.py:165
  12.2 2.6 %collective-permute-done.2 = bf16[16,3072]{1,0:T(8,128)(2,1)S(1)} collective-permute-done((bf16[16,3072]{1,0:T(8,128)(2,1)S(1)}, bf16[16,3072]{1,0:T(8,128)(2,1)S(1)}, u32[]{:S(2)}, u32[]{:S(2)}) %collective-permute-start.2) | collective-permute-done | bytes 98336 | tf_op jit(solution)/shard_map/ppermute | solution.py:165
  14.8 3.1 %collective-permute-start.3 = (bf16[16,3072]{1,0:T(8,128)(2,1)S(1)}, bf16[16,3072]{1,0:T(8,128)(2,1)S(1)}, u32[]{:S(2)}, u32[]{:S(2)}) collective-permute-start(bf16[16,3072]{1,0:T(8,128)(2,1)S(1)} %fusion), channel_id=1, source_target_pairs={{0,8},{1,9},{2,10},{3,11},{4,12},{5,13},{6,14},{7,15},{8,0},{9,1},... | collective-permute-start | bytes 294920 | tf_op jit(solution)/shard_map/ppermute | solution.py:165
  17.9 2.6 %collective-permute-done.3 = bf16[16,3072]{1,0:T(8,128)(2,1)S(1)} collective-permute-done((bf16[16,3072]{1,0:T(8,128)(2,1)S(1)}, bf16[16,3072]{1,0:T(8,128)(2,1)S(1)}, u32[]{:S(2)}, u32[]{:S(2)}) %collective-permute-start.3) | collective-permute-done | bytes 98336 | tf_op jit(solution)/shard_map/ppermute | solution.py:165
  20.6 2.0 %collective-permute-start.5 = (bf16[16,3072]{1,0:T(8,128)(2,1)S(1)}, bf16[16,3072]{1,0:T(8,128)(2,1)S(1)}, u32[]{:S(2)}, u32[]{:S(2)}) collective-permute-start(bf16[16,3072]{1,0:T(8,128)(2,1)S(1)} %add_convert_fusion.refs_0_), channel_id=1, source_target_pairs={{0,2},{1,5},{2,0},{3,7},{4,6},{5,1},{6,4},{7,3},{8,10},{9,13},{10,... | collective-permute-start | bytes 294920 | tf_op jit(solution)/shard_map/ppermute | solution.py:165
  22.6 0.0 collective-permute-start.4
  22.6 2.7 %collective-permute-done.5.refs_0_ = bf16[16,3072]{1,0:T(8,128)(2,1)S(1)} collective-permute-done((bf16[16,3072]{1,0:T(8,128)(2,1)S(1)}, bf16[16,3072]{1,0:T(8,128)(2,1)S(1)}, u32[]{:S(2)}, u32[]{:S(2)}) %collective-permute-start.5) | collective-permute-done | bytes 98336 | tf_op jit(solution)/shard_map/ppermute | solution.py:165
  25.2 0.0 collective-permute-start.6
  25.2 0.0 collective-permute-done.4.refs_1_
  25.3 0.8 %others.2 = bf16[4,32,384]{2,1,0:T(8,128)(2,1)S(1)} custom-call(bf16[4,16,3072]{2,1,0:T(8,128)(2,1)S(1)} %get-tuple-element.28.outside_ref, bf16[384,3072]{1,0:T(8,128)(2,1)S(1)} %get-tuple-element.26.stand_ref, bf16[16,3072]{1,0:T(8,128)(2,1)S(1)} %add_convert_fusion.refs_0_, bf16[16,3072]{1,0:T(8,128)(2,1)S(1)} %collective-permute-done.4.refs_1_), custom_call_target="tpu_custom_call" | custom-call | flops 301989888 | bytes 2359296 | tf_op jit(solution)/shard_map/others/pallas_call | solution.py:183
  26.1 2.0 %collective-permute-start.7 = (bf16[4,32,384]{2,1,0:T(8,128)(2,1)S(1)}, bf16[4,32,384]{2,1,0:T(8,128)(2,1)S(1)}, u32[]{:S(2)}, u32[]{:S(2)}) collective-permute-start(bf16[4,32,384]{2,1,0:T(8,128)(2,1)S(1)} %others.2), channel_id=1, source_target_pairs={{0,16},{16,0},{1,17},{17,1},{2,18},{18,2},{3,19},{19,3},{4,20},{20... | collective-permute-start | bytes 294920 | tf_op jit(solution)/shard_map/ppermute | solution.py:196
  28.1 0.0 collective-permute-done.6.refs_1_
  28.1 0.8 %others.3 = bf16[4,32,384]{2,1,0:T(8,128)(2,1)S(1)} custom-call(bf16[4,16,3072]{2,1,0:T(8,128)(2,1)S(1)} %get-tuple-element.28.outside_ref, bf16[384,3072]{1,0:T(8,128)(2,1)S(1)} %get-tuple-element.26.stand_ref, bf16[16,3072]{1,0:T(8,128)(2,1)S(1)} %collective-permute-done.5.refs_0_, bf16[16,3072]{1,0:T(8,128)(2,1)S(1)} %collective-permute-done.6.refs_1_), custom_call_target="tpu_custom_call" | custom-call | flops 301989888 | bytes 2359296 | tf_op jit(solution)/shard_map/others/pallas_call | solution.py:183
  28.9 0.5 %collective-permute-start.8 = (bf16[4,32,384]{2,1,0:T(8,128)(2,1)S(1)}, bf16[4,32,384]{2,1,0:T(8,128)(2,1)S(1)}, u32[]{:S(2)}, u32[]{:S(2)}) collective-permute-start(bf16[4,32,384]{2,1,0:T(8,128)(2,1)S(1)} %others.3), channel_id=1, source_target_pairs={{0,16},{16,0},{1,17},{17,1},{2,18},{18,2},{3,19},{19,3},{4,20},{20... | collective-permute-start | bytes 294920 | tf_op jit(solution)/shard_map/ppermute | solution.py:196
  29.4 0.8 %own.2.refs_0_ = f32[4,32,384]{2,1,0:T(8,128)S(1)} custom-call(bf16[4,16,3072]{2,1,0:T(8,128)(2,1)S(1)} %get-tuple-element.25.outside_ref, bf16[384,3072]{1,0:T(8,128)(2,1)S(1)} %get-tuple-element.26.stand_ref, bf16[16,3072]{1,0:T(8,128)(2,1)S(1)} %add_convert_fusion.refs_0_, bf16[16,3072]{1,0:T(8,128)(2,1)S(1)} %collective-permute-done.4.refs_1_), custom_call_target="tpu_custom_call" | custom-call | flops 301989888 | bytes 2359296 | tf_op jit(solution)/shard_map/own/pallas_call | solution.py:183
  30.2 0.8 %own.3.refs_1_ = f32[4,32,384]{2,1,0:T(8,128)S(1)} custom-call(bf16[4,16,3072]{2,1,0:T(8,128)(2,1)S(1)} %get-tuple-element.25.outside_ref, bf16[384,3072]{1,0:T(8,128)(2,1)S(1)} %get-tuple-element.26.stand_ref, bf16[16,3072]{1,0:T(8,128)(2,1)S(1)} %collective-permute-done.5.refs_0_, bf16[16,3072]{1,0:T(8,128)(2,1)S(1)} %collective-permute-done.6.refs_1_), custom_call_target="tpu_custom_call" | custom-call | flops 301989888 | bytes 2359296 | tf_op jit(solution)/shard_map/own/pallas_call | solution.py:183
  31.0 0.5 %collective-permute-done.7.refs_2_ = bf16[4,32,384]{2,1,0:T(8,128)(2,1)S(1)} collective-permute-done((bf16[4,32,384]{2,1,0:T(8,128)(2,1)S(1)}, bf16[4,32,384]{2,1,0:T(8,128)(2,1)S(1)}, u32[]{:S(2)}, u32[]{:S(2)}) %collective-permute-start.7) | collective-permute-done | bytes 98336 | tf_op jit(solution)/shard_map/ppermute | solution.py:196
  31.5 2.3 %collective-permute-done.8.refs_3_ = bf16[4,32,384]{2,1,0:T(8,128)(2,1)S(1)} collective-permute-done((bf16[4,32,384]{2,1,0:T(8,128)(2,1)S(1)}, bf16[4,32,384]{2,1,0:T(8,128)(2,1)S(1)}, u32[]{:S(2)}, u32[]{:S(2)}) %collective-permute-start.8) | collective-permute-done | bytes 98336 | tf_op jit(solution)/shard_map/ppermute | solution.py:196
  33.9 0.8 %finish.1 = f32[4,64,384]{2,1,0:T(8,128)} custom-call(f32[4,16,384]{2,1,0:T(8,128)S(1)} %get-tuple-element.23.inverse_ref, f32[64,384]{1,0:T(8,128)S(1)} %get-tuple-element.24.ridged_ref, f32[4,32,384]{2,1,0:T(8,128)S(1)} %own.2.refs_0_, f32[4,32,384]{2,1,0:T(8,128)S(1)} %own.3.refs_1_, bf16[4,32,384]{2,1,0:T(8,128)(2,1)S(1)} %collective-permute-done.7.refs_2_, ...), custom_call_target="tpu_custom_call" | custom-call | tf_op jit(solution)/shard_map/finish/pallas_call | solution.py:211
  (6 shorter events, 0.2 us)
Async XLA Ops:
  0.0 8.1 %copy-start = (f32[384,64]{0,1:T(8,128)S(1)}, f32[384,64]{0,1:T(8,128)}, u32[]{:S(2)}) copy-start(f32[384,64]{0,1:T(8,128)} %param.9) | copy-start | bytes 294916
  0.0 8.1 %copy-start.1 = (s32[8]{0:T(128)S(1)}, s32[8]{0:T(128)}, u32[]{:S(2)}) copy-start(s32[8]{0:T(128)} %widths_ref.1) | copy-start | bytes 100
  2.8 1.6 %collective-permute-start = (bf16[32,3072]{1,0:T(8,128)(2,1)S(1)}, bf16[32,3072]{1,0:T(8,128)(2,1)S(1)}, u32[]{:S(2)}, u32[]{:S(2)}) collective-permute-start(bf16[32,3072]{1,0:T(8,128)(2,1)S(1)} %get-tuple-element.18), channel_id=1, source_target_pairs={{0,1},{1,0},{2,3},{3,2},{4,5},{5,4},{6,7},{7,6},{8,9},{9,8},{10,11... | collective-permute-start | bytes 589832 | tf_op jit(solution)/shard_map/ppermute | solution.py:165
  4.5 5.5 %collective-permute-start.1 = (bf16[16,3072]{1,0:T(8,128)(2,1)S(1)}, bf16[16,3072]{1,0:T(8,128)(2,1)S(1)}, u32[]{:S(2)}, u32[]{:S(2)}) collective-permute-start(bf16[16,3072]{1,0:T(8,128)(2,1)S(1)} %dynamic-slice_convert_fusion), channel_id=1, source_target_pairs={{0,2},{1,5},{2,0},{3,7},{4,6},{5,1},{6,4},{7,3},{8,10},{9,13},{10,... | collective-permute-start | bytes 294920 | tf_op jit(solution)/shard_map/ppermute | solution.py:165
  10.1 4.7 %collective-permute-start.2 = (bf16[16,3072]{1,0:T(8,128)(2,1)S(1)}, bf16[16,3072]{1,0:T(8,128)(2,1)S(1)}, u32[]{:S(2)}, u32[]{:S(2)}) collective-permute-start(bf16[16,3072]{1,0:T(8,128)(2,1)S(1)} %convert_element_type.27), channel_id=1, source_target_pairs={{0,4},{1,3},{2,6},{3,1},{4,0},{5,7},{6,2},{7,5},{8,12},{9,11},{10,... | collective-permute-start | bytes 294920 | tf_op jit(solution)/shard_map/ppermute | solution.py:165
  14.8 5.7 %collective-permute-start.3 = (bf16[16,3072]{1,0:T(8,128)(2,1)S(1)}, bf16[16,3072]{1,0:T(8,128)(2,1)S(1)}, u32[]{:S(2)}, u32[]{:S(2)}) collective-permute-start(bf16[16,3072]{1,0:T(8,128)(2,1)S(1)} %fusion), channel_id=1, source_target_pairs={{0,8},{1,9},{2,10},{3,11},{4,12},{5,13},{6,14},{7,15},{8,0},{9,1},... | collective-permute-start | bytes 294920 | tf_op jit(solution)/shard_map/ppermute | solution.py:165
  20.6 4.7 %collective-permute-start.5 = (bf16[16,3072]{1,0:T(8,128)(2,1)S(1)}, bf16[16,3072]{1,0:T(8,128)(2,1)S(1)}, u32[]{:S(2)}, u32[]{:S(2)}) collective-permute-start(bf16[16,3072]{1,0:T(8,128)(2,1)S(1)} %add_convert_fusion.refs_0_), channel_id=1, source_target_pairs={{0,2},{1,5},{2,0},{3,7},{4,6},{5,1},{6,4},{7,3},{8,10},{9,13},{10,... | collective-permute-start | bytes 294920 | tf_op jit(solution)/shard_map/ppermute | solution.py:165
  22.6 2.7 %collective-permute-start.4 = (bf16[16,3072]{1,0:T(8,128)(2,1)S(1)}, bf16[16,3072]{1,0:T(8,128)(2,1)S(1)}, u32[]{:S(2)}, u32[]{:S(2)}) collective-permute-start(bf16[16,3072]{1,0:T(8,128)(2,1)S(1)} %add_convert_fusion.refs_0_), channel_id=1, source_target_pairs={{0,1},{1,0},{2,3},{3,2},{4,5},{5,4},{6,7},{7,6},{8,9},{9,8},{10,11... | collective-permute-start | bytes 294920 | tf_op jit(solution)/shard_map/ppermute | solution.py:165
  25.2 2.8 %collective-permute-start.6 = (bf16[16,3072]{1,0:T(8,128)(2,1)S(1)}, bf16[16,3072]{1,0:T(8,128)(2,1)S(1)}, u32[]{:S(2)}, u32[]{:S(2)}) collective-permute-start(bf16[16,3072]{1,0:T(8,128)(2,1)S(1)} %collective-permute-done.5.refs_0_), channel_id=1, source_target_pairs={{0,1},{1,0},{2,3},{3,2},{4,5},{5,4},{6,7},{7,6},{8,9},{9,8},{10,11... | collective-permute-start | bytes 294920 | tf_op jit(solution)/shard_map/ppermute | solution.py:165
  26.1 5.5 %collective-permute-start.7 = (bf16[4,32,384]{2,1,0:T(8,128)(2,1)S(1)}, bf16[4,32,384]{2,1,0:T(8,128)(2,1)S(1)}, u32[]{:S(2)}, u32[]{:S(2)}) collective-permute-start(bf16[4,32,384]{2,1,0:T(8,128)(2,1)S(1)} %others.2), channel_id=1, source_target_pairs={{0,16},{16,0},{1,17},{17,1},{2,18},{18,2},{3,19},{19,3},{4,20},{20... | collective-permute-start | bytes 294920 | tf_op jit(solution)/shard_map/ppermute | solution.py:196
  28.9 5.0 %collective-permute-start.8 = (bf16[4,32,384]{2,1,0:T(8,128)(2,1)S(1)}, bf16[4,32,384]{2,1,0:T(8,128)(2,1)S(1)}, u32[]{:S(2)}, u32[]{:S(2)}) collective-permute-start(bf16[4,32,384]{2,1,0:T(8,128)(2,1)S(1)} %others.3), channel_id=1, source_target_pairs={{0,16},{16,0},{1,17},{17,1},{2,18},{18,2},{3,19},{19,3},{4,20},{20... | collective-permute-start | bytes 294920 | tf_op jit(solution)/shard_map/ppermute | solution.py:196

commit v3 on v2

--- a/solution.py
+++ b/solution.py
@@ -62,6 +62,7 @@
     sections = widths_ref.shape[0]
     _, rows, variants = own_ref.shape
     per_device = inverse_ref.shape[0]
+    near = others_ref.shape[0]
     rhs = dir_ref.shape[0]
     chrom = lax.axis_index("chrom")
     side = (chrom // (lax.axis_size("chrom") // 2)) % 2
@@ -77,9 +78,11 @@
         def _():
             own_ref[c % (sections // 2)] = outside
 
-        @pl.when(jnp.logical_not(here))
-        def _():
-            others_ref[c % (sections // 2)] = outside
+        if sections // 2 - near <= c < sections // 2 + near:
+
+            @pl.when(jnp.logical_not(here))
+            def _():
+                others_ref[c - (sections // 2 - near if c < sections // 2 else sections // 2)] = outside
 
         start = end
     for c in range(per_device):
@@ -93,23 +96,33 @@
 def section_kernel(outside_ref, stand_ref, *refs):
     *pieces, out_ref = refs
     count = outside_ref.shape[0]
-    spread = [p[...] * outside_ref[c] for c in range(count) for p in pieces]
+    spread = [p[...] for p in pieces] if out_ref.shape[0] > count else []
+    spread += [p[...] * outside_ref[c] for c in range(count) for p in pieces]
     product = lax.dot_general(
         jnp.concatenate(spread, axis=0), stand_ref[...], (((1,), (1,)), ((), ())), preferred_element_type=jnp.float32
     )
     out_ref[...] = product.reshape(out_ref.shape).astype(out_ref.dtype)
 
 
-def finish_kernel(inverse_ref, ridged_ref, *refs):
+def received(c, sections, near, side):
+    if sections // 2 <= near:
+        return c + 1
+    low = c - (sections // 2 - near) + 1
+    return jnp.where(side == 0, max(low, 0), c + 1 if c < near else 0)
+
+
+def finish_kernel(near, inverse_ref, ridged_ref, *refs):
     owns, gots, out_ref = refs[:2], refs[2:4], refs[4]
     per_device, rhs, _ = out_ref.shape
+    side = lax.axis_index("chrom")
+    places = [received(c, 2 * per_device, near, side) if near else c for c in range(per_device)]
     quarter = rhs // 4
     for p, row in enumerate(piece_rows(rhs)):
         at = pl.ds(pl.multiple_of(row, quarter), quarter)
         ridged = ridged_ref[pl.ds(p * quarter, quarter), :]
         here = pl.ds((p % 2) * quarter, quarter)
         for c in range(per_device):
-            rest = owns[p // 2][c, here, :] + gots[p // 2][c, here, :].astype(jnp.float32)
+            rest = owns[p // 2][c, here, :] + gots[p // 2][places[c], here, :].astype(jnp.float32)
             out_ref[c, at, :] = ridged + rest * inverse_ref[c]
 
 
@@ -146,12 +159,13 @@
         name="cross",
     )(*(pltpu.with_memory_space_constraint(a, pltpu.HBM) for a in operands))
 
-    mask = jax.ShapeDtypeStruct((sections // 2, quarter, variants), jnp.bfloat16)
+    near = max(1, sections // 4)
+    mask = lambda count: jax.ShapeDtypeStruct((count, quarter, variants), jnp.bfloat16)
     outside_others, outside_own, inverse, ridged = pl.pallas_call(
         functools.partial(prepare_kernel, variants * n_chrom),
         out_shape=(
-            mask,
-            mask,
+            mask(near),
+            mask(sections // 2),
             jax.ShapeDtypeStruct((per_device, quarter, rows), jnp.float32),
             jax.ShapeDtypeStruct((rhs, rows), jnp.float32),
         ),
@@ -177,12 +191,11 @@
         mine_sum = mine_sum + swap(mine_sum.astype(jnp.bfloat16), even, odd)
     first = mine_sum.astype(jnp.bfloat16)
     second = swap(first, 2, 4)
-    halves = ((first, swap(first, 1, 1)), (second, swap(second, 1, 1)))
-
-    def products(outside, pieces, dtype, name):
+
+    def products(outside, pieces, count, dtype, name):
         return pl.pallas_call(
             section_kernel,
-            out_shape=jax.ShapeDtypeStruct((sections // 2, half, rows), dtype),
+            out_shape=jax.ShapeDtypeStruct((count, half, rows), dtype),
             in_specs=[vmem] * 4,
             out_specs=vmem,
             compiler_params=params,
@@ -196,8 +209,17 @@
         return lax.ppermute(x, "chrom", [(i, i ^ bit) for i in range(n_chrom)])
 
     bit = n_chrom // 2
-    gots = [swap_chrom(products(outside_others, pieces, jnp.bfloat16, "others"), bit) for pieces in halves]
-    owns = [products(outside_own, pieces, jnp.float32, "own") for pieces in halves]
+    for_others = lambda pieces: products(outside_others, pieces, near + 1, jnp.bfloat16, "others")
+    head = (first, swap(first, 1, 1))
+    products_head = for_others(head)
+    second, products_head = lax.optimization_barrier((second, products_head))
+    tail = (second, swap(second, 1, 1))
+    gots = [swap_chrom(products_head, bit), swap_chrom(for_others(tail), bit)]
+    owns = [products(outside_own, pieces, sections // 2, jnp.float32, "own") for pieces in (head, tail)]
+    if bit > 1:
+        side = (lax.axis_index("chrom") // bit) % 2
+        places = [received(c, sections, near, side) for c in range(sections // 2)]
+        gots = [jnp.stack([lax.dynamic_index_in_dim(got, p, 0, False) for p in places]) for got in gots]
     while bit > 1:
         bit //= 2
         count = owns[0].shape[0] // 2
@@ -209,7 +231,7 @@
         owns = [lax.dynamic_slice_in_dim(s, side * count, count, 0) for s in sums]
 
     out = pl.pallas_call(
-        finish_kernel,
+        functools.partial(finish_kernel, near if n_chrom == 2 else 0),
         out_shape=jax.ShapeDtypeStruct((per_device, rhs, rows), jnp.float32),
         in_specs=[vmem] * 6,
         out_specs=vmem,

time: 34.9 us -> 33.4 us (0.957)
  waiting for transfers between devices: 12.9 us -> 10.8 us
  starting transfers between devices: 13.2 us -> 13.9 us
    ppermute x2, waiting for transfers between devices: 2.87 us -> 1.45 us  [swap_chrom(): return lax.ppermute(x, 'chrom', [(i, i ^ bit) for i in range(n_chrom)])]
    ppermute x2, starting transfers between devices: 2.46 us -> 3.19 us  [swap_chrom(): return lax.ppermute(x, 'chrom', [(i, i ^ bit) for i in range(n_chrom)])]
    ppermute x7, waiting for transfers between devices: 10.1 us -> 9.35 us  [swap(): lax.ppermute(x, 'samp', [(i, i ^ (odd if i % 2 else even)) for i in range...]
  transfers between devices with their start and end apart: 9 -> 9, of which waited for: 7 -> 6; matrix products, arithmetic and copies ran while one was open for 0% -> 0% of each run, Pallas kernels for 12% -> 12%
where the time goes in v3:
time: 33.4 us; the launch traced here: 33.3 us
  starting transfers between devices  13.9 us (42%)
  waiting for transfers between devices  10.8 us (32%)
  Pallas kernels  7.67 us (23%)
  between operations  0.76 us (2%)
    ppermute x7, starting transfers between devices, swap(): lax.ppermute(x, 'samp', [(i, i ^ (odd if i % 2 else even)) for i in range...  10.7 us
    ppermute x7, waiting for transfers between devices, swap(): lax.ppermute(x, 'samp', [(i, i ^ (odd if i % 2 else even)) for i in range...  9.35 us
    pallas_call x4, Pallas kernels, products(): pl.pallas_call(section_kernel, out_shape=jax.ShapeDtypeStruct((count, hal...  3.29 us
    ppermute x2, starting transfers between devices, swap_chrom(): return lax.ppermute(x, 'chrom', [(i, i ^ bit) for i in range(n_chrom)])  3.19 us
    pallas_call x1, Pallas kernels, on_device(): pl.pallas_call(functools.partial(cross_kernel, blocks), out_shape=(jax.Sh...  2.8 us
    ppermute x2, waiting for transfers between devices, swap_chrom(): return lax.ppermute(x, 'chrom', [(i, i ^ bit) for i in range(n_chrom)])  1.45 us
    pallas_call x1, Pallas kernels, on_device(): pl.pallas_call(functools.partial(finish_kernel, near if n_chrom == 2 else...  0.83 us
    pallas_call x1, Pallas kernels, on_device(): pl.pallas_call(functools.partial(prepare_kernel, variants * n_chrom), out...  0.76 us
  transfers between devices with their start and end apart: 9, of which 6 were waited for; matrix products, arithmetic and copies ran while one was open for 0% of the time, Pallas kernels for 12%

profile of v3, /device:TPU:0, one launch (start us, length us, event | category | flops | bytes accessed | tf_op | source)
XLA Modules:
  0.0 33.3 jit_solution(18196058261732552157)
XLA Ops:
  0.0 0.0 copy-start
  0.0 0.0 copy-start.1
  0.0 2.8 %cross.1 = (bf16[384,3072]{1,0:T(8,128)(2,1)S(1)}, f32[32,3072]{1,0:T(8,128)S(1)}, bf16[32,3072]{1,0:T(8,128)(2,1)S(1)}) custom-call(s32[384,3072]{1,0:T(8,128)} %geno_hbm.1, f32[1,3072]{1,0:T(1,128)} %bitcast.5, f32[64,384]{1,0:T(8,128)} %bitcast.3), custom_call_target="tpu_custom_call" | custom-call | tf_op jit(solution)/shard_map/cross/pallas_call | solution.py:143
  2.8 0.5 %collective-permute-start = (bf16[32,3072]{1,0:T(8,128)(2,1)S(1)}, bf16[32,3072]{1,0:T(8,128)(2,1)S(1)}, u32[]{:S(2)}, u32[]{:S(2)}) collective-permute-start(bf16[32,3072]{1,0:T(8,128)(2,1)S(1)} %get-tuple-element.20), channel_id=1, source_target_pairs={{0,1},{1,0},{2,3},{3,2},{4,5},{5,4},{6,7},{7,6},{8,9},{9,8},{10,11... | collective-permute-start | bytes 589832 | tf_op jit(solution)/shard_map/ppermute | solution.py:179
  3.3 1.1 %collective-permute-done = bf16[32,3072]{1,0:T(8,128)(2,1)S(1)} collective-permute-done((bf16[32,3072]{1,0:T(8,128)(2,1)S(1)}, bf16[32,3072]{1,0:T(8,128)(2,1)S(1)}, u32[]{:S(2)}, u32[]{:S(2)}) %collective-permute-start) | collective-permute-done | bytes 196640 | tf_op jit(solution)/shard_map/ppermute | solution.py:179
  4.5 3.0 %collective-permute-start.1 = (bf16[16,3072]{1,0:T(8,128)(2,1)S(1)}, bf16[16,3072]{1,0:T(8,128)(2,1)S(1)}, u32[]{:S(2)}, u32[]{:S(2)}) collective-permute-start(bf16[16,3072]{1,0:T(8,128)(2,1)S(1)} %dynamic-slice_convert_fusion), channel_id=1, source_target_pairs={{0,2},{1,5},{2,0},{3,7},{4,6},{5,1},{6,4},{7,3},{8,10},{9,13},{10,... | collective-permute-start | bytes 294920 | tf_op jit(solution)/shard_map/ppermute | solution.py:179
  8.1 0.0 copy-done
  8.1 0.0 copy-done.1
  8.1 0.8 %prepare.1 = (bf16[2,16,3072]{2,1,0:T(8,128)(2,1)S(1)}, bf16[4,16,3072]{2,1,0:T(8,128)(2,1)S(1)}, f32[4,16,384]{2,1,0:T(8,128)S(1)}, f32[64,384]{1,0:T(8,128)S(1)}) custom-call(s32[8]{0:T(128)S(1)} %copy-done.1, f32[1]{0:T(128)S(6)} %copy.6.ridge_ref, f32[64,384]{1,0:T(8,128)S(1)} %bitcast.4), custom_call_target="tpu_custom_call" | custom-call | tf_op jit(solution)/shard_map/prepare/pallas_call | solution.py:164
  8.9 1.2 %collective-permute-done.1 = bf16[16,3072]{1,0:T(8,128)(2,1)S(1)} collective-permute-done((bf16[16,3072]{1,0:T(8,128)(2,1)S(1)}, bf16[16,3072]{1,0:T(8,128)(2,1)S(1)}, u32[]{:S(2)}, u32[]{:S(2)}) %collective-permute-start.1) | collective-permute-done | bytes 98336 | tf_op jit(solution)/shard_map/ppermute | solution.py:179
  10.1 2.1 %collective-permute-start.2 = (bf16[16,3072]{1,0:T(8,128)(2,1)S(1)}, bf16[16,3072]{1,0:T(8,128)(2,1)S(1)}, u32[]{:S(2)}, u32[]{:S(2)}) collective-permute-start(bf16[16,3072]{1,0:T(8,128)(2,1)S(1)} %convert_element_type.27), channel_id=1, source_target_pairs={{0,4},{1,3},{2,6},{3,1},{4,0},{5,7},{6,2},{7,5},{8,12},{9,11},{10,... | collective-permute-start | bytes 294920 | tf_op jit(solution)/shard_map/ppermute | solution.py:179
  12.2 2.6 %collective-permute-done.2 = bf16[16,3072]{1,0:T(8,128)(2,1)S(1)} collective-permute-done((bf16[16,3072]{1,0:T(8,128)(2,1)S(1)}, bf16[16,3072]{1,0:T(8,128)(2,1)S(1)}, u32[]{:S(2)}, u32[]{:S(2)}) %collective-permute-start.2) | collective-permute-done | bytes 98336 | tf_op jit(solution)/shard_map/ppermute | solution.py:179
  14.8 3.1 %collective-permute-start.3 = (bf16[16,3072]{1,0:T(8,128)(2,1)S(1)}, bf16[16,3072]{1,0:T(8,128)(2,1)S(1)}, u32[]{:S(2)}, u32[]{:S(2)}) collective-permute-start(bf16[16,3072]{1,0:T(8,128)(2,1)S(1)} %fusion), channel_id=1, source_target_pairs={{0,8},{1,9},{2,10},{3,11},{4,12},{5,13},{6,14},{7,15},{8,0},{9,1},... | collective-permute-start | bytes 294920 | tf_op jit(solution)/shard_map/ppermute | solution.py:179
  17.9 2.6 %collective-permute-done.3 = bf16[16,3072]{1,0:T(8,128)(2,1)S(1)} collective-permute-done((bf16[16,3072]{1,0:T(8,128)(2,1)S(1)}, bf16[16,3072]{1,0:T(8,128)(2,1)S(1)}, u32[]{:S(2)}, u32[]{:S(2)}) %collective-permute-start.3) | collective-permute-done | bytes 98336 | tf_op jit(solution)/shard_map/ppermute | solution.py:179
  20.6 0.1 collective-permute-start.4
  20.7 1.9 %collective-permute-start.5 = (bf16[16,3072]{1,0:T(8,128)(2,1)S(1)}, bf16[16,3072]{1,0:T(8,128)(2,1)S(1)}, u32[]{:S(2)}, u32[]{:S(2)}) collective-permute-start(bf16[16,3072]{1,0:T(8,128)(2,1)S(1)} %add_convert_fusion.refs_0_), channel_id=1, source_target_pairs={{0,2},{1,5},{2,0},{3,7},{4,6},{5,1},{6,4},{7,3},{8,10},{9,13},{10,... | collective-permute-start | bytes 294920 | tf_op jit(solution)/shard_map/ppermute | solution.py:179
  22.6 0.0 collective-permute-done.4.refs_1_
  22.6 0.8 %others.2 = bf16[3,32,384]{2,1,0:T(8,128)(2,1)S(1)} custom-call(bf16[2,16,3072]{2,1,0:T(8,128)(2,1)S(1)} %get-tuple-element.30.outside_ref, bf16[384,3072]{1,0:T(8,128)(2,1)S(1)} %get-tuple-element.28.stand_ref, bf16[16,3072]{1,0:T(8,128)(2,1)S(1)} %add_convert_fusion.refs_0_, bf16[16,3072]{1,0:T(8,128)(2,1)S(1)} %collective-permute-done.4.refs_1_), custom_call_target="tpu_custom_call" | custom-call | flops 301989888 | bytes 2359296 | tf_op jit(solution)/shard_map/others/pallas_call | solution.py:196
  23.4 1.9 %collective-permute-done.5.refs_0_ = bf16[16,3072]{1,0:T(8,128)(2,1)S(1)} collective-permute-done((bf16[16,3072]{1,0:T(8,128)(2,1)S(1)}, bf16[16,3072]{1,0:T(8,128)(2,1)S(1)}, u32[]{:S(2)}, u32[]{:S(2)}) %collective-permute-start.5) | collective-permute-done | bytes 98336 | tf_op jit(solution)/shard_map/ppermute | solution.py:179
  25.3 0.0 collective-permute-start.6
  25.3 1.8 %collective-permute-start.7 = (bf16[3,32,384]{2,1,0:T(8,128)(2,1)S(1)}, bf16[3,32,384]{2,1,0:T(8,128)(2,1)S(1)}, u32[]{:S(2)}, u32[]{:S(2)}) collective-permute-start(bf16[3,32,384]{2,1,0:T(8,128)(2,1)S(1)} %others.2), channel_id=1, source_target_pairs={{0,16},{16,0},{1,17},{17,1},{2,18},{18,2},{3,19},{19,3},{4,20},{20... | collective-permute-start | bytes 221192 | tf_op jit(solution)/shard_map/ppermute | solution.py:209
  27.2 0.0 collective-permute-done.6.refs_1_
  27.2 0.8 %others.3 = bf16[3,32,384]{2,1,0:T(8,128)(2,1)S(1)} custom-call(bf16[2,16,3072]{2,1,0:T(8,128)(2,1)S(1)} %get-tuple-element.30.outside_ref, bf16[384,3072]{1,0:T(8,128)(2,1)S(1)} %get-tuple-element.28.stand_ref, bf16[16,3072]{1,0:T(8,128)(2,1)S(1)} %collective-permute-done.5.refs_0_, bf16[16,3072]{1,0:T(8,128)(2,1)S(1)} %collective-permute-done.6.refs_1_), custom_call_target="tpu_custom_call" | custom-call | flops 301989888 | bytes 2359296 | tf_op jit(solution)/shard_map/others/pallas_call | solution.py:196
  28.0 1.4 %collective-permute-start.8 = (bf16[3,32,384]{2,1,0:T(8,128)(2,1)S(1)}, bf16[3,32,384]{2,1,0:T(8,128)(2,1)S(1)}, u32[]{:S(2)}, u32[]{:S(2)}) collective-permute-start(bf16[3,32,384]{2,1,0:T(8,128)(2,1)S(1)} %others.3), channel_id=1, source_target_pairs={{0,16},{16,0},{1,17},{17,1},{2,18},{18,2},{3,19},{19,3},{4,20},{20... | collective-permute-start | bytes 221192 | tf_op jit(solution)/shard_map/ppermute | solution.py:209
  29.4 0.8 %own.2.refs_0_ = f32[4,32,384]{2,1,0:T(8,128)S(1)} custom-call(bf16[4,16,3072]{2,1,0:T(8,128)(2,1)S(1)} %get-tuple-element.27.outside_ref, bf16[384,3072]{1,0:T(8,128)(2,1)S(1)} %get-tuple-element.28.stand_ref, bf16[16,3072]{1,0:T(8,128)(2,1)S(1)} %add_convert_fusion.refs_0_, bf16[16,3072]{1,0:T(8,128)(2,1)S(1)} %collective-permute-done.4.refs_1_), custom_call_target="tpu_custom_call" | custom-call | flops 301989888 | bytes 2359296 | tf_op jit(solution)/shard_map/own/pallas_call | solution.py:196
  30.2 0.8 %own.3.refs_1_ = f32[4,32,384]{2,1,0:T(8,128)S(1)} custom-call(bf16[4,16,3072]{2,1,0:T(8,128)(2,1)S(1)} %get-tuple-element.27.outside_ref, bf16[384,3072]{1,0:T(8,128)(2,1)S(1)} %get-tuple-element.28.stand_ref, bf16[16,3072]{1,0:T(8,128)(2,1)S(1)} %collective-permute-done.5.refs_0_, bf16[16,3072]{1,0:T(8,128)(2,1)S(1)} %collective-permute-done.6.refs_1_), custom_call_target="tpu_custom_call" | custom-call | flops 301989888 | bytes 2359296 | tf_op jit(solution)/shard_map/own/pallas_call | solution.py:196
  31.0 0.0 collective-permute-done.7.refs_2_
  31.0 1.4 %collective-permute-done.8.refs_3_ = bf16[3,32,384]{2,1,0:T(8,128)(2,1)S(1)} collective-permute-done((bf16[3,32,384]{2,1,0:T(8,128)(2,1)S(1)}, bf16[3,32,384]{2,1,0:T(8,128)(2,1)S(1)}, u32[]{:S(2)}, u32[]{:S(2)}) %collective-permute-start.8) | collective-permute-done | bytes 73760 | tf_op jit(solution)/shard_map/ppermute | solution.py:209
  32.5 0.8 %finish.1 = f32[4,64,384]{2,1,0:T(8,128)} custom-call(f32[4,16,384]{2,1,0:T(8,128)S(1)} %get-tuple-element.25.inverse_ref, f32[64,384]{1,0:T(8,128)S(1)} %get-tuple-element.26.ridged_ref, f32[4,32,384]{2,1,0:T(8,128)S(1)} %own.2.refs_0_, f32[4,32,384]{2,1,0:T(8,128)S(1)} %own.3.refs_1_, bf16[3,32,384]{2,1,0:T(8,128)(2,1)S(1)} %collective-permute-done.7.refs_2_, ...), custom_call_target="tpu_custom_call" | custom-call | tf_op jit(solution)/shard_map/finish/pallas_call | solution.py:233
  (6 shorter events, 0.2 us)
Async XLA Ops:
  0.0 8.1 %copy-start = (f32[384,64]{0,1:T(8,128)S(1)}, f32[384,64]{0,1:T(8,128)}, u32[]{:S(2)}) copy-start(f32[384,64]{0,1:T(8,128)} %param.9) | copy-start | bytes 294916
  0.0 8.1 %copy-start.1 = (s32[8]{0:T(128)S(1)}, s32[8]{0:T(128)}, u32[]{:S(2)}) copy-start(s32[8]{0:T(128)} %widths_ref.1) | copy-start | bytes 100
  2.8 1.6 %collective-permute-start = (bf16[32,3072]{1,0:T(8,128)(2,1)S(1)}, bf16[32,3072]{1,0:T(8,128)(2,1)S(1)}, u32[]{:S(2)}, u32[]{:S(2)}) collective-permute-start(bf16[32,3072]{1,0:T(8,128)(2,1)S(1)} %get-tuple-element.20), channel_id=1, source_target_pairs={{0,1},{1,0},{2,3},{3,2},{4,5},{5,4},{6,7},{7,6},{8,9},{9,8},{10,11... | collective-permute-start | bytes 589832 | tf_op jit(solution)/shard_map/ppermute | solution.py:179
  4.5 5.5 %collective-permute-start.1 = (bf16[16,3072]{1,0:T(8,128)(2,1)S(1)}, bf16[16,3072]{1,0:T(8,128)(2,1)S(1)}, u32[]{:S(2)}, u32[]{:S(2)}) collective-permute-start(bf16[16,3072]{1,0:T(8,128)(2,1)S(1)} %dynamic-slice_convert_fusion), channel_id=1, source_target_pairs={{0,2},{1,5},{2,0},{3,7},{4,6},{5,1},{6,4},{7,3},{8,10},{9,13},{10,... | collective-permute-start | bytes 294920 | tf_op jit(solution)/shard_map/ppermute | solution.py:179
  10.1 4.7 %collective-permute-start.2 = (bf16[16,3072]{1,0:T(8,128)(2,1)S(1)}, bf16[16,3072]{1,0:T(8,128)(2,1)S(1)}, u32[]{:S(2)}, u32[]{:S(2)}) collective-permute-start(bf16[16,3072]{1,0:T(8,128)(2,1)S(1)} %convert_element_type.27), channel_id=1, source_target_pairs={{0,4},{1,3},{2,6},{3,1},{4,0},{5,7},{6,2},{7,5},{8,12},{9,11},{10,... | collective-permute-start | bytes 294920 | tf_op jit(solution)/shard_map/ppermute | solution.py:179
  14.8 5.7 %collective-permute-start.3 = (bf16[16,3072]{1,0:T(8,128)(2,1)S(1)}, bf16[16,3072]{1,0:T(8,128)(2,1)S(1)}, u32[]{:S(2)}, u32[]{:S(2)}) collective-permute-start(bf16[16,3072]{1,0:T(8,128)(2,1)S(1)} %fusion), channel_id=1, source_target_pairs={{0,8},{1,9},{2,10},{3,11},{4,12},{5,13},{6,14},{7,15},{8,0},{9,1},... | collective-permute-start | bytes 294920 | tf_op jit(solution)/shard_map/ppermute | solution.py:179
  20.6 2.0 %collective-permute-start.4 = (bf16[16,3072]{1,0:T(8,128)(2,1)S(1)}, bf16[16,3072]{1,0:T(8,128)(2,1)S(1)}, u32[]{:S(2)}, u32[]{:S(2)}) collective-permute-start(bf16[16,3072]{1,0:T(8,128)(2,1)S(1)} %add_convert_fusion.refs_0_), channel_id=1, source_target_pairs={{0,1},{1,0},{2,3},{3,2},{4,5},{5,4},{6,7},{7,6},{8,9},{9,8},{10,11... | collective-permute-start | bytes 294920 | tf_op jit(solution)/shard_map/ppermute | solution.py:179
  20.7 4.7 %collective-permute-start.5 = (bf16[16,3072]{1,0:T(8,128)(2,1)S(1)}, bf16[16,3072]{1,0:T(8,128)(2,1)S(1)}, u32[]{:S(2)}, u32[]{:S(2)}) collective-permute-start(bf16[16,3072]{1,0:T(8,128)(2,1)S(1)} %add_convert_fusion.refs_0_), channel_id=1, source_target_pairs={{0,2},{1,5},{2,0},{3,7},{4,6},{5,1},{6,4},{7,3},{8,10},{9,13},{10,... | collective-permute-start | bytes 294920 | tf_op jit(solution)/shard_map/ppermute | solution.py:179
  25.3 1.8 %collective-permute-start.6 = (bf16[16,3072]{1,0:T(8,128)(2,1)S(1)}, bf16[16,3072]{1,0:T(8,128)(2,1)S(1)}, u32[]{:S(2)}, u32[]{:S(2)}) collective-permute-start(bf16[16,3072]{1,0:T(8,128)(2,1)S(1)} %collective-permute-done.5.refs_0_), channel_id=1, source_target_pairs={{0,1},{1,0},{2,3},{3,2},{4,5},{5,4},{6,7},{7,6},{8,9},{9,8},{10,11... | collective-permute-start | bytes 294920 | tf_op jit(solution)/shard_map/ppermute | solution.py:179
  25.3 5.7 %collective-permute-start.7 = (bf16[3,32,384]{2,1,0:T(8,128)(2,1)S(1)}, bf16[3,32,384]{2,1,0:T(8,128)(2,1)S(1)}, u32[]{:S(2)}, u32[]{:S(2)}) collective-permute-start(bf16[3,32,384]{2,1,0:T(8,128)(2,1)S(1)} %others.2), channel_id=1, source_target_pairs={{0,16},{16,0},{1,17},{17,1},{2,18},{18,2},{3,19},{19,3},{4,20},{20... | collective-permute-start | bytes 221192 | tf_op jit(solution)/shard_map/ppermute | solution.py:209
  28.0 4.5 %collective-permute-start.8 = (bf16[3,32,384]{2,1,0:T(8,128)(2,1)S(1)}, bf16[3,32,384]{2,1,0:T(8,128)(2,1)S(1)}, u32[]{:S(2)}, u32[]{:S(2)}) collective-permute-start(bf16[3,32,384]{2,1,0:T(8,128)(2,1)S(1)} %others.3), channel_id=1, source_target_pairs={{0,16},{16,0},{1,17},{17,1},{2,18},{18,2},{3,19},{19,3},{4,20},{20... | collective-permute-start | bytes 221192 | tf_op jit(solution)/shard_map/ppermute | solution.py:209

commit v4 on v3

--- a/solution.py
+++ b/solution.py
@@ -17,7 +17,19 @@
     return core, jnp.where(core == 0, y, z), jnp.where(core == 0, z, y)
 
 
-def cross_kernel(blocks, geno_hbm, freq_hbm, dir_hbm, stand_ref, keep_ref, send_ref, geno, freq_ref, dir_ref, sems):
+def piece_rows(rhs):
+    core, mine, sibling = core_and_bits()
+    half, quarter = rhs // 2, rhs // 4
+    return [
+        core * half + mine * quarter,
+        (1 - core) * half + sibling * quarter,
+        core * half + (1 - mine) * quarter,
+        (1 - core) * half + (1 - sibling) * quarter,
+    ]
+
+
+def cross_kernel(blocks, geno_hbm, freq_hbm, dir_hbm, stand_ref, *refs):
+    quarters, (geno, freq_ref, dir_ref, sems) = refs[:4], refs[4:]
     width = geno_hbm.shape[1] // blocks
     small = [
         pltpu.make_async_copy(freq_hbm, freq_ref, sems.at[blocks]),
@@ -30,11 +42,13 @@
         columns = pl.ds(i * width, width)
         copies.append(pltpu.make_async_copy(geno_hbm.at[:, columns], geno.at[:, columns], sems.at[i]))
         copies[-1].start()
-    half = dir_ref.shape[0] // 2
-    first = lax.axis_index("samp") % 2 == 0
+    quarter = dir_ref.shape[0] // 4
+    mine, sibling, sent, sibling_sent = piece_rows(dir_ref.shape[0])
     for copy in small:
         copy.wait()
-    vector = dir_ref[...].astype(jnp.bfloat16)
+    vector = jnp.concatenate(
+        [dir_ref[pl.ds(pl.multiple_of(row, quarter), quarter), :] for row in (sibling_sent, sibling, sent, mine)], axis=0
+    ).astype(jnp.bfloat16)
     for i in range(blocks):
         columns = pl.ds(i * width, width)
         doubled = 2.0 * freq_ref[:, columns]
@@ -43,19 +57,8 @@
         standard = ((geno[:, columns].astype(jnp.float32) - doubled) * scale).astype(jnp.bfloat16)
         stand_ref[:, columns] = standard
         crossed = jnp.dot(vector, standard, preferred_element_type=jnp.float32)
-        keep_ref[:, columns] = jnp.where(first, crossed[:half], crossed[half:])
-        send_ref[:, columns] = jnp.where(first, crossed[half:], crossed[:half]).astype(jnp.bfloat16)
-
-
-def piece_rows(rhs):
-    core, mine, sibling = core_and_bits()
-    half, quarter = rhs // 2, rhs // 4
-    return [
-        core * half + mine * quarter,
-        (1 - core) * half + sibling * quarter,
-        core * half + (1 - mine) * quarter,
-        (1 - core) * half + (1 - sibling) * quarter,
-    ]
+        for q, ref in enumerate(quarters):
+            ref[:, columns] = crossed[q * quarter : (q + 1) * quarter].astype(ref.dtype)
 
 
 def prepare_kernel(total, widths_ref, ridge_ref, dir_ref, others_ref, own_ref, inverse_ref, ridged_ref):
@@ -93,26 +96,32 @@
         ridged_ref[pl.ds(p * quarter, quarter), :] = ridge_ref[0] * dir_ref[pl.ds(pl.multiple_of(row, quarter), quarter), :]
 
 
-def section_kernel(outside_ref, stand_ref, *refs):
-    *pieces, out_ref = refs
+def received(c, sections, near, side):
+    if sections // 2 <= near:
+        return c + 1
+    low = c - (sections // 2 - near) + 1
+    return jnp.where(side == 0, max(low, 0), c + 1 if c < near else 0)
+
+
+def section_kernel(near, outside_ref, stand_ref, *refs):
+    pieces, got_ref, out_ref = refs[:2], refs[2], refs[-1]
     count = outside_ref.shape[0]
     spread = [p[...] for p in pieces] if out_ref.shape[0] > count else []
     spread += [p[...] * outside_ref[c] for c in range(count) for p in pieces]
     product = lax.dot_general(
         jnp.concatenate(spread, axis=0), stand_ref[...], (((1,), (1,)), ((), ())), preferred_element_type=jnp.float32
     )
-    out_ref[...] = product.reshape(out_ref.shape).astype(out_ref.dtype)
-
-
-def received(c, sections, near, side):
-    if sections // 2 <= near:
-        return c + 1
-    low = c - (sections // 2 - near) + 1
-    return jnp.where(side == 0, max(low, 0), c + 1 if c < near else 0)
+    product = product.reshape(out_ref.shape)
+    if not near:
+        out_ref[...] = product.astype(out_ref.dtype)
+        return
+    side = lax.axis_index("chrom")
+    for c in range(count):
+        out_ref[c] = product[c] + got_ref[received(c, 2 * count, near, side)].astype(jnp.float32)
 
 
 def finish_kernel(near, inverse_ref, ridged_ref, *refs):
-    owns, gots, out_ref = refs[:2], refs[2:4], refs[4]
+    head_ref, tail_ref, got_ref, out_ref = refs
     per_device, rhs, _ = out_ref.shape
     side = lax.axis_index("chrom")
     places = [received(c, 2 * per_device, near, side) if near else c for c in range(per_device)]
@@ -122,7 +131,10 @@
         ridged = ridged_ref[pl.ds(p * quarter, quarter), :]
         here = pl.ds((p % 2) * quarter, quarter)
         for c in range(per_device):
-            rest = owns[p // 2][c, here, :] + gots[p // 2][places[c], here, :].astype(jnp.float32)
+            if p < 2:
+                rest = head_ref[c, here, :]
+            else:
+                rest = tail_ref[c, here, :] + got_ref[places[c], here, :].astype(jnp.float32)
             out_ref[c, at, :] = ridged + rest * inverse_ref[c]
 
 
@@ -140,15 +152,15 @@
 
     blocks = max(1, variants // BLOCK)
     operands = (genotypes, frequency.reshape(1, variants), dir_t)
-    standard, keep, send = pl.pallas_call(
+    parts = [jax.ShapeDtypeStruct((quarter, variants), dtype) for dtype in (jnp.bfloat16, jnp.float32)]
+    standard, give_first, give_second, keep_first, keep_second = pl.pallas_call(
         functools.partial(cross_kernel, blocks),
         out_shape=(
             jax.ShapeDtypeStruct((rows, variants), jnp.bfloat16),
-            jax.ShapeDtypeStruct((half, variants), jnp.float32),
-            jax.ShapeDtypeStruct((half, variants), jnp.bfloat16),
+            *(parts[i] for i in (0, 0, 1, 1)),
         ),
         in_specs=[pl.BlockSpec(memory_space=pl.ANY)] * 3,
-        out_specs=(vmem, vmem, vmem),
+        out_specs=(vmem,) * 5,
         scratch_shapes=[
             pltpu.VMEM((rows, variants), jnp.int32),
             pltpu.VMEM((1, variants), jnp.float32),
@@ -178,10 +190,8 @@
     def swap(x, even, odd):
         return lax.ppermute(x, "samp", [(i, i ^ (odd if i % 2 else even)) for i in range(n_samp)])
 
-    _, mine, _ = core_and_bits()
-    sums = keep + swap(send, 1, 1)
-    at = lambda b: lax.dynamic_slice_in_dim(sums, b * quarter, quarter, 0)
-    mine_sum = at(mine) + swap(at(1 - mine).astype(jnp.bfloat16), 2, 4)
+    sent = (keep_first + swap(give_first, 1, 1)).astype(jnp.bfloat16)
+    mine_sum = keep_second + swap(give_second, 1, 1) + swap(sent, 2, 4)
     mine_sum, outside_others, outside_own, inverse, ridged = lax.optimization_barrier(
         (mine_sum, outside_others, outside_own, inverse, ridged)
     )
@@ -190,20 +200,20 @@
     for even, odd in zip(even_bits, odd_bits):
         mine_sum = mine_sum + swap(mine_sum.astype(jnp.bfloat16), even, odd)
     first = mine_sum.astype(jnp.bfloat16)
-    second = swap(first, 2, 4)
-
-    def products(outside, pieces, count, dtype, name):
+    second, second_sibling = swap(first, 2, 4), swap(first, 3, 5)
+
+    def products(outside, pieces, count, dtype, name, *got):
         return pl.pallas_call(
-            section_kernel,
+            functools.partial(section_kernel, near if got else 0),
             out_shape=jax.ShapeDtypeStruct((count, half, rows), dtype),
-            in_specs=[vmem] * 4,
+            in_specs=[vmem] * (4 + len(got)),
             out_specs=vmem,
             compiler_params=params,
             cost_estimate=pl.CostEstimate(
                 flops=rows * variants * half * sections, bytes_accessed=rows * variants * 2, transcendentals=0
             ),
             name=name,
-        )(outside, standard, *pieces)
+        )(outside, standard, *pieces, *got)
 
     def swap_chrom(x, bit):
         return lax.ppermute(x, "chrom", [(i, i ^ bit) for i in range(n_chrom)])
@@ -212,11 +222,13 @@
     for_others = lambda pieces: products(outside_others, pieces, near + 1, jnp.bfloat16, "others")
     head = (first, swap(first, 1, 1))
     products_head = for_others(head)
-    second, products_head = lax.optimization_barrier((second, products_head))
-    tail = (second, swap(second, 1, 1))
+    tail = (second, second_sibling)
     gots = [swap_chrom(products_head, bit), swap_chrom(for_others(tail), bit)]
-    owns = [products(outside_own, pieces, sections // 2, jnp.float32, "own") for pieces in (head, tail)]
-    if bit > 1:
+    for_own = lambda pieces, *got: products(outside_own, pieces, sections // 2, jnp.float32, "own", *got)
+    if n_chrom == 2:
+        owns = [for_own(head, gots[0]), for_own(tail)]
+    else:
+        owns = [for_own(head), for_own(tail)]
         side = (lax.axis_index("chrom") // bit) % 2
         places = [received(c, sections, near, side) for c in range(sections // 2)]
         gots = [jnp.stack([lax.dynamic_index_in_dim(got, p, 0, False) for p in places]) for got in gots]
@@ -229,15 +241,17 @@
             swap_chrom(lax.dynamic_slice_in_dim(s, (1 - side) * count, count, 0).astype(jnp.bfloat16), bit) for s in sums
         ]
         owns = [lax.dynamic_slice_in_dim(s, side * count, count, 0) for s in sums]
+    if n_chrom > 2:
+        owns[0] = owns[0] + gots[0]
 
     out = pl.pallas_call(
         functools.partial(finish_kernel, near if n_chrom == 2 else 0),
         out_shape=jax.ShapeDtypeStruct((per_device, rhs, rows), jnp.float32),
-        in_specs=[vmem] * 6,
+        in_specs=[vmem] * 5,
         out_specs=vmem,
         compiler_params=params,
         name="finish",
-    )(inverse, ridged, *owns, *gots)
+    )(inverse, ridged, *owns, gots[1])
     return jnp.transpose(out, (0, 2, 1))
 
 

time: 33.4 us -> 32.8 us (0.982)
  waiting for transfers between devices: 10.8 us -> 8.72 us
  starting transfers between devices: 13.9 us -> 15.4 us
    ppermute x7 -> x8, waiting for transfers between devices: 9.35 us -> 7.38 us  [swap(): lax.ppermute(x, 'samp', [(i, i ^ (odd if i % 2 else even)) for i in range...]
    ppermute x7 -> x8, starting transfers between devices: 10.7 us -> 12.2 us  [swap(): lax.ppermute(x, 'samp', [(i, i ^ (odd if i % 2 else even)) for i in range...]
  transfers between devices with their start and end apart: 9 -> 10, of which waited for: 6 -> 6; matrix products, arithmetic and copies ran while one was open for 0% -> 0% of each run, Pallas kernels for 12% -> 12%
where the time goes in v4:
time: 32.8 us; the launch traced here: 32.7 us
  starting transfers between devices  15.4 us (47%)
  waiting for transfers between devices  8.72 us (27%)
  Pallas kernels  7.68 us (23%)
  between operations  0.76 us (2%)
    ppermute x8, starting transfers between devices, swap(): lax.ppermute(x, 'samp', [(i, i ^ (odd if i % 2 else even)) for i in range...  12.2 us
    ppermute x8, waiting for transfers between devices, swap(): lax.ppermute(x, 'samp', [(i, i ^ (odd if i % 2 else even)) for i in range...  7.38 us
    pallas_call x4, Pallas kernels, products(): pl.pallas_call(functools.partial(section_kernel, near if got else 0), out...  3.31 us
    ppermute x2, starting transfers between devices, swap_chrom(): return lax.ppermute(x, 'chrom', [(i, i ^ bit) for i in range(n_chrom)])  3.13 us
    pallas_call x1, Pallas kernels, on_device(): pl.pallas_call(functools.partial(cross_kernel, blocks), out_shape=(jax.Sh...  2.79 us
    ppermute x2, waiting for transfers between devices, swap_chrom(): return lax.ppermute(x, 'chrom', [(i, i ^ bit) for i in range(n_chrom)])  1.34 us
    pallas_call x1, Pallas kernels, on_device(): pl.pallas_call(functools.partial(finish_kernel, near if n_chrom == 2 else...  0.82 us
    pallas_call x1, Pallas kernels, on_device(): pl.pallas_call(functools.partial(prepare_kernel, variants * n_chrom), out...  0.76 us
  transfers between devices with their start and end apart: 10, of which 6 were waited for; matrix products, arithmetic and copies ran while one was open for 0% of the time, Pallas kernels for 12%

profile of v4, /device:TPU:0, one launch (start us, length us, event | category | flops | bytes accessed | tf_op | source)
XLA Modules:
  0.0 32.7 jit_solution(2796519017471824493)
XLA Ops:
  0.0 0.0 copy-start
  0.0 0.0 copy-start.1
  0.0 2.8 %cross.1 = (bf16[384,3072]{1,0:T(8,128)(2,1)S(1)}, bf16[16,3072]{1,0:T(8,128)(2,1)S(1)}, bf16[16,3072]{1,0:T(8,128)(2,1)S(1)}, f32[16,3072]{1,0:T(8,128)S(1)}, f32[16,3072]{1,0:T(8,128)S(1)}) custom-call(s32[384,3072]{1,0:T(8,128)} %geno_hbm.1, f32[1,3072]{1,0:T(1,128)} %bitcast.5, f32[64,384]{1,0:T(8,128)} %bitcast.3), custom_call_target="tpu_custom_call" | custom-call | tf_op jit(solution)/shard_map/cross/pallas_call | solution.py:156
  2.8 0.5 %collective-permute-start.1 = (bf16[16,3072]{1,0:T(8,128)(2,1)S(1)}, bf16[16,3072]{1,0:T(8,128)(2,1)S(1)}, u32[]{:S(2)}, u32[]{:S(2)}) collective-permute-start(bf16[16,3072]{1,0:T(8,128)(2,1)S(1)} %get-tuple-element.22), channel_id=1, source_target_pairs={{0,1},{1,0},{2,3},{3,2},{4,5},{5,4},{6,7},{7,6},{8,9},{9,8},{10,11... | collective-permute-start | bytes 294920 | tf_op jit(solution)/shard_map/ppermute | solution.py:191
  3.3 0.1 collective-permute-start
  3.4 0.9 %collective-permute-done.1 = bf16[16,3072]{1,0:T(8,128)(2,1)S(1)} collective-permute-done((bf16[16,3072]{1,0:T(8,128)(2,1)S(1)}, bf16[16,3072]{1,0:T(8,128)(2,1)S(1)}, u32[]{:S(2)}, u32[]{:S(2)}) %collective-permute-start.1) | collective-permute-done | bytes 98336 | tf_op jit(solution)/shard_map/ppermute | solution.py:191
  4.3 2.9 %collective-permute-start.2 = (bf16[16,3072]{1,0:T(8,128)(2,1)S(1)}, bf16[16,3072]{1,0:T(8,128)(2,1)S(1)}, u32[]{:S(2)}, u32[]{:S(2)}) collective-permute-start(bf16[16,3072]{1,0:T(8,128)(2,1)S(1)} %add_convert_fusion.1), channel_id=1, source_target_pairs={{0,2},{1,5},{2,0},{3,7},{4,6},{5,1},{6,4},{7,3},{8,10},{9,13},{10,... | collective-permute-start | bytes 294920 | tf_op jit(solution)/shard_map/ppermute | solution.py:191
  7.9 0.0 copy-done
  7.9 0.0 copy-done.1
  7.9 0.8 %prepare.1 = (bf16[2,16,3072]{2,1,0:T(8,128)(2,1)S(1)}, bf16[4,16,3072]{2,1,0:T(8,128)(2,1)S(1)}, f32[4,16,384]{2,1,0:T(8,128)S(1)}, f32[64,384]{1,0:T(8,128)S(1)}) custom-call(s32[8]{0:T(128)S(1)} %copy-done.1, f32[1]{0:T(128)S(6)} %copy.6.ridge_ref, f32[64,384]{1,0:T(8,128)S(1)} %bitcast.4), custom_call_target="tpu_custom_call" | custom-call | tf_op jit(solution)/shard_map/prepare/pallas_call | solution.py:176
  8.7 0.0 collective-permute-done
  8.7 1.1 %collective-permute-done.2 = bf16[16,3072]{1,0:T(8,128)(2,1)S(1)} collective-permute-done((bf16[16,3072]{1,0:T(8,128)(2,1)S(1)}, bf16[16,3072]{1,0:T(8,128)(2,1)S(1)}, u32[]{:S(2)}, u32[]{:S(2)}) %collective-permute-start.2) | collective-permute-done | bytes 98336 | tf_op jit(solution)/shard_map/ppermute | solution.py:191
  9.9 2.1 %collective-permute-start.3 = (bf16[16,3072]{1,0:T(8,128)(2,1)S(1)}, bf16[16,3072]{1,0:T(8,128)(2,1)S(1)}, u32[]{:S(2)}, u32[]{:S(2)}) collective-permute-start(bf16[16,3072]{1,0:T(8,128)(2,1)S(1)} %convert_element_type.31), channel_id=1, source_target_pairs={{0,4},{1,3},{2,6},{3,1},{4,0},{5,7},{6,2},{7,5},{8,12},{9,11},{10,... | collective-permute-start | bytes 294920 | tf_op jit(solution)/shard_map/ppermute | solution.py:191
  12.0 2.6 %collective-permute-done.3 = bf16[16,3072]{1,0:T(8,128)(2,1)S(1)} collective-permute-done((bf16[16,3072]{1,0:T(8,128)(2,1)S(1)}, bf16[16,3072]{1,0:T(8,128)(2,1)S(1)}, u32[]{:S(2)}, u32[]{:S(2)}) %collective-permute-start.3) | collective-permute-done | bytes 98336 | tf_op jit(solution)/shard_map/ppermute | solution.py:191
  14.6 3.1 %collective-permute-start.4 = (bf16[16,3072]{1,0:T(8,128)(2,1)S(1)}, bf16[16,3072]{1,0:T(8,128)(2,1)S(1)}, u32[]{:S(2)}, u32[]{:S(2)}) collective-permute-start(bf16[16,3072]{1,0:T(8,128)(2,1)S(1)} %fusion), channel_id=1, source_target_pairs={{0,8},{1,9},{2,10},{3,11},{4,12},{5,13},{6,14},{7,15},{8,0},{9,1},... | collective-permute-start | bytes 294920 | tf_op jit(solution)/shard_map/ppermute | solution.py:191
  17.7 2.6 %collective-permute-done.4 = bf16[16,3072]{1,0:T(8,128)(2,1)S(1)} collective-permute-done((bf16[16,3072]{1,0:T(8,128)(2,1)S(1)}, bf16[16,3072]{1,0:T(8,128)(2,1)S(1)}, u32[]{:S(2)}, u32[]{:S(2)}) %collective-permute-start.4) | collective-permute-done | bytes 98336 | tf_op jit(solution)/shard_map/ppermute | solution.py:191
  20.4 0.1 collective-permute-start.5
  20.5 1.9 %collective-permute-start.7 = (bf16[16,3072]{1,0:T(8,128)(2,1)S(1)}, bf16[16,3072]{1,0:T(8,128)(2,1)S(1)}, u32[]{:S(2)}, u32[]{:S(2)}) collective-permute-start(bf16[16,3072]{1,0:T(8,128)(2,1)S(1)} %add_convert_fusion.refs_0_), channel_id=1, source_target_pairs={{0,2},{1,5},{2,0},{3,7},{4,6},{5,1},{6,4},{7,3},{8,10},{9,13},{10,... | collective-permute-start | bytes 294920 | tf_op jit(solution)/shard_map/ppermute | solution.py:191
  22.4 1.5 %collective-permute-start.8 = (bf16[16,3072]{1,0:T(8,128)(2,1)S(1)}, bf16[16,3072]{1,0:T(8,128)(2,1)S(1)}, u32[]{:S(2)}, u32[]{:S(2)}) collective-permute-start(bf16[16,3072]{1,0:T(8,128)(2,1)S(1)} %add_convert_fusion.refs_0_), channel_id=1, source_target_pairs={{0,3},{1,4},{2,1},{3,6},{4,7},{5,0},{6,5},{7,2},{8,11},{9,12},{10,... | collective-permute-start | bytes 294920 | tf_op jit(solution)/shard_map/ppermute | solution.py:191
  23.9 0.0 collective-permute-done.5.refs_1_
  23.9 0.8 %others.2 = bf16[3,32,384]{2,1,0:T(8,128)(2,1)S(1)} custom-call(bf16[2,16,3072]{2,1,0:T(8,128)(2,1)S(1)} %get-tuple-element.32.outside_ref, bf16[384,3072]{1,0:T(8,128)(2,1)S(1)} %get-tuple-element.30.stand_ref, bf16[16,3072]{1,0:T(8,128)(2,1)S(1)} %add_convert_fusion.refs_0_, bf16[16,3072]{1,0:T(8,128)(2,1)S(1)} %collective-permute-done.5.refs_1_), custom_call_target="tpu_custom_call" | custom-call | flops 301989888 | bytes 2359296 | tf_op jit(solution)/shard_map/others/pallas_call | solution.py:206
  24.7 1.6 %collective-permute-start.6 = (bf16[3,32,384]{2,1,0:T(8,128)(2,1)S(1)}, bf16[3,32,384]{2,1,0:T(8,128)(2,1)S(1)}, u32[]{:S(2)}, u32[]{:S(2)}) collective-permute-start(bf16[3,32,384]{2,1,0:T(8,128)(2,1)S(1)} %others.2), channel_id=1, source_target_pairs={{0,16},{16,0},{1,17},{17,1},{2,18},{18,2},{3,19},{19,3},{4,20},{20... | collective-permute-start | bytes 221192 | tf_op jit(solution)/shard_map/ppermute | solution.py:219
  26.3 0.0 collective-permute-done.7.refs_0_
  26.3 0.2 collective-permute-done.8.refs_1_
  26.4 0.8 %others.3 = bf16[3,32,384]{2,1,0:T(8,128)(2,1)S(1)} custom-call(bf16[2,16,3072]{2,1,0:T(8,128)(2,1)S(1)} %get-tuple-element.32.outside_ref, bf16[384,3072]{1,0:T(8,128)(2,1)S(1)} %get-tuple-element.30.stand_ref, bf16[16,3072]{1,0:T(8,128)(2,1)S(1)} %collective-permute-done.7.refs_0_, bf16[16,3072]{1,0:T(8,128)(2,1)S(1)} %collective-permute-done.8.refs_1_), custom_call_target="tpu_custom_call" | custom-call | flops 301989888 | bytes 2359296 | tf_op jit(solution)/shard_map/others/pallas_call | solution.py:206
  27.3 1.6 %collective-permute-start.9 = (bf16[3,32,384]{2,1,0:T(8,128)(2,1)S(1)}, bf16[3,32,384]{2,1,0:T(8,128)(2,1)S(1)}, u32[]{:S(2)}, u32[]{:S(2)}) collective-permute-start(bf16[3,32,384]{2,1,0:T(8,128)(2,1)S(1)} %others.3), channel_id=1, source_target_pairs={{0,16},{16,0},{1,17},{17,1},{2,18},{18,2},{3,19},{19,3},{4,20},{20... | collective-permute-start | bytes 221192 | tf_op jit(solution)/shard_map/ppermute | solution.py:219
  28.8 0.8 %own.3.refs_1_ = f32[4,32,384]{2,1,0:T(8,128)S(1)} custom-call(bf16[4,16,3072]{2,1,0:T(8,128)(2,1)S(1)} %get-tuple-element.29.outside_ref, bf16[384,3072]{1,0:T(8,128)(2,1)S(1)} %get-tuple-element.30.stand_ref, bf16[16,3072]{1,0:T(8,128)(2,1)S(1)} %collective-permute-done.7.refs_0_, bf16[16,3072]{1,0:T(8,128)(2,1)S(1)} %collective-permute-done.8.refs_1_), custom_call_target="tpu_custom_call" | custom-call | flops 301989888 | bytes 2359296 | tf_op jit(solution)/shard_map/own/pallas_call | solution.py:206
  29.7 0.0 collective-permute-done.6.refs_2_
  29.7 0.8 %own.2.refs_0_ = f32[4,32,384]{2,1,0:T(8,128)S(1)} custom-call(bf16[4,16,3072]{2,1,0:T(8,128)(2,1)S(1)} %get-tuple-element.29.outside_ref, bf16[384,3072]{1,0:T(8,128)(2,1)S(1)} %get-tuple-element.30.stand_ref, bf16[16,3072]{1,0:T(8,128)(2,1)S(1)} %add_convert_fusion.refs_0_, bf16[16,3072]{1,0:T(8,128)(2,1)S(1)} %collective-permute-done.5.refs_1_, ...), custom_call_target="tpu_custom_call" | custom-call | flops 301989888 | bytes 2359296 | tf_op jit(solution)/shard_map/own/pallas_call | solution.py:206
  30.5 1.3 %collective-permute-done.9.refs_2_ = bf16[3,32,384]{2,1,0:T(8,128)(2,1)S(1)} collective-permute-done((bf16[3,32,384]{2,1,0:T(8,128)(2,1)S(1)}, bf16[3,32,384]{2,1,0:T(8,128)(2,1)S(1)}, u32[]{:S(2)}, u32[]{:S(2)}) %collective-permute-start.9) | collective-permute-done | bytes 73760 | tf_op jit(solution)/shard_map/ppermute | solution.py:219
  31.8 0.8 %finish.1 = f32[4,64,384]{2,1,0:T(8,128)} custom-call(f32[4,16,384]{2,1,0:T(8,128)S(1)} %get-tuple-element.27.inverse_ref, f32[64,384]{1,0:T(8,128)S(1)} %get-tuple-element.28.ridged_ref, f32[4,32,384]{2,1,0:T(8,128)S(1)} %own.2.refs_0_, f32[4,32,384]{2,1,0:T(8,128)S(1)} %own.3.refs_1_, bf16[3,32,384]{2,1,0:T(8,128)(2,1)S(1)} %collective-permute-done.9.refs_2_), custom_call_target="tpu_custom_call" | custom-call | tf_op jit(solution)/shard_map/finish/pallas_call | solution.py:247
  (5 shorter events, 0.1 us)
Async XLA Ops:
  0.0 7.9 %copy-start = (f32[384,64]{0,1:T(8,128)S(1)}, f32[384,64]{0,1:T(8,128)}, u32[]{:S(2)}) copy-start(f32[384,64]{0,1:T(8,128)} %param.9) | copy-start | bytes 294916
  0.0 7.9 %copy-start.1 = (s32[8]{0:T(128)S(1)}, s32[8]{0:T(128)}, u32[]{:S(2)}) copy-start(s32[8]{0:T(128)} %widths_ref.1) | copy-start | bytes 100
  2.8 1.5 %collective-permute-start.1 = (bf16[16,3072]{1,0:T(8,128)(2,1)S(1)}, bf16[16,3072]{1,0:T(8,128)(2,1)S(1)}, u32[]{:S(2)}, u32[]{:S(2)}) collective-permute-start(bf16[16,3072]{1,0:T(8,128)(2,1)S(1)} %get-tuple-element.22), channel_id=1, source_target_pairs={{0,1},{1,0},{2,3},{3,2},{4,5},{5,4},{6,7},{7,6},{8,9},{9,8},{10,11... | collective-permute-start | bytes 294920 | tf_op jit(solution)/shard_map/ppermute | solution.py:191
  3.3 5.3 %collective-permute-start = (bf16[16,3072]{1,0:T(8,128)(2,1)S(1)}, bf16[16,3072]{1,0:T(8,128)(2,1)S(1)}, u32[]{:S(2)}, u32[]{:S(2)}) collective-permute-start(bf16[16,3072]{1,0:T(8,128)(2,1)S(1)} %get-tuple-element.20), channel_id=1, source_target_pairs={{0,1},{1,0},{2,3},{3,2},{4,5},{5,4},{6,7},{7,6},{8,9},{9,8},{10,11... | collective-permute-start | bytes 294920 | tf_op jit(solution)/shard_map/ppermute | solution.py:191
  4.3 5.5 %collective-permute-start.2 = (bf16[16,3072]{1,0:T(8,128)(2,1)S(1)}, bf16[16,3072]{1,0:T(8,128)(2,1)S(1)}, u32[]{:S(2)}, u32[]{:S(2)}) collective-permute-start(bf16[16,3072]{1,0:T(8,128)(2,1)S(1)} %add_convert_fusion.1), channel_id=1, source_target_pairs={{0,2},{1,5},{2,0},{3,7},{4,6},{5,1},{6,4},{7,3},{8,10},{9,13},{10,... | collective-permute-start | bytes 294920 | tf_op jit(solution)/shard_map/ppermute | solution.py:191
  9.9 4.7 %collective-permute-start.3 = (bf16[16,3072]{1,0:T(8,128)(2,1)S(1)}, bf16[16,3072]{1,0:T(8,128)(2,1)S(1)}, u32[]{:S(2)}, u32[]{:S(2)}) collective-permute-start(bf16[16,3072]{1,0:T(8,128)(2,1)S(1)} %convert_element_type.31), channel_id=1, source_target_pairs={{0,4},{1,3},{2,6},{3,1},{4,0},{5,7},{6,2},{7,5},{8,12},{9,11},{10,... | collective-permute-start | bytes 294920 | tf_op jit(solution)/shard_map/ppermute | solution.py:191
  14.6 5.7 %collective-permute-start.4 = (bf16[16,3072]{1,0:T(8,128)(2,1)S(1)}, bf16[16,3072]{1,0:T(8,128)(2,1)S(1)}, u32[]{:S(2)}, u32[]{:S(2)}) collective-permute-start(bf16[16,3072]{1,0:T(8,128)(2,1)S(1)} %fusion), channel_id=1, source_target_pairs={{0,8},{1,9},{2,10},{3,11},{4,12},{5,13},{6,14},{7,15},{8,0},{9,1},... | collective-permute-start | bytes 294920 | tf_op jit(solution)/shard_map/ppermute | solution.py:191
  20.4 3.5 %collective-permute-start.5 = (bf16[16,3072]{1,0:T(8,128)(2,1)S(1)}, bf16[16,3072]{1,0:T(8,128)(2,1)S(1)}, u32[]{:S(2)}, u32[]{:S(2)}) collective-permute-start(bf16[16,3072]{1,0:T(8,128)(2,1)S(1)} %add_convert_fusion.refs_0_), channel_id=1, source_target_pairs={{0,1},{1,0},{2,3},{3,2},{4,5},{5,4},{6,7},{7,6},{8,9},{9,8},{10,11... | collective-permute-start | bytes 294920 | tf_op jit(solution)/shard_map/ppermute | solution.py:191
  20.5 5.8 %collective-permute-start.7 = (bf16[16,3072]{1,0:T(8,128)(2,1)S(1)}, bf16[16,3072]{1,0:T(8,128)(2,1)S(1)}, u32[]{:S(2)}, u32[]{:S(2)}) collective-permute-start(bf16[16,3072]{1,0:T(8,128)(2,1)S(1)} %add_convert_fusion.refs_0_), channel_id=1, source_target_pairs={{0,2},{1,5},{2,0},{3,7},{4,6},{5,1},{6,4},{7,3},{8,10},{9,13},{10,... | collective-permute-start | bytes 294920 | tf_op jit(solution)/shard_map/ppermute | solution.py:191
  22.4 4.0 %collective-permute-start.8 = (bf16[16,3072]{1,0:T(8,128)(2,1)S(1)}, bf16[16,3072]{1,0:T(8,128)(2,1)S(1)}, u32[]{:S(2)}, u32[]{:S(2)}) collective-permute-start(bf16[16,3072]{1,0:T(8,128)(2,1)S(1)} %add_convert_fusion.refs_0_), channel_id=1, source_target_pairs={{0,3},{1,4},{2,1},{3,6},{4,7},{5,0},{6,5},{7,2},{8,11},{9,12},{10,... | collective-permute-start | bytes 294920 | tf_op jit(solution)/shard_map/ppermute | solution.py:191
  24.7 5.0 %collective-permute-start.6 = (bf16[3,32,384]{2,1,0:T(8,128)(2,1)S(1)}, bf16[3,32,384]{2,1,0:T(8,128)(2,1)S(1)}, u32[]{:S(2)}, u32[]{:S(2)}) collective-permute-start(bf16[3,32,384]{2,1,0:T(8,128)(2,1)S(1)} %others.2), channel_id=1, source_target_pairs={{0,16},{16,0},{1,17},{17,1},{2,18},{18,2},{3,19},{19,3},{4,20},{20... | collective-permute-start | bytes 221192 | tf_op jit(solution)/shard_map/ppermute | solution.py:219
  27.3 4.6 %collective-permute-start.9 = (bf16[3,32,384]{2,1,0:T(8,128)(2,1)S(1)}, bf16[3,32,384]{2,1,0:T(8,128)(2,1)S(1)}, u32[]{:S(2)}, u32[]{:S(2)}) collective-permute-start(bf16[3,32,384]{2,1,0:T(8,128)(2,1)S(1)} %others.3), channel_id=1, source_target_pairs={{0,16},{16,0},{1,17},{17,1},{2,18},{18,2},{3,19},{19,3},{4,20},{20... | collective-permute-start | bytes 221192 | tf_op jit(solution)/shard_map/ppermute | solution.py:219

commit v5 on v4

--- a/solution.py
+++ b/solution.py
@@ -11,20 +11,24 @@
 BLOCK = 512
 
 
-def core_and_bits():
+def half_and_bits():
     samp = lax.axis_index("samp")
-    core, y, z = samp % 2, (samp // 2) % 2, (samp // 4) % 2
-    return core, jnp.where(core == 0, y, z), jnp.where(core == 0, z, y)
+    half, bit = samp % 2, 2
+    while bit < lax.axis_size("samp"):
+        half, bit = half + (samp // bit) % 2, bit * 2
+    half = half % 2
+    y, z = (samp // 2) % 2, (samp // 4) % 2
+    return half, jnp.where(half == 0, y, z), jnp.where(half == 0, z, y)
 
 
 def piece_rows(rhs):
-    core, mine, sibling = core_and_bits()
+    which, mine, sibling = half_and_bits()
     half, quarter = rhs // 2, rhs // 4
     return [
-        core * half + mine * quarter,
-        (1 - core) * half + sibling * quarter,
-        core * half + (1 - mine) * quarter,
-        (1 - core) * half + (1 - sibling) * quarter,
+        which * half + mine * quarter,
+        (1 - which) * half + sibling * quarter,
+        which * half + (1 - mine) * quarter,
+        (1 - which) * half + (1 - sibling) * quarter,
     ]
 
 
@@ -187,20 +191,20 @@
         name="prepare",
     )(widths, ridge_term, dir_t)
 
-    def swap(x, even, odd):
-        return lax.ppermute(x, "samp", [(i, i ^ (odd if i % 2 else even)) for i in range(n_samp)])
+    def swap(x, low, high):
+        return lax.ppermute(x, "samp", [(i, i ^ (high if i.bit_count() % 2 else low)) for i in range(n_samp)])
 
     sent = (keep_first + swap(give_first, 1, 1)).astype(jnp.bfloat16)
-    mine_sum = keep_second + swap(give_second, 1, 1) + swap(sent, 2, 4)
+    mine_sum = keep_second + swap(give_second, 1, 1) + swap(sent, 3, 5)
     mine_sum, outside_others, outside_own, inverse, ridged = lax.optimization_barrier(
         (mine_sum, outside_others, outside_own, inverse, ridged)
     )
     rest = [1 << b for b in range(3, n_samp.bit_length() - 1)]
-    even_bits, odd_bits = [4] + rest, [2] + rest
-    for even, odd in zip(even_bits, odd_bits):
-        mine_sum = mine_sum + swap(mine_sum.astype(jnp.bfloat16), even, odd)
+    low_bits, high_bits = rest + [4], [2] + rest
+    for low, high in zip(low_bits, high_bits):
+        mine_sum = mine_sum + swap(mine_sum.astype(jnp.bfloat16), low | 1, high | 1)
     first = mine_sum.astype(jnp.bfloat16)
-    second, second_sibling = swap(first, 2, 4), swap(first, 3, 5)
+    second, second_sibling = swap(first, 3, 5), swap(first, 2, 4)
 
     def products(outside, pieces, count, dtype, name, *got):
         return pl.pallas_call(

time: 32.8 us -> 32.3 us (0.985)
  starting transfers between devices: 15.4 us -> 14.6 us
    ppermute x8, starting transfers between devices: 12.2 us -> 11.5 us  [swap(): lax.ppermute(x, 'samp', [(i, i ^ (high if i.bit_count() % 2 else low)) fo...]
    ppermute x8, waiting for transfers between devices: 7.38 us -> 7.77 us  [swap(): lax.ppermute(x, 'samp', [(i, i ^ (high if i.bit_count() % 2 else low)) fo...]
  transfers between devices with their start and end apart: 10 -> 10, of which waited for: 6 -> 6; matrix products, arithmetic and copies ran while one was open for 0% -> 0% of each run, Pallas kernels for 12% -> 13%
where the time goes in v5:
time: 32.3 us; the launch traced here: 32.2 us
  starting transfers between devices  14.6 us (45%)
  waiting for transfers between devices  8.95 us (28%)
  Pallas kernels  7.69 us (24%)
  between operations  0.75 us (2%)
    ppermute x8, starting transfers between devices, swap(): lax.ppermute(x, 'samp', [(i, i ^ (high if i.bit_count() % 2 else low)) fo...  11.5 us
    ppermute x8, waiting for transfers between devices, swap(): lax.ppermute(x, 'samp', [(i, i ^ (high if i.bit_count() % 2 else low)) fo...  7.77 us
    pallas_call x4, Pallas kernels, products(): pl.pallas_call(functools.partial(section_kernel, near if got else 0), out...  3.31 us
    ppermute x2, starting transfers between devices, swap_chrom(): return lax.ppermute(x, 'chrom', [(i, i ^ bit) for i in range(n_chrom)])  3.11 us
    pallas_call x1, Pallas kernels, on_device(): pl.pallas_call(functools.partial(cross_kernel, blocks), out_shape=(jax.Sh...  2.79 us
    ppermute x2, waiting for transfers between devices, swap_chrom(): return lax.ppermute(x, 'chrom', [(i, i ^ bit) for i in range(n_chrom)])  1.18 us
    pallas_call x1, Pallas kernels, on_device(): pl.pallas_call(functools.partial(finish_kernel, near if n_chrom == 2 else...  0.82 us
    pallas_call x1, Pallas kernels, on_device(): pl.pallas_call(functools.partial(prepare_kernel, variants * n_chrom), out...  0.77 us
  transfers between devices with their start and end apart: 10, of which 6 were waited for; matrix products, arithmetic and copies ran while one was open for 0% of the time, Pallas kernels for 13%

profile of v5, /device:TPU:0, one launch (start us, length us, event | category | flops | bytes accessed | tf_op | source)
XLA Modules:
  0.0 32.2 jit_solution(5328941457651675113)
XLA Ops:
  0.0 0.0 copy-start
  0.0 0.0 copy-start.1
  0.0 2.8 %cross.1 = (bf16[384,3072]{1,0:T(8,128)(2,1)S(1)}, bf16[16,3072]{1,0:T(8,128)(2,1)S(1)}, bf16[16,3072]{1,0:T(8,128)(2,1)S(1)}, f32[16,3072]{1,0:T(8,128)S(1)}, f32[16,3072]{1,0:T(8,128)S(1)}) custom-call(s32[384,3072]{1,0:T(8,128)} %geno_hbm.1, f32[1,3072]{1,0:T(1,128)} %bitcast.5, f32[64,384]{1,0:T(8,128)} %bitcast.3), custom_call_target="tpu_custom_call" | custom-call | tf_op jit(solution)/shard_map/cross/pallas_call | solution.py:160
  2.8 0.5 %collective-permute-start.1 = (bf16[16,3072]{1,0:T(8,128)(2,1)S(1)}, bf16[16,3072]{1,0:T(8,128)(2,1)S(1)}, u32[]{:S(2)}, u32[]{:S(2)}) collective-permute-start(bf16[16,3072]{1,0:T(8,128)(2,1)S(1)} %get-tuple-element.22), channel_id=1, source_target_pairs={{0,1},{1,0},{2,3},{3,2},{4,5},{5,4},{6,7},{7,6},{8,9},{9,8},{10,11... | collective-permute-start | bytes 294920 | tf_op jit(solution)/shard_map/ppermute | solution.py:195
  3.3 0.1 collective-permute-start
  3.4 0.9 %collective-permute-done.1 = bf16[16,3072]{1,0:T(8,128)(2,1)S(1)} collective-permute-done((bf16[16,3072]{1,0:T(8,128)(2,1)S(1)}, bf16[16,3072]{1,0:T(8,128)(2,1)S(1)}, u32[]{:S(2)}, u32[]{:S(2)}) %collective-permute-start.1) | collective-permute-done | bytes 98336 | tf_op jit(solution)/shard_map/ppermute | solution.py:195
  4.3 2.7 %collective-permute-start.2 = (bf16[16,3072]{1,0:T(8,128)(2,1)S(1)}, bf16[16,3072]{1,0:T(8,128)(2,1)S(1)}, u32[]{:S(2)}, u32[]{:S(2)}) collective-permute-start(bf16[16,3072]{1,0:T(8,128)(2,1)S(1)} %add_convert_fusion.1), channel_id=1, source_target_pairs={{0,3},{1,4},{2,7},{3,0},{4,1},{5,6},{6,5},{7,2},{8,13},{9,10},{10,... | collective-permute-start | bytes 294920 | tf_op jit(solution)/shard_map/ppermute | solution.py:195
  7.6 0.0 copy-done
  7.6 0.0 copy-done.1
  7.7 0.8 %prepare.1 = (bf16[2,16,3072]{2,1,0:T(8,128)(2,1)S(1)}, bf16[4,16,3072]{2,1,0:T(8,128)(2,1)S(1)}, f32[4,16,384]{2,1,0:T(8,128)S(1)}, f32[64,384]{1,0:T(8,128)S(1)}) custom-call(s32[8]{0:T(128)S(1)} %copy-done.1, f32[1]{0:T(128)S(6)} %copy.6.ridge_ref, f32[64,384]{1,0:T(8,128)S(1)} %bitcast.4), custom_call_target="tpu_custom_call" | custom-call | tf_op jit(solution)/shard_map/prepare/pallas_call | solution.py:180
  8.4 0.0 collective-permute-done
  8.4 0.8 %collective-permute-done.2 = bf16[16,3072]{1,0:T(8,128)(2,1)S(1)} collective-permute-done((bf16[16,3072]{1,0:T(8,128)(2,1)S(1)}, bf16[16,3072]{1,0:T(8,128)(2,1)S(1)}, u32[]{:S(2)}, u32[]{:S(2)}) %collective-permute-start.2) | collective-permute-done | bytes 98336 | tf_op jit(solution)/shard_map/ppermute | solution.py:195
  9.3 2.9 %collective-permute-start.3 = (bf16[16,3072]{1,0:T(8,128)(2,1)S(1)}, bf16[16,3072]{1,0:T(8,128)(2,1)S(1)}, u32[]{:S(2)}, u32[]{:S(2)}) collective-permute-start(bf16[16,3072]{1,0:T(8,128)(2,1)S(1)} %convert_element_type.31), channel_id=1, source_target_pairs={{0,9},{1,2},{2,1},{3,10},{4,7},{5,12},{6,15},{7,4},{8,11},{9,0},{1... | collective-permute-start | bytes 294920 | tf_op jit(solution)/shard_map/ppermute | solution.py:195
  12.2 2.3 %collective-permute-done.3 = bf16[16,3072]{1,0:T(8,128)(2,1)S(1)} collective-permute-done((bf16[16,3072]{1,0:T(8,128)(2,1)S(1)}, bf16[16,3072]{1,0:T(8,128)(2,1)S(1)}, u32[]{:S(2)}, u32[]{:S(2)}) %collective-permute-start.3) | collective-permute-done | bytes 98336 | tf_op jit(solution)/shard_map/ppermute | solution.py:195
  14.5 1.9 %collective-permute-start.4 = (bf16[16,3072]{1,0:T(8,128)(2,1)S(1)}, bf16[16,3072]{1,0:T(8,128)(2,1)S(1)}, u32[]{:S(2)}, u32[]{:S(2)}) collective-permute-start(bf16[16,3072]{1,0:T(8,128)(2,1)S(1)} %fusion), channel_id=1, source_target_pairs={{0,5},{1,8},{2,11},{3,6},{4,13},{5,0},{6,3},{7,14},{8,1},{9,12},{1... | collective-permute-start | bytes 294920 | tf_op jit(solution)/shard_map/ppermute | solution.py:195
  16.5 3.0 %collective-permute-done.4 = bf16[16,3072]{1,0:T(8,128)(2,1)S(1)} collective-permute-done((bf16[16,3072]{1,0:T(8,128)(2,1)S(1)}, bf16[16,3072]{1,0:T(8,128)(2,1)S(1)}, u32[]{:S(2)}, u32[]{:S(2)}) %collective-permute-start.4) | collective-permute-done | bytes 98336 | tf_op jit(solution)/shard_map/ppermute | solution.py:195
  19.5 0.9 %collective-permute-start.5 = (bf16[16,3072]{1,0:T(8,128)(2,1)S(1)}, bf16[16,3072]{1,0:T(8,128)(2,1)S(1)}, u32[]{:S(2)}, u32[]{:S(2)}) collective-permute-start(bf16[16,3072]{1,0:T(8,128)(2,1)S(1)} %add_convert_fusion.refs_0_), channel_id=1, source_target_pairs={{0,1},{1,0},{2,3},{3,2},{4,5},{5,4},{6,7},{7,6},{8,9},{9,8},{10,11... | collective-permute-start | bytes 294920 | tf_op jit(solution)/shard_map/ppermute | solution.py:195
  20.4 1.1 %collective-permute-start.7 = (bf16[16,3072]{1,0:T(8,128)(2,1)S(1)}, bf16[16,3072]{1,0:T(8,128)(2,1)S(1)}, u32[]{:S(2)}, u32[]{:S(2)}) collective-permute-start(bf16[16,3072]{1,0:T(8,128)(2,1)S(1)} %add_convert_fusion.refs_0_), channel_id=1, source_target_pairs={{0,3},{1,4},{2,7},{3,0},{4,1},{5,6},{6,5},{7,2},{8,13},{9,10},{10,... | collective-permute-start | bytes 294920 | tf_op jit(solution)/shard_map/ppermute | solution.py:195
  21.5 1.5 %collective-permute-start.8 = (bf16[16,3072]{1,0:T(8,128)(2,1)S(1)}, bf16[16,3072]{1,0:T(8,128)(2,1)S(1)}, u32[]{:S(2)}, u32[]{:S(2)}) collective-permute-start(bf16[16,3072]{1,0:T(8,128)(2,1)S(1)} %add_convert_fusion.refs_0_), channel_id=1, source_target_pairs={{0,2},{1,5},{2,6},{3,1},{4,0},{5,7},{6,4},{7,3},{8,12},{9,11},{10,... | collective-permute-start | bytes 294920 | tf_op jit(solution)/shard_map/ppermute | solution.py:195
  22.9 0.0 collective-permute-done.5.refs_1_
  22.9 0.8 %others.2 = bf16[3,32,384]{2,1,0:T(8,128)(2,1)S(1)} custom-call(bf16[2,16,3072]{2,1,0:T(8,128)(2,1)S(1)} %get-tuple-element.32.outside_ref, bf16[384,3072]{1,0:T(8,128)(2,1)S(1)} %get-tuple-element.30.stand_ref, bf16[16,3072]{1,0:T(8,128)(2,1)S(1)} %add_convert_fusion.refs_0_, bf16[16,3072]{1,0:T(8,128)(2,1)S(1)} %collective-permute-done.5.refs_1_), custom_call_target="tpu_custom_call" | custom-call | flops 301989888 | bytes 2359296 | tf_op jit(solution)/shard_map/others/pallas_call | solution.py:210
  23.8 1.6 %collective-permute-start.6 = (bf16[3,32,384]{2,1,0:T(8,128)(2,1)S(1)}, bf16[3,32,384]{2,1,0:T(8,128)(2,1)S(1)}, u32[]{:S(2)}, u32[]{:S(2)}) collective-permute-start(bf16[3,32,384]{2,1,0:T(8,128)(2,1)S(1)} %others.2), channel_id=1, source_target_pairs={{0,16},{16,0},{1,17},{17,1},{2,18},{18,2},{3,19},{19,3},{4,20},{20... | collective-permute-start | bytes 221192 | tf_op jit(solution)/shard_map/ppermute | solution.py:223
  25.3 0.0 collective-permute-done.7.refs_0_
  25.3 0.8 %collective-permute-done.8.refs_1_ = bf16[16,3072]{1,0:T(8,128)(2,1)S(1)} collective-permute-done((bf16[16,3072]{1,0:T(8,128)(2,1)S(1)}, bf16[16,3072]{1,0:T(8,128)(2,1)S(1)}, u32[]{:S(2)}, u32[]{:S(2)}) %collective-permute-start.8) | collective-permute-done | bytes 98336 | tf_op jit(solution)/shard_map/ppermute | solution.py:195
  26.1 0.8 %others.3 = bf16[3,32,384]{2,1,0:T(8,128)(2,1)S(1)} custom-call(bf16[2,16,3072]{2,1,0:T(8,128)(2,1)S(1)} %get-tuple-element.32.outside_ref, bf16[384,3072]{1,0:T(8,128)(2,1)S(1)} %get-tuple-element.30.stand_ref, bf16[16,3072]{1,0:T(8,128)(2,1)S(1)} %collective-permute-done.7.refs_0_, bf16[16,3072]{1,0:T(8,128)(2,1)S(1)} %collective-permute-done.8.refs_1_), custom_call_target="tpu_custom_call" | custom-call | flops 301989888 | bytes 2359296 | tf_op jit(solution)/shard_map/others/pallas_call | solution.py:210
  26.9 1.6 %collective-permute-start.9 = (bf16[3,32,384]{2,1,0:T(8,128)(2,1)S(1)}, bf16[3,32,384]{2,1,0:T(8,128)(2,1)S(1)}, u32[]{:S(2)}, u32[]{:S(2)}) collective-permute-start(bf16[3,32,384]{2,1,0:T(8,128)(2,1)S(1)} %others.3), channel_id=1, source_target_pairs={{0,16},{16,0},{1,17},{17,1},{2,18},{18,2},{3,19},{19,3},{4,20},{20... | collective-permute-start | bytes 221192 | tf_op jit(solution)/shard_map/ppermute | solution.py:223
  28.5 0.8 %own.3.refs_1_ = f32[4,32,384]{2,1,0:T(8,128)S(1)} custom-call(bf16[4,16,3072]{2,1,0:T(8,128)(2,1)S(1)} %get-tuple-element.29.outside_ref, bf16[384,3072]{1,0:T(8,128)(2,1)S(1)} %get-tuple-element.30.stand_ref, bf16[16,3072]{1,0:T(8,128)(2,1)S(1)} %collective-permute-done.7.refs_0_, bf16[16,3072]{1,0:T(8,128)(2,1)S(1)} %collective-permute-done.8.refs_1_), custom_call_target="tpu_custom_call" | custom-call | flops 301989888 | bytes 2359296 | tf_op jit(solution)/shard_map/own/pallas_call | solution.py:210
  29.3 0.0 collective-permute-done.6.refs_2_
  29.3 0.8 %own.2.refs_0_ = f32[4,32,384]{2,1,0:T(8,128)S(1)} custom-call(bf16[4,16,3072]{2,1,0:T(8,128)(2,1)S(1)} %get-tuple-element.29.outside_ref, bf16[384,3072]{1,0:T(8,128)(2,1)S(1)} %get-tuple-element.30.stand_ref, bf16[16,3072]{1,0:T(8,128)(2,1)S(1)} %add_convert_fusion.refs_0_, bf16[16,3072]{1,0:T(8,128)(2,1)S(1)} %collective-permute-done.5.refs_1_, ...), custom_call_target="tpu_custom_call" | custom-call | flops 301989888 | bytes 2359296 | tf_op jit(solution)/shard_map/own/pallas_call | solution.py:210
  30.2 1.2 %collective-permute-done.9.refs_2_ = bf16[3,32,384]{2,1,0:T(8,128)(2,1)S(1)} collective-permute-done((bf16[3,32,384]{2,1,0:T(8,128)(2,1)S(1)}, bf16[3,32,384]{2,1,0:T(8,128)(2,1)S(1)}, u32[]{:S(2)}, u32[]{:S(2)}) %collective-permute-start.9) | collective-permute-done | bytes 73760 | tf_op jit(solution)/shard_map/ppermute | solution.py:223
  31.3 0.8 %finish.1 = f32[4,64,384]{2,1,0:T(8,128)} custom-call(f32[4,16,384]{2,1,0:T(8,128)S(1)} %get-tuple-element.27.inverse_ref, f32[64,384]{1,0:T(8,128)S(1)} %get-tuple-element.28.ridged_ref, f32[4,32,384]{2,1,0:T(8,128)S(1)} %own.2.refs_0_, f32[4,32,384]{2,1,0:T(8,128)S(1)} %own.3.refs_1_, bf16[3,32,384]{2,1,0:T(8,128)(2,1)S(1)} %collective-permute-done.9.refs_2_), custom_call_target="tpu_custom_call" | custom-call | tf_op jit(solution)/shard_map/finish/pallas_call | solution.py:251
  (5 shorter events, 0.1 us)
Async XLA Ops:
  0.0 7.6 %copy-start = (f32[384,64]{0,1:T(8,128)S(1)}, f32[384,64]{0,1:T(8,128)}, u32[]{:S(2)}) copy-start(f32[384,64]{0,1:T(8,128)} %param.9) | copy-start | bytes 294916
  0.0 7.6 %copy-start.1 = (s32[8]{0:T(128)S(1)}, s32[8]{0:T(128)}, u32[]{:S(2)}) copy-start(s32[8]{0:T(128)} %widths_ref.1) | copy-start | bytes 100
  2.8 1.5 %collective-permute-start.1 = (bf16[16,3072]{1,0:T(8,128)(2,1)S(1)}, bf16[16,3072]{1,0:T(8,128)(2,1)S(1)}, u32[]{:S(2)}, u32[]{:S(2)}) collective-permute-start(bf16[16,3072]{1,0:T(8,128)(2,1)S(1)} %get-tuple-element.22), channel_id=1, source_target_pairs={{0,1},{1,0},{2,3},{3,2},{4,5},{5,4},{6,7},{7,6},{8,9},{9,8},{10,11... | collective-permute-start | bytes 294920 | tf_op jit(solution)/shard_map/ppermute | solution.py:195
  3.3 5.1 %collective-permute-start = (bf16[16,3072]{1,0:T(8,128)(2,1)S(1)}, bf16[16,3072]{1,0:T(8,128)(2,1)S(1)}, u32[]{:S(2)}, u32[]{:S(2)}) collective-permute-start(bf16[16,3072]{1,0:T(8,128)(2,1)S(1)} %get-tuple-element.20), channel_id=1, source_target_pairs={{0,1},{1,0},{2,3},{3,2},{4,5},{5,4},{6,7},{7,6},{8,9},{9,8},{10,11... | collective-permute-start | bytes 294920 | tf_op jit(solution)/shard_map/ppermute | solution.py:195
  4.3 5.0 %collective-permute-start.2 = (bf16[16,3072]{1,0:T(8,128)(2,1)S(1)}, bf16[16,3072]{1,0:T(8,128)(2,1)S(1)}, u32[]{:S(2)}, u32[]{:S(2)}) collective-permute-start(bf16[16,3072]{1,0:T(8,128)(2,1)S(1)} %add_convert_fusion.1), channel_id=1, source_target_pairs={{0,3},{1,4},{2,7},{3,0},{4,1},{5,6},{6,5},{7,2},{8,13},{9,10},{10,... | collective-permute-start | bytes 294920 | tf_op jit(solution)/shard_map/ppermute | solution.py:195
  9.3 5.2 %collective-permute-start.3 = (bf16[16,3072]{1,0:T(8,128)(2,1)S(1)}, bf16[16,3072]{1,0:T(8,128)(2,1)S(1)}, u32[]{:S(2)}, u32[]{:S(2)}) collective-permute-start(bf16[16,3072]{1,0:T(8,128)(2,1)S(1)} %convert_element_type.31), channel_id=1, source_target_pairs={{0,9},{1,2},{2,1},{3,10},{4,7},{5,12},{6,15},{7,4},{8,11},{9,0},{1... | collective-permute-start | bytes 294920 | tf_op jit(solution)/shard_map/ppermute | solution.py:195
  14.5 4.9 %collective-permute-start.4 = (bf16[16,3072]{1,0:T(8,128)(2,1)S(1)}, bf16[16,3072]{1,0:T(8,128)(2,1)S(1)}, u32[]{:S(2)}, u32[]{:S(2)}) collective-permute-start(bf16[16,3072]{1,0:T(8,128)(2,1)S(1)} %fusion), channel_id=1, source_target_pairs={{0,5},{1,8},{2,11},{3,6},{4,13},{5,0},{6,3},{7,14},{8,1},{9,12},{1... | collective-permute-start | bytes 294920 | tf_op jit(solution)/shard_map/ppermute | solution.py:195
  19.5 3.4 %collective-permute-start.5 = (bf16[16,3072]{1,0:T(8,128)(2,1)S(1)}, bf16[16,3072]{1,0:T(8,128)(2,1)S(1)}, u32[]{:S(2)}, u32[]{:S(2)}) collective-permute-start(bf16[16,3072]{1,0:T(8,128)(2,1)S(1)} %add_convert_fusion.refs_0_), channel_id=1, source_target_pairs={{0,1},{1,0},{2,3},{3,2},{4,5},{5,4},{6,7},{7,6},{8,9},{9,8},{10,11... | collective-permute-start | bytes 294920 | tf_op jit(solution)/shard_map/ppermute | solution.py:195
  20.4 5.0 %collective-permute-start.7 = (bf16[16,3072]{1,0:T(8,128)(2,1)S(1)}, bf16[16,3072]{1,0:T(8,128)(2,1)S(1)}, u32[]{:S(2)}, u32[]{:S(2)}) collective-permute-start(bf16[16,3072]{1,0:T(8,128)(2,1)S(1)} %add_convert_fusion.refs_0_), channel_id=1, source_target_pairs={{0,3},{1,4},{2,7},{3,0},{4,1},{5,6},{6,5},{7,2},{8,13},{9,10},{10,... | collective-permute-start | bytes 294920 | tf_op jit(solution)/shard_map/ppermute | solution.py:195
  21.5 4.6 %collective-permute-start.8 = (bf16[16,3072]{1,0:T(8,128)(2,1)S(1)}, bf16[16,3072]{1,0:T(8,128)(2,1)S(1)}, u32[]{:S(2)}, u32[]{:S(2)}) collective-permute-start(bf16[16,3072]{1,0:T(8,128)(2,1)S(1)} %add_convert_fusion.refs_0_), channel_id=1, source_target_pairs={{0,2},{1,5},{2,6},{3,1},{4,0},{5,7},{6,4},{7,3},{8,12},{9,11},{10,... | collective-permute-start | bytes 294920 | tf_op jit(solution)/shard_map/ppermute | solution.py:195
  23.8 5.5 %collective-permute-start.6 = (bf16[3,32,384]{2,1,0:T(8,128)(2,1)S(1)}, bf16[3,32,384]{2,1,0:T(8,128)(2,1)S(1)}, u32[]{:S(2)}, u32[]{:S(2)}) collective-permute-start(bf16[3,32,384]{2,1,0:T(8,128)(2,1)S(1)} %others.2), channel_id=1, source_target_pairs={{0,16},{16,0},{1,17},{17,1},{2,18},{18,2},{3,19},{19,3},{4,20},{20... | collective-permute-start | bytes 221192 | tf_op jit(solution)/shard_map/ppermute | solution.py:223
  26.9 4.4 %collective-permute-start.9 = (bf16[3,32,384]{2,1,0:T(8,128)(2,1)S(1)}, bf16[3,32,384]{2,1,0:T(8,128)(2,1)S(1)}, u32[]{:S(2)}, u32[]{:S(2)}) collective-permute-start(bf16[3,32,384]{2,1,0:T(8,128)(2,1)S(1)} %others.3), channel_id=1, source_target_pairs={{0,16},{16,0},{1,17},{17,1},{2,18},{18,2},{3,19},{19,3},{4,20},{20... | collective-permute-start | bytes 221192 | tf_op jit(solution)/shard_map/ppermute | solution.py:223

commit v6 on v5

--- a/solution.py
+++ b/solution.py
@@ -107,14 +107,16 @@
     return jnp.where(side == 0, max(low, 0), c + 1 if c < near else 0)
 
 
-def section_kernel(near, outside_ref, stand_ref, *refs):
+def turn_kernel(stand_ref, turned_ref):
+    turned_ref[...] = stand_ref[...].T
+
+
+def section_kernel(near, outside_ref, turned_ref, *refs):
     pieces, got_ref, out_ref = refs[:2], refs[2], refs[-1]
     count = outside_ref.shape[0]
     spread = [p[...] for p in pieces] if out_ref.shape[0] > count else []
     spread += [p[...] * outside_ref[c] for c in range(count) for p in pieces]
-    product = lax.dot_general(
-        jnp.concatenate(spread, axis=0), stand_ref[...], (((1,), (1,)), ((), ())), preferred_element_type=jnp.float32
-    )
+    product = jnp.dot(jnp.concatenate(spread, axis=0), turned_ref[...], preferred_element_type=jnp.float32)
     product = product.reshape(out_ref.shape)
     if not near:
         out_ref[...] = product.astype(out_ref.dtype)
@@ -201,8 +203,18 @@
     )
     rest = [1 << b for b in range(3, n_samp.bit_length() - 1)]
     low_bits, high_bits = rest + [4], [2] + rest
-    for low, high in zip(low_bits, high_bits):
+    turned = pl.pallas_call(
+        turn_kernel,
+        out_shape=jax.ShapeDtypeStruct((variants, rows), jnp.bfloat16),
+        in_specs=[vmem],
+        out_specs=vmem,
+        compiler_params=params,
+        name="turn",
+    )(standard)
+    for step, (low, high) in enumerate(zip(low_bits, high_bits)):
         mine_sum = mine_sum + swap(mine_sum.astype(jnp.bfloat16), low | 1, high | 1)
+        if step == 0:
+            mine_sum, turned = lax.optimization_barrier((mine_sum, turned))
     first = mine_sum.astype(jnp.bfloat16)
     second, second_sibling = swap(first, 3, 5), swap(first, 2, 4)
 
@@ -217,7 +229,7 @@
                 flops=rows * variants * half * sections, bytes_accessed=rows * variants * 2, transcendentals=0
             ),
             name=name,
-        )(outside, standard, *pieces, *got)
+        )(outside, turned, *pieces, *got)
 
     def swap_chrom(x, bit):
         return lax.ppermute(x, "chrom", [(i, i ^ bit) for i in range(n_chrom)])

time: 32.3 us -> 31.9 us (0.988)
  starting transfers between devices: 14.6 us -> 13.6 us
  waiting for transfers between devices: 8.95 us -> 9.9 us
  Pallas kernels: 7.69 us -> 7.31 us
    ppermute x8, starting transfers between devices: 11.5 us -> 10.4 us  [swap(): lax.ppermute(x, 'samp', [(i, i ^ (high if i.bit_count() % 2 else low)) fo...]
    pallas_call x4, Pallas kernels: 3.31 us -> 2.26 us  [products(): pl.pallas_call(functools.partial(section_kernel, near if got else 0), out...]
    pallas_call x0 -> x1, Pallas kernels: none -> 0.67 us  [on_device(): pl.pallas_call(turn_kernel, out_shape=jax.ShapeDtypeStruct((variants, row...]
    ppermute x2, waiting for transfers between devices: 1.18 us -> 1.81 us  [swap_chrom(): return lax.ppermute(x, 'chrom', [(i, i ^ bit) for i in range(n_chrom)])]
    ppermute x8, waiting for transfers between devices: 7.77 us -> 8.09 us  [swap(): lax.ppermute(x, 'samp', [(i, i ^ (high if i.bit_count() % 2 else low)) fo...]
  transfers between devices with their start and end apart: 10 -> 10, of which waited for: 6 -> 7; matrix products, arithmetic and copies ran while one was open for 0% -> 0% of each run, Pallas kernels for 13% -> 12%
where the time goes in v6:
time: 31.9 us; the launch traced here: 31.8 us
  starting transfers between devices  13.6 us (43%)
  waiting for transfers between devices  9.9 us (31%)
  Pallas kernels  7.31 us (23%)
  between operations  0.76 us (2%)
    ppermute x8, starting transfers between devices, swap(): lax.ppermute(x, 'samp', [(i, i ^ (high if i.bit_count() % 2 else low)) fo...  10.4 us
    ppermute x8, waiting for transfers between devices, swap(): lax.ppermute(x, 'samp', [(i, i ^ (high if i.bit_count() % 2 else low)) fo...  8.09 us
    ppermute x2, starting transfers between devices, swap_chrom(): return lax.ppermute(x, 'chrom', [(i, i ^ bit) for i in range(n_chrom)])  3.26 us
    pallas_call x1, Pallas kernels, on_device(): pl.pallas_call(functools.partial(cross_kernel, blocks), out_shape=(jax.Sh...  2.79 us
    pallas_call x4, Pallas kernels, products(): pl.pallas_call(functools.partial(section_kernel, near if got else 0), out...  2.26 us
    ppermute x2, waiting for transfers between devices, swap_chrom(): return lax.ppermute(x, 'chrom', [(i, i ^ bit) for i in range(n_chrom)])  1.81 us
    pallas_call x1, Pallas kernels, on_device(): pl.pallas_call(functools.partial(finish_kernel, near if n_chrom == 2 else...  0.82 us
    pallas_call x1, Pallas kernels, on_device(): pl.pallas_call(functools.partial(prepare_kernel, variants * n_chrom), out...  0.77 us
  transfers between devices with their start and end apart: 10, of which 7 were waited for; matrix products, arithmetic and copies ran while one was open for 0% of the time, Pallas kernels for 12%

profile of v6, /device:TPU:0, one launch (start us, length us, event | category | flops | bytes accessed | tf_op | source)
XLA Modules:
  0.0 31.8 jit_solution(10178741619265696238)
XLA Ops:
  0.0 0.0 copy-start
  0.0 0.0 copy-start.1
  0.0 2.8 %cross.1 = (bf16[384,3072]{1,0:T(8,128)(2,1)S(1)}, bf16[16,3072]{1,0:T(8,128)(2,1)S(1)}, bf16[16,3072]{1,0:T(8,128)(2,1)S(1)}, f32[16,3072]{1,0:T(8,128)S(1)}, f32[16,3072]{1,0:T(8,128)S(1)}) custom-call(s32[384,3072]{1,0:T(8,128)} %geno_hbm.1, f32[1,3072]{1,0:T(1,128)} %bitcast.5, f32[64,384]{1,0:T(8,128)} %bitcast.3), custom_call_target="tpu_custom_call" | custom-call | tf_op jit(solution)/shard_map/cross/pallas_call | solution.py:162
  2.8 0.5 %collective-permute-start.1 = (bf16[16,3072]{1,0:T(8,128)(2,1)S(1)}, bf16[16,3072]{1,0:T(8,128)(2,1)S(1)}, u32[]{:S(2)}, u32[]{:S(2)}) collective-permute-start(bf16[16,3072]{1,0:T(8,128)(2,1)S(1)} %get-tuple-element.24), channel_id=1, source_target_pairs={{0,1},{1,0},{2,3},{3,2},{4,5},{5,4},{6,7},{7,6},{8,9},{9,8},{10,11... | collective-permute-start | bytes 294920 | tf_op jit(solution)/shard_map/ppermute | solution.py:197
  3.3 0.1 collective-permute-start
  3.4 0.9 %collective-permute-done.1 = bf16[16,3072]{1,0:T(8,128)(2,1)S(1)} collective-permute-done((bf16[16,3072]{1,0:T(8,128)(2,1)S(1)}, bf16[16,3072]{1,0:T(8,128)(2,1)S(1)}, u32[]{:S(2)}, u32[]{:S(2)}) %collective-permute-start.1) | collective-permute-done | bytes 98336 | tf_op jit(solution)/shard_map/ppermute | solution.py:197
  4.3 2.7 %collective-permute-start.2 = (bf16[16,3072]{1,0:T(8,128)(2,1)S(1)}, bf16[16,3072]{1,0:T(8,128)(2,1)S(1)}, u32[]{:S(2)}, u32[]{:S(2)}) collective-permute-start(bf16[16,3072]{1,0:T(8,128)(2,1)S(1)} %add_convert_fusion.1), channel_id=1, source_target_pairs={{0,3},{1,4},{2,7},{3,0},{4,1},{5,6},{6,5},{7,2},{8,13},{9,10},{10,... | collective-permute-start | bytes 294920 | tf_op jit(solution)/shard_map/ppermute | solution.py:197
  7.6 0.0 copy-done
  7.6 0.0 copy-done.1
  7.7 0.8 %prepare.1 = (bf16[2,16,3072]{2,1,0:T(8,128)(2,1)S(1)}, bf16[4,16,3072]{2,1,0:T(8,128)(2,1)S(1)}, f32[4,16,384]{2,1,0:T(8,128)S(1)}, f32[64,384]{1,0:T(8,128)S(1)}) custom-call(s32[8]{0:T(128)S(1)} %copy-done.1, f32[1]{0:T(128)S(6)} %copy.6.ridge_ref, f32[64,384]{1,0:T(8,128)S(1)} %bitcast.4), custom_call_target="tpu_custom_call" | custom-call | tf_op jit(solution)/shard_map/prepare/pallas_call | solution.py:182
  8.4 0.0 collective-permute-done
  8.4 0.8 %collective-permute-done.2 = bf16[16,3072]{1,0:T(8,128)(2,1)S(1)} collective-permute-done((bf16[16,3072]{1,0:T(8,128)(2,1)S(1)}, bf16[16,3072]{1,0:T(8,128)(2,1)S(1)}, u32[]{:S(2)}, u32[]{:S(2)}) %collective-permute-start.2) | collective-permute-done | bytes 98336 | tf_op jit(solution)/shard_map/ppermute | solution.py:197
  9.3 2.9 %collective-permute-start.3 = (bf16[16,3072]{1,0:T(8,128)(2,1)S(1)}, bf16[16,3072]{1,0:T(8,128)(2,1)S(1)}, u32[]{:S(2)}, u32[]{:S(2)}) collective-permute-start(bf16[16,3072]{1,0:T(8,128)(2,1)S(1)} %convert_element_type.31), channel_id=1, source_target_pairs={{0,9},{1,2},{2,1},{3,10},{4,7},{5,12},{6,15},{7,4},{8,11},{9,0},{1... | collective-permute-start | bytes 294920 | tf_op jit(solution)/shard_map/ppermute | solution.py:197
  12.2 0.7 %turn.1.turned_ref = bf16[3072,384]{1,0:T(8,128)(2,1)S(1)} custom-call(bf16[384,3072]{1,0:T(8,128)(2,1)S(1)} %get-tuple-element.33.stand_ref), custom_call_target="tpu_custom_call" | custom-call | tf_op jit(solution)/shard_map/turn/pallas_call | solution.py:206
  12.9 1.6 %collective-permute-done.3 = bf16[16,3072]{1,0:T(8,128)(2,1)S(1)} collective-permute-done((bf16[16,3072]{1,0:T(8,128)(2,1)S(1)}, bf16[16,3072]{1,0:T(8,128)(2,1)S(1)}, u32[]{:S(2)}, u32[]{:S(2)}) %collective-permute-start.3) | collective-permute-done | bytes 98336 | tf_op jit(solution)/shard_map/ppermute | solution.py:197
  14.6 1.9 %collective-permute-start.4 = (bf16[16,3072]{1,0:T(8,128)(2,1)S(1)}, bf16[16,3072]{1,0:T(8,128)(2,1)S(1)}, u32[]{:S(2)}, u32[]{:S(2)}) collective-permute-start(bf16[16,3072]{1,0:T(8,128)(2,1)S(1)} %convert_element_type.33), channel_id=1, source_target_pairs={{0,5},{1,8},{2,11},{3,6},{4,13},{5,0},{6,3},{7,14},{8,1},{9,12},{1... | collective-permute-start | bytes 294920 | tf_op jit(solution)/shard_map/ppermute | solution.py:197
  16.5 3.0 %collective-permute-done.4 = bf16[16,3072]{1,0:T(8,128)(2,1)S(1)} collective-permute-done((bf16[16,3072]{1,0:T(8,128)(2,1)S(1)}, bf16[16,3072]{1,0:T(8,128)(2,1)S(1)}, u32[]{:S(2)}, u32[]{:S(2)}) %collective-permute-start.4) | collective-permute-done | bytes 98336 | tf_op jit(solution)/shard_map/ppermute | solution.py:197
  19.5 0.9 %collective-permute-start.5 = (bf16[16,3072]{1,0:T(8,128)(2,1)S(1)}, bf16[16,3072]{1,0:T(8,128)(2,1)S(1)}, u32[]{:S(2)}, u32[]{:S(2)}) collective-permute-start(bf16[16,3072]{1,0:T(8,128)(2,1)S(1)} %add_convert_fusion.refs_0_), channel_id=1, source_target_pairs={{0,1},{1,0},{2,3},{3,2},{4,5},{5,4},{6,7},{7,6},{8,9},{9,8},{10,11... | collective-permute-start | bytes 294920 | tf_op jit(solution)/shard_map/ppermute | solution.py:197
  20.4 1.4 %collective-permute-start.8 = (bf16[16,3072]{1,0:T(8,128)(2,1)S(1)}, bf16[16,3072]{1,0:T(8,128)(2,1)S(1)}, u32[]{:S(2)}, u32[]{:S(2)}) collective-permute-start(bf16[16,3072]{1,0:T(8,128)(2,1)S(1)} %add_convert_fusion.refs_0_), channel_id=1, source_target_pairs={{0,2},{1,5},{2,6},{3,1},{4,0},{5,7},{6,4},{7,3},{8,12},{9,11},{10,... | collective-permute-start | bytes 294920 | tf_op jit(solution)/shard_map/ppermute | solution.py:197
  21.8 0.0 collective-permute-start.7
  21.8 0.0 collective-permute-done.5.refs_1_
  21.8 0.5 %others.2 = bf16[3,32,384]{2,1,0:T(8,128)(2,1)S(1)} custom-call(bf16[2,16,3072]{2,1,0:T(8,128)(2,1)S(1)} %get-tuple-element.36.outside_ref, bf16[3072,384]{1,0:T(8,128)(2,1)S(1)} %turn.1.turned_ref, bf16[16,3072]{1,0:T(8,128)(2,1)S(1)} %add_convert_fusion.refs_0_, bf16[16,3072]{1,0:T(8,128)(2,1)S(1)} %collective-permute-done.5.refs_1_), custom_call_target="tpu_custom_call" | custom-call | flops 301989888 | bytes 2359296 | tf_op jit(solution)/shard_map/others/pallas_call | solution.py:222
  22.4 1.7 %collective-permute-start.6 = (bf16[3,32,384]{2,1,0:T(8,128)(2,1)S(1)}, bf16[3,32,384]{2,1,0:T(8,128)(2,1)S(1)}, u32[]{:S(2)}, u32[]{:S(2)}) collective-permute-start(bf16[3,32,384]{2,1,0:T(8,128)(2,1)S(1)} %others.2), channel_id=1, source_target_pairs={{0,16},{16,0},{1,17},{17,1},{2,18},{18,2},{3,19},{19,3},{4,20},{20... | collective-permute-start | bytes 221192 | tf_op jit(solution)/shard_map/ppermute | solution.py:235
  24.1 0.9 %collective-permute-done.8.refs_1_ = bf16[16,3072]{1,0:T(8,128)(2,1)S(1)} collective-permute-done((bf16[16,3072]{1,0:T(8,128)(2,1)S(1)}, bf16[16,3072]{1,0:T(8,128)(2,1)S(1)}, u32[]{:S(2)}, u32[]{:S(2)}) %collective-permute-start.8) | collective-permute-done | bytes 98336 | tf_op jit(solution)/shard_map/ppermute | solution.py:197
  25.0 0.9 %collective-permute-done.7.refs_0_ = bf16[16,3072]{1,0:T(8,128)(2,1)S(1)} collective-permute-done((bf16[16,3072]{1,0:T(8,128)(2,1)S(1)}, bf16[16,3072]{1,0:T(8,128)(2,1)S(1)}, u32[]{:S(2)}, u32[]{:S(2)}) %collective-permute-start.7) | collective-permute-done | bytes 98336 | tf_op jit(solution)/shard_map/ppermute | solution.py:197
  25.9 0.5 %others.3 = bf16[3,32,384]{2,1,0:T(8,128)(2,1)S(1)} custom-call(bf16[2,16,3072]{2,1,0:T(8,128)(2,1)S(1)} %get-tuple-element.36.outside_ref, bf16[3072,384]{1,0:T(8,128)(2,1)S(1)} %turn.1.turned_ref, bf16[16,3072]{1,0:T(8,128)(2,1)S(1)} %collective-permute-done.7.refs_0_, bf16[16,3072]{1,0:T(8,128)(2,1)S(1)} %collective-permute-done.8.refs_1_), custom_call_target="tpu_custom_call" | custom-call | flops 301989888 | bytes 2359296 | tf_op jit(solution)/shard_map/others/pallas_call | solution.py:222
  26.4 1.5 %collective-permute-start.9 = (bf16[3,32,384]{2,1,0:T(8,128)(2,1)S(1)}, bf16[3,32,384]{2,1,0:T(8,128)(2,1)S(1)}, u32[]{:S(2)}, u32[]{:S(2)}) collective-permute-start(bf16[3,32,384]{2,1,0:T(8,128)(2,1)S(1)} %others.3), channel_id=1, source_target_pairs={{0,16},{16,0},{1,17},{17,1},{2,18},{18,2},{3,19},{19,3},{4,20},{20... | collective-permute-start | bytes 221192 | tf_op jit(solution)/shard_map/ppermute | solution.py:235
  27.9 0.6 %own.3.refs_1_ = f32[4,32,384]{2,1,0:T(8,128)S(1)} custom-call(bf16[4,16,3072]{2,1,0:T(8,128)(2,1)S(1)} %get-tuple-element.31.outside_ref, bf16[3072,384]{1,0:T(8,128)(2,1)S(1)} %turn.1.turned_ref, bf16[16,3072]{1,0:T(8,128)(2,1)S(1)} %collective-permute-done.7.refs_0_, bf16[16,3072]{1,0:T(8,128)(2,1)S(1)} %collective-permute-done.8.refs_1_), custom_call_target="tpu_custom_call" | custom-call | flops 301989888 | bytes 2359296 | tf_op jit(solution)/shard_map/own/pallas_call | solution.py:222
  28.5 0.0 collective-permute-done.6.refs_2_
  28.5 0.6 %own.2.refs_0_ = f32[4,32,384]{2,1,0:T(8,128)S(1)} custom-call(bf16[4,16,3072]{2,1,0:T(8,128)(2,1)S(1)} %get-tuple-element.31.outside_ref, bf16[3072,384]{1,0:T(8,128)(2,1)S(1)} %turn.1.turned_ref, bf16[16,3072]{1,0:T(8,128)(2,1)S(1)} %add_convert_fusion.refs_0_, bf16[16,3072]{1,0:T(8,128)(2,1)S(1)} %collective-permute-done.5.refs_1_, ...), custom_call_target="tpu_custom_call" | custom-call | flops 301989888 | bytes 2359296 | tf_op jit(solution)/shard_map/own/pallas_call | solution.py:222
  29.1 1.8 %collective-permute-done.9.refs_2_ = bf16[3,32,384]{2,1,0:T(8,128)(2,1)S(1)} collective-permute-done((bf16[3,32,384]{2,1,0:T(8,128)(2,1)S(1)}, bf16[3,32,384]{2,1,0:T(8,128)(2,1)S(1)}, u32[]{:S(2)}, u32[]{:S(2)}) %collective-permute-start.9) | collective-permute-done | bytes 73760 | tf_op jit(solution)/shard_map/ppermute | solution.py:235
  30.9 0.8 %finish.1 = f32[4,64,384]{2,1,0:T(8,128)} custom-call(f32[4,16,384]{2,1,0:T(8,128)S(1)} %get-tuple-element.29.inverse_ref, f32[64,384]{1,0:T(8,128)S(1)} %get-tuple-element.30.ridged_ref, f32[4,32,384]{2,1,0:T(8,128)S(1)} %own.2.refs_0_, f32[4,32,384]{2,1,0:T(8,128)S(1)} %own.3.refs_1_, bf16[3,32,384]{2,1,0:T(8,128)(2,1)S(1)} %collective-permute-done.9.refs_2_), custom_call_target="tpu_custom_call" | custom-call | tf_op jit(solution)/shard_map/finish/pallas_call | solution.py:263
  (6 shorter events, 0.1 us)
Async XLA Ops:
  0.0 7.6 %copy-start = (f32[384,64]{0,1:T(8,128)S(1)}, f32[384,64]{0,1:T(8,128)}, u32[]{:S(2)}) copy-start(f32[384,64]{0,1:T(8,128)} %param.9) | copy-start | bytes 294916
  0.0 7.6 %copy-start.1 = (s32[8]{0:T(128)S(1)}, s32[8]{0:T(128)}, u32[]{:S(2)}) copy-start(s32[8]{0:T(128)} %widths_ref.1) | copy-start | bytes 100
  2.8 1.5 %collective-permute-start.1 = (bf16[16,3072]{1,0:T(8,128)(2,1)S(1)}, bf16[16,3072]{1,0:T(8,128)(2,1)S(1)}, u32[]{:S(2)}, u32[]{:S(2)}) collective-permute-start(bf16[16,3072]{1,0:T(8,128)(2,1)S(1)} %get-tuple-element.24), channel_id=1, source_target_pairs={{0,1},{1,0},{2,3},{3,2},{4,5},{5,4},{6,7},{7,6},{8,9},{9,8},{10,11... | collective-permute-start | bytes 294920 | tf_op jit(solution)/shard_map/ppermute | solution.py:197
  3.3 5.1 %collective-permute-start = (bf16[16,3072]{1,0:T(8,128)(2,1)S(1)}, bf16[16,3072]{1,0:T(8,128)(2,1)S(1)}, u32[]{:S(2)}, u32[]{:S(2)}) collective-permute-start(bf16[16,3072]{1,0:T(8,128)(2,1)S(1)} %get-tuple-element.22), channel_id=1, source_target_pairs={{0,1},{1,0},{2,3},{3,2},{4,5},{5,4},{6,7},{7,6},{8,9},{9,8},{10,11... | collective-permute-start | bytes 294920 | tf_op jit(solution)/shard_map/ppermute | solution.py:197
  4.3 5.0 %collective-permute-start.2 = (bf16[16,3072]{1,0:T(8,128)(2,1)S(1)}, bf16[16,3072]{1,0:T(8,128)(2,1)S(1)}, u32[]{:S(2)}, u32[]{:S(2)}) collective-permute-start(bf16[16,3072]{1,0:T(8,128)(2,1)S(1)} %add_convert_fusion.1), channel_id=1, source_target_pairs={{0,3},{1,4},{2,7},{3,0},{4,1},{5,6},{6,5},{7,2},{8,13},{9,10},{10,... | collective-permute-start | bytes 294920 | tf_op jit(solution)/shard_map/ppermute | solution.py:197
  9.3 5.2 %collective-permute-start.3 = (bf16[16,3072]{1,0:T(8,128)(2,1)S(1)}, bf16[16,3072]{1,0:T(8,128)(2,1)S(1)}, u32[]{:S(2)}, u32[]{:S(2)}) collective-permute-start(bf16[16,3072]{1,0:T(8,128)(2,1)S(1)} %convert_element_type.31), channel_id=1, source_target_pairs={{0,9},{1,2},{2,1},{3,10},{4,7},{5,12},{6,15},{7,4},{8,11},{9,0},{1... | collective-permute-start | bytes 294920 | tf_op jit(solution)/shard_map/ppermute | solution.py:197
  14.6 4.9 %collective-permute-start.4 = (bf16[16,3072]{1,0:T(8,128)(2,1)S(1)}, bf16[16,3072]{1,0:T(8,128)(2,1)S(1)}, u32[]{:S(2)}, u32[]{:S(2)}) collective-permute-start(bf16[16,3072]{1,0:T(8,128)(2,1)S(1)} %convert_element_type.33), channel_id=1, source_target_pairs={{0,5},{1,8},{2,11},{3,6},{4,13},{5,0},{6,3},{7,14},{8,1},{9,12},{1... | collective-permute-start | bytes 294920 | tf_op jit(solution)/shard_map/ppermute | solution.py:197
  19.5 2.3 %collective-permute-start.5 = (bf16[16,3072]{1,0:T(8,128)(2,1)S(1)}, bf16[16,3072]{1,0:T(8,128)(2,1)S(1)}, u32[]{:S(2)}, u32[]{:S(2)}) collective-permute-start(bf16[16,3072]{1,0:T(8,128)(2,1)S(1)} %add_convert_fusion.refs_0_), channel_id=1, source_target_pairs={{0,1},{1,0},{2,3},{3,2},{4,5},{5,4},{6,7},{7,6},{8,9},{9,8},{10,11... | collective-permute-start | bytes 294920 | tf_op jit(solution)/shard_map/ppermute | solution.py:197
  20.4 4.6 %collective-permute-start.8 = (bf16[16,3072]{1,0:T(8,128)(2,1)S(1)}, bf16[16,3072]{1,0:T(8,128)(2,1)S(1)}, u32[]{:S(2)}, u32[]{:S(2)}) collective-permute-start(bf16[16,3072]{1,0:T(8,128)(2,1)S(1)} %add_convert_fusion.refs_0_), channel_id=1, source_target_pairs={{0,2},{1,5},{2,6},{3,1},{4,0},{5,7},{6,4},{7,3},{8,12},{9,11},{10,... | collective-permute-start | bytes 294920 | tf_op jit(solution)/shard_map/ppermute | solution.py:197
  21.8 4.0 %collective-permute-start.7 = (bf16[16,3072]{1,0:T(8,128)(2,1)S(1)}, bf16[16,3072]{1,0:T(8,128)(2,1)S(1)}, u32[]{:S(2)}, u32[]{:S(2)}) collective-permute-start(bf16[16,3072]{1,0:T(8,128)(2,1)S(1)} %add_convert_fusion.refs_0_), channel_id=1, source_target_pairs={{0,3},{1,4},{2,7},{3,0},{4,1},{5,6},{6,5},{7,2},{8,13},{9,10},{10,... | collective-permute-start | bytes 294920 | tf_op jit(solution)/shard_map/ppermute | solution.py:197
  22.4 6.2 %collective-permute-start.6 = (bf16[3,32,384]{2,1,0:T(8,128)(2,1)S(1)}, bf16[3,32,384]{2,1,0:T(8,128)(2,1)S(1)}, u32[]{:S(2)}, u32[]{:S(2)}) collective-permute-start(bf16[3,32,384]{2,1,0:T(8,128)(2,1)S(1)} %others.2), channel_id=1, source_target_pairs={{0,16},{16,0},{1,17},{17,1},{2,18},{18,2},{3,19},{19,3},{4,20},{20... | collective-permute-start | bytes 221192 | tf_op jit(solution)/shard_map/ppermute | solution.py:235
  26.4 4.5 %collective-permute-start.9 = (bf16[3,32,384]{2,1,0:T(8,128)(2,1)S(1)}, bf16[3,32,384]{2,1,0:T(8,128)(2,1)S(1)}, u32[]{:S(2)}, u32[]{:S(2)}) collective-permute-start(bf16[3,32,384]{2,1,0:T(8,128)(2,1)S(1)} %others.3), channel_id=1, source_target_pairs={{0,16},{16,0},{1,17},{17,1},{2,18},{18,2},{3,19},{19,3},{4,20},{20... | collective-permute-start | bytes 221192 | tf_op jit(solution)/shard_map/ppermute | solution.py:235

commit v7 on v6

--- a/solution.py
+++ b/solution.py
@@ -126,22 +126,28 @@
         out_ref[c] = product[c] + got_ref[received(c, 2 * count, near, side)].astype(jnp.float32)
 
 
-def finish_kernel(near, inverse_ref, ridged_ref, *refs):
-    head_ref, tail_ref, got_ref, out_ref = refs
-    per_device, rhs, _ = out_ref.shape
+def finish_kernel(near, group, inverse_ref, ridged_ref, own_ref, *refs):
+    out_hbm, done, sems = refs[-3:]
+    got = refs[:-3]
+    per_device, rhs, _ = out_hbm.shape
     side = lax.axis_index("chrom")
     places = [received(c, 2 * per_device, near, side) if near else c for c in range(per_device)]
     quarter = rhs // 4
-    for p, row in enumerate(piece_rows(rhs)):
-        at = pl.ds(pl.multiple_of(row, quarter), quarter)
-        ridged = ridged_ref[pl.ds(p * quarter, quarter), :]
-        here = pl.ds((p % 2) * quarter, quarter)
+    rows = piece_rows(rhs)[2 * group : 2 * group + 2]
+    copies = []
+    for p, row in enumerate(rows):
+        here = pl.ds(p * quarter, quarter)
+        ridged = ridged_ref[pl.ds((2 * group + p) * quarter, quarter), :]
         for c in range(per_device):
-            if p < 2:
-                rest = head_ref[c, here, :]
-            else:
-                rest = tail_ref[c, here, :] + got_ref[places[c], here, :].astype(jnp.float32)
-            out_ref[c, at, :] = ridged + rest * inverse_ref[c]
+            rest = own_ref[c, here, :]
+            if group == 1:
+                rest = rest + got[0][places[c], here, :].astype(jnp.float32)
+            done[p, c] = ridged + rest * inverse_ref[c]
+        to = out_hbm.at[:, pl.ds(pl.multiple_of(row, quarter), quarter), :]
+        copies.append(pltpu.make_async_copy(done.at[p], to, sems.at[p]))
+        copies[-1].start()
+    for copy in copies:
+        copy.wait()
 
 
 def on_device(genotypes, frequency, widths, ridge_term, direction):
@@ -153,6 +159,7 @@
     half, quarter = rhs // 2, rhs // 4
     vmem = pl.BlockSpec(memory_space=pltpu.VMEM)
     smem = pl.BlockSpec(memory_space=pltpu.SMEM)
+    anywhere = pl.BlockSpec(memory_space=pl.ANY)
     params = pltpu.CompilerParams(vmem_limit_bytes=VMEM_LIMIT)
     dir_t = direction.T
 
@@ -177,7 +184,7 @@
         name="cross",
     )(*(pltpu.with_memory_space_constraint(a, pltpu.HBM) for a in operands))
 
-    near = max(1, sections // 4)
+    near = max(1, sections // 2 - 2)
     mask = lambda count: jax.ShapeDtypeStruct((count, quarter, variants), jnp.bfloat16)
     outside_others, outside_own, inverse, ridged = pl.pallas_call(
         functools.partial(prepare_kernel, variants * n_chrom),
@@ -260,14 +267,23 @@
     if n_chrom > 2:
         owns[0] = owns[0] + gots[0]
 
-    out = pl.pallas_call(
-        functools.partial(finish_kernel, near if n_chrom == 2 else 0),
-        out_shape=jax.ShapeDtypeStruct((per_device, rhs, rows), jnp.float32),
-        in_specs=[vmem] * 5,
-        out_specs=vmem,
-        compiler_params=params,
-        name="finish",
-    )(inverse, ridged, *owns, gots[1])
+    def finish(group, *operands):
+        return pl.pallas_call(
+            functools.partial(finish_kernel, near if n_chrom == 2 else 0, group),
+            out_shape=jax.ShapeDtypeStruct((per_device, rhs, rows), jnp.float32),
+            in_specs=[vmem] * (3 + group) + [anywhere] * group,
+            out_specs=anywhere,
+            scratch_shapes=[
+                pltpu.VMEM((2, per_device, quarter, rows), jnp.float32),
+                pltpu.SemaphoreType.DMA((2,)),
+            ],
+            input_output_aliases={4: 0} if group else {},
+            compiler_params=params,
+            name="finish",
+        )(inverse, ridged, *operands)
+
+    out = pltpu.with_memory_space_constraint(finish(0, owns[0]), pltpu.HBM)
+    out = finish(1, owns[1], gots[1], out)
     return jnp.transpose(out, (0, 2, 1))
 
 

time: 31.9 us -> 31.8 us (level)
  waiting for transfers between devices: 9.9 us -> 9.17 us
  Pallas kernels: 7.31 us -> 7.93 us
    ppermute x2, waiting for transfers between devices: 1.81 us -> 1.08 us  [swap_chrom(): return lax.ppermute(x, 'chrom', [(i, i ^ bit) for i in range(n_chrom)])]
    pallas_call x1 -> x2, Pallas kernels: 0.82 us -> 1.44 us  [finish(): pl.pallas_call(functools.partial(finish_kernel, near if n_chrom == 2 else...]
  transfers between devices with their start and end apart: 10 -> 10, of which waited for: 7 -> 7; matrix products, arithmetic and copies ran while one was open for 0% -> 0% of each run, Pallas kernels for 12% -> 14%
where the time goes in v7:
time: 31.8 us; the launch traced here: 31.7 us
  starting transfers between devices  13.6 us (43%)
  waiting for transfers between devices  9.17 us (29%)
  Pallas kernels  7.93 us (25%)
  between operations  0.77 us (2%)
    ppermute x8, starting transfers between devices, swap(): lax.ppermute(x, 'samp', [(i, i ^ (high if i.bit_count() % 2 else low)) fo...  10.4 us
    ppermute x8, waiting for transfers between devices, swap(): lax.ppermute(x, 'samp', [(i, i ^ (high if i.bit_count() % 2 else low)) fo...  8.09 us
    ppermute x2, starting transfers between devices, swap_chrom(): return lax.ppermute(x, 'chrom', [(i, i ^ bit) for i in range(n_chrom)])  3.26 us
    pallas_call x1, Pallas kernels, on_device(): pl.pallas_call(functools.partial(cross_kernel, blocks), out_shape=(jax.Sh...  2.79 us
    pallas_call x4, Pallas kernels, products(): pl.pallas_call(functools.partial(section_kernel, near if got else 0), out...  2.26 us
    pallas_call x2, Pallas kernels, finish(): pl.pallas_call(functools.partial(finish_kernel, near if n_chrom == 2 else...  1.44 us
    ppermute x2, waiting for transfers between devices, swap_chrom(): return lax.ppermute(x, 'chrom', [(i, i ^ bit) for i in range(n_chrom)])  1.08 us
    pallas_call x1, Pallas kernels, on_device(): pl.pallas_call(functools.partial(prepare_kernel, variants * n_chrom), out...  0.77 us
  transfers between devices with their start and end apart: 10, of which 7 were waited for; matrix products, arithmetic and copies ran while one was open for 0% of the time, Pallas kernels for 14%

profile of v7, /device:TPU:0, one launch (start us, length us, event | category | flops | bytes accessed | tf_op | source)
XLA Modules:
  0.0 31.7 jit_solution(17629346343245068805)
XLA Ops:
  0.0 0.0 copy-start
  0.0 2.8 %cross.1 = (bf16[384,3072]{1,0:T(8,128)(2,1)S(1)}, bf16[16,3072]{1,0:T(8,128)(2,1)S(1)}, bf16[16,3072]{1,0:T(8,128)(2,1)S(1)}, f32[16,3072]{1,0:T(8,128)S(1)}, f32[16,3072]{1,0:T(8,128)S(1)}) custom-call(s32[384,3072]{1,0:T(8,128)} %geno_hbm.1, f32[1,3072]{1,0:T(1,128)} %bitcast.5, f32[64,384]{1,0:T(8,128)} %bitcast.3), custom_call_target="tpu_custom_call" | custom-call | tf_op jit(solution)/shard_map/cross/pallas_call | solution.py:169
  2.8 0.5 %collective-permute-start.1 = (bf16[16,3072]{1,0:T(8,128)(2,1)S(1)}, bf16[16,3072]{1,0:T(8,128)(2,1)S(1)}, u32[]{:S(2)}, u32[]{:S(2)}) collective-permute-start(bf16[16,3072]{1,0:T(8,128)(2,1)S(1)} %get-tuple-element.24), channel_id=1, source_target_pairs={{0,1},{1,0},{2,3},{3,2},{4,5},{5,4},{6,7},{7,6},{8,9},{9,8},{10,11... | collective-permute-start | bytes 294920 | tf_op jit(solution)/shard_map/ppermute | solution.py:204
  3.3 0.1 collective-permute-start
  3.4 0.9 %collective-permute-done.1 = bf16[16,3072]{1,0:T(8,128)(2,1)S(1)} collective-permute-done((bf16[16,3072]{1,0:T(8,128)(2,1)S(1)}, bf16[16,3072]{1,0:T(8,128)(2,1)S(1)}, u32[]{:S(2)}, u32[]{:S(2)}) %collective-permute-start.1) | collective-permute-done | bytes 98336 | tf_op jit(solution)/shard_map/ppermute | solution.py:204
  4.3 2.7 %collective-permute-start.2 = (bf16[16,3072]{1,0:T(8,128)(2,1)S(1)}, bf16[16,3072]{1,0:T(8,128)(2,1)S(1)}, u32[]{:S(2)}, u32[]{:S(2)}) collective-permute-start(bf16[16,3072]{1,0:T(8,128)(2,1)S(1)} %add_convert_fusion.1), channel_id=1, source_target_pairs={{0,3},{1,4},{2,7},{3,0},{4,1},{5,6},{6,5},{7,2},{8,13},{9,10},{10,... | collective-permute-start | bytes 294920 | tf_op jit(solution)/shard_map/ppermute | solution.py:204
  7.6 0.0 copy-done
  7.6 0.0 copy-done.1
  7.7 0.8 %prepare.1 = (bf16[2,16,3072]{2,1,0:T(8,128)(2,1)S(1)}, bf16[4,16,3072]{2,1,0:T(8,128)(2,1)S(1)}, f32[4,16,384]{2,1,0:T(8,128)S(1)}, f32[64,384]{1,0:T(8,128)S(1)}) custom-call(s32[8]{0:T(128)S(1)} %copy-done.1, f32[1]{0:T(128)S(6)} %copy.8.ridge_ref, f32[64,384]{1,0:T(8,128)S(1)} %bitcast.4), custom_call_target="tpu_custom_call" | custom-call | tf_op jit(solution)/shard_map/prepare/pallas_call | solution.py:189
  8.4 0.0 collective-permute-done
  8.4 0.8 %collective-permute-done.2 = bf16[16,3072]{1,0:T(8,128)(2,1)S(1)} collective-permute-done((bf16[16,3072]{1,0:T(8,128)(2,1)S(1)}, bf16[16,3072]{1,0:T(8,128)(2,1)S(1)}, u32[]{:S(2)}, u32[]{:S(2)}) %collective-permute-start.2) | collective-permute-done | bytes 98336 | tf_op jit(solution)/shard_map/ppermute | solution.py:204
  9.3 2.9 %collective-permute-start.3 = (bf16[16,3072]{1,0:T(8,128)(2,1)S(1)}, bf16[16,3072]{1,0:T(8,128)(2,1)S(1)}, u32[]{:S(2)}, u32[]{:S(2)}) collective-permute-start(bf16[16,3072]{1,0:T(8,128)(2,1)S(1)} %convert_element_type.31), channel_id=1, source_target_pairs={{0,9},{1,2},{2,1},{3,10},{4,7},{5,12},{6,15},{7,4},{8,11},{9,0},{1... | collective-permute-start | bytes 294920 | tf_op jit(solution)/shard_map/ppermute | solution.py:204
  12.2 0.7 %turn.1.turned_ref = bf16[3072,384]{1,0:T(8,128)(2,1)S(1)} custom-call(bf16[384,3072]{1,0:T(8,128)(2,1)S(1)} %get-tuple-element.33.stand_ref), custom_call_target="tpu_custom_call" | custom-call | tf_op jit(solution)/shard_map/turn/pallas_call | solution.py:213
  12.9 1.6 %collective-permute-done.3 = bf16[16,3072]{1,0:T(8,128)(2,1)S(1)} collective-permute-done((bf16[16,3072]{1,0:T(8,128)(2,1)S(1)}, bf16[16,3072]{1,0:T(8,128)(2,1)S(1)}, u32[]{:S(2)}, u32[]{:S(2)}) %collective-permute-start.3) | collective-permute-done | bytes 98336 | tf_op jit(solution)/shard_map/ppermute | solution.py:204
  14.6 1.9 %collective-permute-start.4 = (bf16[16,3072]{1,0:T(8,128)(2,1)S(1)}, bf16[16,3072]{1,0:T(8,128)(2,1)S(1)}, u32[]{:S(2)}, u32[]{:S(2)}) collective-permute-start(bf16[16,3072]{1,0:T(8,128)(2,1)S(1)} %convert_element_type.33), channel_id=1, source_target_pairs={{0,5},{1,8},{2,11},{3,6},{4,13},{5,0},{6,3},{7,14},{8,1},{9,12},{1... | collective-permute-start | bytes 294920 | tf_op jit(solution)/shard_map/ppermute | solution.py:204
  16.5 3.0 %collective-permute-done.4 = bf16[16,3072]{1,0:T(8,128)(2,1)S(1)} collective-permute-done((bf16[16,3072]{1,0:T(8,128)(2,1)S(1)}, bf16[16,3072]{1,0:T(8,128)(2,1)S(1)}, u32[]{:S(2)}, u32[]{:S(2)}) %collective-permute-start.4) | collective-permute-done | bytes 98336 | tf_op jit(solution)/shard_map/ppermute | solution.py:204
  19.5 0.9 %collective-permute-start.8 = (bf16[16,3072]{1,0:T(8,128)(2,1)S(1)}, bf16[16,3072]{1,0:T(8,128)(2,1)S(1)}, u32[]{:S(2)}, u32[]{:S(2)}) collective-permute-start(bf16[16,3072]{1,0:T(8,128)(2,1)S(1)} %add_convert_fusion.refs_0_), channel_id=1, source_target_pairs={{0,1},{1,0},{2,3},{3,2},{4,5},{5,4},{6,7},{7,6},{8,9},{9,8},{10,11... | collective-permute-start | bytes 294920 | tf_op jit(solution)/shard_map/ppermute | solution.py:204
  20.4 1.4 %collective-permute-start.6 = (bf16[16,3072]{1,0:T(8,128)(2,1)S(1)}, bf16[16,3072]{1,0:T(8,128)(2,1)S(1)}, u32[]{:S(2)}, u32[]{:S(2)}) collective-permute-start(bf16[16,3072]{1,0:T(8,128)(2,1)S(1)} %add_convert_fusion.refs_0_), channel_id=1, source_target_pairs={{0,2},{1,5},{2,6},{3,1},{4,0},{5,7},{6,4},{7,3},{8,12},{9,11},{10,... | collective-permute-start | bytes 294920 | tf_op jit(solution)/shard_map/ppermute | solution.py:204
  21.8 0.0 collective-permute-start.5
  21.8 0.0 collective-permute-done.8.refs_1_
  21.8 0.5 %others.3 = bf16[3,32,384]{2,1,0:T(8,128)(2,1)S(1)} custom-call(bf16[2,16,3072]{2,1,0:T(8,128)(2,1)S(1)} %get-tuple-element.36.outside_ref, bf16[3072,384]{1,0:T(8,128)(2,1)S(1)} %turn.1.turned_ref, bf16[16,3072]{1,0:T(8,128)(2,1)S(1)} %add_convert_fusion.refs_0_, bf16[16,3072]{1,0:T(8,128)(2,1)S(1)} %collective-permute-done.8.refs_1_), custom_call_target="tpu_custom_call" | custom-call | flops 301989888 | bytes 2359296 | tf_op jit(solution)/shard_map/others/pallas_call | solution.py:229
  22.4 1.7 %collective-permute-start.9 = (bf16[3,32,384]{2,1,0:T(8,128)(2,1)S(1)}, bf16[3,32,384]{2,1,0:T(8,128)(2,1)S(1)}, u32[]{:S(2)}, u32[]{:S(2)}) collective-permute-start(bf16[3,32,384]{2,1,0:T(8,128)(2,1)S(1)} %others.3), channel_id=1, source_target_pairs={{0,16},{16,0},{1,17},{17,1},{2,18},{18,2},{3,19},{19,3},{4,20},{20... | collective-permute-start | bytes 221192 | tf_op jit(solution)/shard_map/ppermute | solution.py:242
  24.1 0.9 %collective-permute-done.6.refs_1_ = bf16[16,3072]{1,0:T(8,128)(2,1)S(1)} collective-permute-done((bf16[16,3072]{1,0:T(8,128)(2,1)S(1)}, bf16[16,3072]{1,0:T(8,128)(2,1)S(1)}, u32[]{:S(2)}, u32[]{:S(2)}) %collective-permute-start.6) | collective-permute-done | bytes 98336 | tf_op jit(solution)/shard_map/ppermute | solution.py:204
  25.0 0.9 %collective-permute-done.5.refs_0_ = bf16[16,3072]{1,0:T(8,128)(2,1)S(1)} collective-permute-done((bf16[16,3072]{1,0:T(8,128)(2,1)S(1)}, bf16[16,3072]{1,0:T(8,128)(2,1)S(1)}, u32[]{:S(2)}, u32[]{:S(2)}) %collective-permute-start.5) | collective-permute-done | bytes 98336 | tf_op jit(solution)/shard_map/ppermute | solution.py:204
  25.9 0.5 %others.2 = bf16[3,32,384]{2,1,0:T(8,128)(2,1)S(1)} custom-call(bf16[2,16,3072]{2,1,0:T(8,128)(2,1)S(1)} %get-tuple-element.36.outside_ref, bf16[3072,384]{1,0:T(8,128)(2,1)S(1)} %turn.1.turned_ref, bf16[16,3072]{1,0:T(8,128)(2,1)S(1)} %collective-permute-done.5.refs_0_, bf16[16,3072]{1,0:T(8,128)(2,1)S(1)} %collective-permute-done.6.refs_1_), custom_call_target="tpu_custom_call" | custom-call | flops 301989888 | bytes 2359296 | tf_op jit(solution)/shard_map/others/pallas_call | solution.py:229
  26.4 1.5 %collective-permute-start.7 = (bf16[3,32,384]{2,1,0:T(8,128)(2,1)S(1)}, bf16[3,32,384]{2,1,0:T(8,128)(2,1)S(1)}, u32[]{:S(2)}, u32[]{:S(2)}) collective-permute-start(bf16[3,32,384]{2,1,0:T(8,128)(2,1)S(1)} %others.2), channel_id=1, source_target_pairs={{0,16},{16,0},{1,17},{17,1},{2,18},{18,2},{3,19},{19,3},{4,20},{20... | collective-permute-start | bytes 221192 | tf_op jit(solution)/shard_map/ppermute | solution.py:242
  27.9 0.6 %own.2.own_ref = f32[4,32,384]{2,1,0:T(8,128)S(1)} custom-call(bf16[4,16,3072]{2,1,0:T(8,128)(2,1)S(1)} %get-tuple-element.31.outside_ref, bf16[3072,384]{1,0:T(8,128)(2,1)S(1)} %turn.1.turned_ref, bf16[16,3072]{1,0:T(8,128)(2,1)S(1)} %collective-permute-done.5.refs_0_, bf16[16,3072]{1,0:T(8,128)(2,1)S(1)} %collective-permute-done.6.refs_1_), custom_call_target="tpu_custom_call" | custom-call | flops 301989888 | bytes 2359296 | tf_op jit(solution)/shard_map/own/pallas_call | solution.py:229
  28.5 0.0 collective-permute-done.9.refs_2_
  28.5 0.6 %own.3.own_ref = f32[4,32,384]{2,1,0:T(8,128)S(1)} custom-call(bf16[4,16,3072]{2,1,0:T(8,128)(2,1)S(1)} %get-tuple-element.31.outside_ref, bf16[3072,384]{1,0:T(8,128)(2,1)S(1)} %turn.1.turned_ref, bf16[16,3072]{1,0:T(8,128)(2,1)S(1)} %add_convert_fusion.refs_0_, bf16[16,3072]{1,0:T(8,128)(2,1)S(1)} %collective-permute-done.8.refs_1_, ...), custom_call_target="tpu_custom_call" | custom-call | flops 301989888 | bytes 2359296 | tf_op jit(solution)/shard_map/own/pallas_call | solution.py:229
  29.1 0.7 %finish.2.refs_1_ = f32[4,64,384]{2,1,0:T(8,128)} custom-call(f32[4,16,384]{2,1,0:T(8,128)S(1)} %get-tuple-element.29.inverse_ref, f32[64,384]{1,0:T(8,128)S(1)} %get-tuple-element.30.ridged_ref, f32[4,32,384]{2,1,0:T(8,128)S(1)} %own.3.own_ref), custom_call_target="tpu_custom_call" | custom-call | tf_op jit(solution)/shard_map/finish/pallas_call | solution.py:271
  29.9 1.1 %collective-permute-done.7.refs_0_ = bf16[3,32,384]{2,1,0:T(8,128)(2,1)S(1)} collective-permute-done((bf16[3,32,384]{2,1,0:T(8,128)(2,1)S(1)}, bf16[3,32,384]{2,1,0:T(8,128)(2,1)S(1)}, u32[]{:S(2)}, u32[]{:S(2)}) %collective-permute-start.7) | collective-permute-done | bytes 73760 | tf_op jit(solution)/shard_map/ppermute | solution.py:242
  30.9 0.7 %finish.3 = f32[4,64,384]{2,1,0:T(8,128)} custom-call(f32[4,16,384]{2,1,0:T(8,128)S(1)} %get-tuple-element.29.inverse_ref, f32[64,384]{1,0:T(8,128)S(1)} %get-tuple-element.30.ridged_ref, f32[4,32,384]{2,1,0:T(8,128)S(1)} %own.2.own_ref, bf16[3,32,384]{2,1,0:T(8,128)(2,1)S(1)} %collective-permute-done.7.refs_0_, ...), custom_call_target="tpu_custom_call", output_to_operand_aliasing={{}: (4, {})} | custom-call | tf_op jit(solution)/shard_map/finish/pallas_call | solution.py:271
  (7 shorter events, 0.1 us)
Async XLA Ops:
  0.0 7.6 %copy-start = (f32[384,64]{0,1:T(8,128)S(1)}, f32[384,64]{0,1:T(8,128)}, u32[]{:S(2)}) copy-start(f32[384,64]{0,1:T(8,128)} %param.9) | copy-start | bytes 294916
  0.0 7.6 %copy-start.1 = (s32[8]{0:T(128)S(1)}, s32[8]{0:T(128)}, u32[]{:S(2)}) copy-start(s32[8]{0:T(128)} %widths_ref.1) | copy-start | bytes 100
  2.8 1.5 %collective-permute-start.1 = (bf16[16,3072]{1,0:T(8,128)(2,1)S(1)}, bf16[16,3072]{1,0:T(8,128)(2,1)S(1)}, u32[]{:S(2)}, u32[]{:S(2)}) collective-permute-start(bf16[16,3072]{1,0:T(8,128)(2,1)S(1)} %get-tuple-element.24), channel_id=1, source_target_pairs={{0,1},{1,0},{2,3},{3,2},{4,5},{5,4},{6,7},{7,6},{8,9},{9,8},{10,11... | collective-permute-start | bytes 294920 | tf_op jit(solution)/shard_map/ppermute | solution.py:204
  3.3 5.1 %collective-permute-start = (bf16[16,3072]{1,0:T(8,128)(2,1)S(1)}, bf16[16,3072]{1,0:T(8,128)(2,1)S(1)}, u32[]{:S(2)}, u32[]{:S(2)}) collective-permute-start(bf16[16,3072]{1,0:T(8,128)(2,1)S(1)} %get-tuple-element.22), channel_id=1, source_target_pairs={{0,1},{1,0},{2,3},{3,2},{4,5},{5,4},{6,7},{7,6},{8,9},{9,8},{10,11... | collective-permute-start | bytes 294920 | tf_op jit(solution)/shard_map/ppermute | solution.py:204
  4.3 5.0 %collective-permute-start.2 = (bf16[16,3072]{1,0:T(8,128)(2,1)S(1)}, bf16[16,3072]{1,0:T(8,128)(2,1)S(1)}, u32[]{:S(2)}, u32[]{:S(2)}) collective-permute-start(bf16[16,3072]{1,0:T(8,128)(2,1)S(1)} %add_convert_fusion.1), channel_id=1, source_target_pairs={{0,3},{1,4},{2,7},{3,0},{4,1},{5,6},{6,5},{7,2},{8,13},{9,10},{10,... | collective-permute-start | bytes 294920 | tf_op jit(solution)/shard_map/ppermute | solution.py:204
  9.3 5.2 %collective-permute-start.3 = (bf16[16,3072]{1,0:T(8,128)(2,1)S(1)}, bf16[16,3072]{1,0:T(8,128)(2,1)S(1)}, u32[]{:S(2)}, u32[]{:S(2)}) collective-permute-start(bf16[16,3072]{1,0:T(8,128)(2,1)S(1)} %convert_element_type.31), channel_id=1, source_target_pairs={{0,9},{1,2},{2,1},{3,10},{4,7},{5,12},{6,15},{7,4},{8,11},{9,0},{1... | collective-permute-start | bytes 294920 | tf_op jit(solution)/shard_map/ppermute | solution.py:204
  14.6 4.9 %collective-permute-start.4 = (bf16[16,3072]{1,0:T(8,128)(2,1)S(1)}, bf16[16,3072]{1,0:T(8,128)(2,1)S(1)}, u32[]{:S(2)}, u32[]{:S(2)}) collective-permute-start(bf16[16,3072]{1,0:T(8,128)(2,1)S(1)} %convert_element_type.33), channel_id=1, source_target_pairs={{0,5},{1,8},{2,11},{3,6},{4,13},{5,0},{6,3},{7,14},{8,1},{9,12},{1... | collective-permute-start | bytes 294920 | tf_op jit(solution)/shard_map/ppermute | solution.py:204
  19.5 2.3 %collective-permute-start.8 = (bf16[16,3072]{1,0:T(8,128)(2,1)S(1)}, bf16[16,3072]{1,0:T(8,128)(2,1)S(1)}, u32[]{:S(2)}, u32[]{:S(2)}) collective-permute-start(bf16[16,3072]{1,0:T(8,128)(2,1)S(1)} %add_convert_fusion.refs_0_), channel_id=1, source_target_pairs={{0,1},{1,0},{2,3},{3,2},{4,5},{5,4},{6,7},{7,6},{8,9},{9,8},{10,11... | collective-permute-start | bytes 294920 | tf_op jit(solution)/shard_map/ppermute | solution.py:204
  20.4 4.6 %collective-permute-start.6 = (bf16[16,3072]{1,0:T(8,128)(2,1)S(1)}, bf16[16,3072]{1,0:T(8,128)(2,1)S(1)}, u32[]{:S(2)}, u32[]{:S(2)}) collective-permute-start(bf16[16,3072]{1,0:T(8,128)(2,1)S(1)} %add_convert_fusion.refs_0_), channel_id=1, source_target_pairs={{0,2},{1,5},{2,6},{3,1},{4,0},{5,7},{6,4},{7,3},{8,12},{9,11},{10,... | collective-permute-start | bytes 294920 | tf_op jit(solution)/shard_map/ppermute | solution.py:204
  21.8 4.0 %collective-permute-start.5 = (bf16[16,3072]{1,0:T(8,128)(2,1)S(1)}, bf16[16,3072]{1,0:T(8,128)(2,1)S(1)}, u32[]{:S(2)}, u32[]{:S(2)}) collective-permute-start(bf16[16,3072]{1,0:T(8,128)(2,1)S(1)} %add_convert_fusion.refs_0_), channel_id=1, source_target_pairs={{0,3},{1,4},{2,7},{3,0},{4,1},{5,6},{6,5},{7,2},{8,13},{9,10},{10,... | collective-permute-start | bytes 294920 | tf_op jit(solution)/shard_map/ppermute | solution.py:204
  22.4 6.2 %collective-permute-start.9 = (bf16[3,32,384]{2,1,0:T(8,128)(2,1)S(1)}, bf16[3,32,384]{2,1,0:T(8,128)(2,1)S(1)}, u32[]{:S(2)}, u32[]{:S(2)}) collective-permute-start(bf16[3,32,384]{2,1,0:T(8,128)(2,1)S(1)} %others.3), channel_id=1, source_target_pairs={{0,16},{16,0},{1,17},{17,1},{2,18},{18,2},{3,19},{19,3},{4,20},{20... | collective-permute-start | bytes 221192 | tf_op jit(solution)/shard_map/ppermute | solution.py:242
  26.4 4.5 %collective-permute-start.7 = (bf16[3,32,384]{2,1,0:T(8,128)(2,1)S(1)}, bf16[3,32,384]{2,1,0:T(8,128)(2,1)S(1)}, u32[]{:S(2)}, u32[]{:S(2)}) collective-permute-start(bf16[3,32,384]{2,1,0:T(8,128)(2,1)S(1)} %others.2), channel_id=1, source_target_pairs={{0,16},{16,0},{1,17},{17,1},{2,18},{18,2},{3,19},{19,3},{4,20},{20... | collective-permute-start | bytes 221192 | tf_op jit(solution)/shard_map/ppermute | solution.py:242

commit v8 on v6

--- a/solution.py
+++ b/solution.py
@@ -112,7 +112,7 @@
 
 
 def section_kernel(near, outside_ref, turned_ref, *refs):
-    pieces, got_ref, out_ref = refs[:2], refs[2], refs[-1]
+    pieces, got_ref, out_ref = (refs[:-2] if near else refs[:-1]), refs[-2], refs[-1]
     count = outside_ref.shape[0]
     spread = [p[...] for p in pieces] if out_ref.shape[0] > count else []
     spread += [p[...] * outside_ref[c] for c in range(count) for p in pieces]
@@ -126,8 +126,14 @@
         out_ref[c] = product[c] + got_ref[received(c, 2 * count, near, side)].astype(jnp.float32)
 
 
-def finish_kernel(near, inverse_ref, ridged_ref, *refs):
-    head_ref, tail_ref, got_ref, out_ref = refs
+def join_kernel(near, own_ref, got_ref, out_ref):
+    count = own_ref.shape[0]
+    side = lax.axis_index("chrom")
+    for c in range(count):
+        out_ref[c] = own_ref[c] + got_ref[received(c, 2 * count, near, side)].astype(jnp.float32)
+
+
+def finish_kernel(near, inverse_ref, ridged_ref, head_ref, tail_ref, got_ref, out_ref):
     per_device, rhs, _ = out_ref.shape
     side = lax.axis_index("chrom")
     places = [received(c, 2 * per_device, near, side) if near else c for c in range(per_device)]
@@ -135,12 +141,11 @@
     for p, row in enumerate(piece_rows(rhs)):
         at = pl.ds(pl.multiple_of(row, quarter), quarter)
         ridged = ridged_ref[pl.ds(p * quarter, quarter), :]
-        here = pl.ds((p % 2) * quarter, quarter)
         for c in range(per_device):
-            if p < 2:
-                rest = head_ref[c, here, :]
+            if p == 2:
+                rest = tail_ref[c] + got_ref[places[c]].astype(jnp.float32)
             else:
-                rest = tail_ref[c, here, :] + got_ref[places[c], here, :].astype(jnp.float32)
+                rest = head_ref[c, pl.ds(min(p, 2) * quarter, quarter), :]
             out_ref[c, at, :] = ridged + rest * inverse_ref[c]
 
 
@@ -153,6 +158,7 @@
     half, quarter = rhs // 2, rhs // 4
     vmem = pl.BlockSpec(memory_space=pltpu.VMEM)
     smem = pl.BlockSpec(memory_space=pltpu.SMEM)
+    anywhere = pl.BlockSpec(memory_space=pl.ANY)
     params = pltpu.CompilerParams(vmem_limit_bytes=VMEM_LIMIT)
     dir_t = direction.T
 
@@ -177,7 +183,7 @@
         name="cross",
     )(*(pltpu.with_memory_space_constraint(a, pltpu.HBM) for a in operands))
 
-    near = max(1, sections // 4)
+    near = max(1, sections // 2 - 2)
     mask = lambda count: jax.ShapeDtypeStruct((count, quarter, variants), jnp.bfloat16)
     outside_others, outside_own, inverse, ridged = pl.pallas_call(
         functools.partial(prepare_kernel, variants * n_chrom),
@@ -221,8 +227,8 @@
     def products(outside, pieces, count, dtype, name, *got):
         return pl.pallas_call(
             functools.partial(section_kernel, near if got else 0),
-            out_shape=jax.ShapeDtypeStruct((count, half, rows), dtype),
-            in_specs=[vmem] * (4 + len(got)),
+            out_shape=jax.ShapeDtypeStruct((count, len(pieces) * quarter, rows), dtype),
+            in_specs=[vmem] * (2 + len(pieces) + len(got)),
             out_specs=vmem,
             compiler_params=params,
             cost_estimate=pl.CostEstimate(
@@ -236,13 +242,23 @@
 
     bit = n_chrom // 2
     for_others = lambda pieces: products(outside_others, pieces, near + 1, jnp.bfloat16, "others")
-    head = (first, swap(first, 1, 1))
+    late = (second, second_sibling)
+    head = (first, swap(first, 1, 1), late[1])
     products_head = for_others(head)
-    tail = (second, second_sibling)
+    tail = (late[0],)
     gots = [swap_chrom(products_head, bit), swap_chrom(for_others(tail), bit)]
     for_own = lambda pieces, *got: products(outside_own, pieces, sections // 2, jnp.float32, "own", *got)
     if n_chrom == 2:
-        owns = [for_own(head, gots[0]), for_own(tail)]
+        own_head = for_own(head)
+        own_head = pl.pallas_call(
+            functools.partial(join_kernel, near),
+            out_shape=jax.ShapeDtypeStruct(own_head.shape, jnp.float32),
+            in_specs=[vmem] * 2,
+            out_specs=vmem,
+            compiler_params=params,
+            name="join",
+        )(own_head, gots[0])
+        owns = [own_head, for_own(tail)]
     else:
         owns = [for_own(head), for_own(tail)]
         side = (lax.axis_index("chrom") // bit) % 2

time: 31.9 us -> 31.8 us (level)
    ppermute x8, starting transfers between devices: 10.4 us -> 11.5 us  [swap(): lax.ppermute(x, 'samp', [(i, i ^ (high if i.bit_count() % 2 else low)) fo...]
    ppermute x2, starting transfers between devices: 3.26 us -> 2.16 us  [swap_chrom(): return lax.ppermute(x, 'chrom', [(i, i ^ bit) for i in range(n_chrom)])]
    ppermute x8, waiting for transfers between devices: 8.09 us -> 7.6 us  [swap(): lax.ppermute(x, 'samp', [(i, i ^ (high if i.bit_count() % 2 else low)) fo...]
where the time goes in v8:
time: 31.8 us; the launch traced here: 31.6 us
  starting transfers between devices  13.7 us (43%)
  waiting for transfers between devices  9.67 us (30%)
  Pallas kernels  7.44 us (23%)
  between operations  0.76 us (2%)
    ppermute x8, starting transfers between devices, swap(): lax.ppermute(x, 'samp', [(i, i ^ (high if i.bit_count() % 2 else low)) fo...  11.5 us
    ppermute x8, waiting for transfers between devices, swap(): lax.ppermute(x, 'samp', [(i, i ^ (high if i.bit_count() % 2 else low)) fo...  7.6 us
    pallas_call x1, Pallas kernels, on_device(): pl.pallas_call(functools.partial(cross_kernel, blocks), out_shape=(jax.Sh...  2.79 us
    pallas_call x4, Pallas kernels, products(): pl.pallas_call(functools.partial(section_kernel, near if got else 0), out...  2.37 us
    ppermute x2, starting transfers between devices, swap_chrom(): return lax.ppermute(x, 'chrom', [(i, i ^ bit) for i in range(n_chrom)])  2.16 us
    ppermute x2, waiting for transfers between devices, swap_chrom(): return lax.ppermute(x, 'chrom', [(i, i ^ bit) for i in range(n_chrom)])  2.07 us
    pallas_call x1, Pallas kernels, on_device(): pl.pallas_call(functools.partial(finish_kernel, near if n_chrom == 2 else...  0.82 us
    pallas_call x1, Pallas kernels, on_device(): pl.pallas_call(functools.partial(prepare_kernel, variants * n_chrom), out...  0.77 us
  transfers between devices with their start and end apart: 10, of which 7 were waited for; matrix products, arithmetic and copies ran while one was open for 0% of the time, Pallas kernels for 12%

profile of v8, /device:TPU:0, one launch (start us, length us, event | category | flops | bytes accessed | tf_op | source)
XLA Modules:
  0.0 31.6 jit_solution(13955058251561089605)
XLA Ops:
  0.0 0.0 copy-start
  0.0 0.0 copy-start.1
  0.0 2.8 %cross.1 = (bf16[384,3072]{1,0:T(8,128)(2,1)S(1)}, bf16[16,3072]{1,0:T(8,128)(2,1)S(1)}, bf16[16,3072]{1,0:T(8,128)(2,1)S(1)}, f32[16,3072]{1,0:T(8,128)S(1)}, f32[16,3072]{1,0:T(8,128)S(1)}) custom-call(s32[384,3072]{1,0:T(8,128)} %geno_hbm.1, f32[1,3072]{1,0:T(1,128)} %bitcast.5, f32[64,384]{1,0:T(8,128)} %bitcast.3), custom_call_target="tpu_custom_call" | custom-call | tf_op jit(solution)/shard_map/cross/pallas_call | solution.py:168
  2.8 0.5 %collective-permute-start.1 = (bf16[16,3072]{1,0:T(8,128)(2,1)S(1)}, bf16[16,3072]{1,0:T(8,128)(2,1)S(1)}, u32[]{:S(2)}, u32[]{:S(2)}) collective-permute-start(bf16[16,3072]{1,0:T(8,128)(2,1)S(1)} %get-tuple-element.24), channel_id=1, source_target_pairs={{0,1},{1,0},{2,3},{3,2},{4,5},{5,4},{6,7},{7,6},{8,9},{9,8},{10,11... | collective-permute-start | bytes 294920 | tf_op jit(solution)/shard_map/ppermute | solution.py:203
  3.3 0.1 collective-permute-start
  3.4 0.9 %collective-permute-done.1 = bf16[16,3072]{1,0:T(8,128)(2,1)S(1)} collective-permute-done((bf16[16,3072]{1,0:T(8,128)(2,1)S(1)}, bf16[16,3072]{1,0:T(8,128)(2,1)S(1)}, u32[]{:S(2)}, u32[]{:S(2)}) %collective-permute-start.1) | collective-permute-done | bytes 98336 | tf_op jit(solution)/shard_map/ppermute | solution.py:203
  4.3 2.7 %collective-permute-start.2 = (bf16[16,3072]{1,0:T(8,128)(2,1)S(1)}, bf16[16,3072]{1,0:T(8,128)(2,1)S(1)}, u32[]{:S(2)}, u32[]{:S(2)}) collective-permute-start(bf16[16,3072]{1,0:T(8,128)(2,1)S(1)} %add_convert_fusion.1), channel_id=1, source_target_pairs={{0,3},{1,4},{2,7},{3,0},{4,1},{5,6},{6,5},{7,2},{8,13},{9,10},{10,... | collective-permute-start | bytes 294920 | tf_op jit(solution)/shard_map/ppermute | solution.py:203
  7.6 0.0 copy-done
  7.6 0.0 copy-done.1
  7.7 0.8 %prepare.1 = (bf16[2,16,3072]{2,1,0:T(8,128)(2,1)S(1)}, bf16[4,16,3072]{2,1,0:T(8,128)(2,1)S(1)}, f32[4,16,384]{2,1,0:T(8,128)S(1)}, f32[64,384]{1,0:T(8,128)S(1)}) custom-call(s32[8]{0:T(128)S(1)} %copy-done.1, f32[1]{0:T(128)S(6)} %copy.6.ridge_ref, f32[64,384]{1,0:T(8,128)S(1)} %bitcast.4), custom_call_target="tpu_custom_call" | custom-call | tf_op jit(solution)/shard_map/prepare/pallas_call | solution.py:188
  8.4 0.0 collective-permute-done
  8.4 0.8 %collective-permute-done.2 = bf16[16,3072]{1,0:T(8,128)(2,1)S(1)} collective-permute-done((bf16[16,3072]{1,0:T(8,128)(2,1)S(1)}, bf16[16,3072]{1,0:T(8,128)(2,1)S(1)}, u32[]{:S(2)}, u32[]{:S(2)}) %collective-permute-start.2) | collective-permute-done | bytes 98336 | tf_op jit(solution)/shard_map/ppermute | solution.py:203
  9.3 2.9 %collective-permute-start.3 = (bf16[16,3072]{1,0:T(8,128)(2,1)S(1)}, bf16[16,3072]{1,0:T(8,128)(2,1)S(1)}, u32[]{:S(2)}, u32[]{:S(2)}) collective-permute-start(bf16[16,3072]{1,0:T(8,128)(2,1)S(1)} %convert_element_type.31), channel_id=1, source_target_pairs={{0,9},{1,2},{2,1},{3,10},{4,7},{5,12},{6,15},{7,4},{8,11},{9,0},{1... | collective-permute-start | bytes 294920 | tf_op jit(solution)/shard_map/ppermute | solution.py:203
  12.2 0.7 %turn.1.turned_ref = bf16[3072,384]{1,0:T(8,128)(2,1)S(1)} custom-call(bf16[384,3072]{1,0:T(8,128)(2,1)S(1)} %get-tuple-element.33.stand_ref), custom_call_target="tpu_custom_call" | custom-call | tf_op jit(solution)/shard_map/turn/pallas_call | solution.py:212
  12.9 1.6 %collective-permute-done.3 = bf16[16,3072]{1,0:T(8,128)(2,1)S(1)} collective-permute-done((bf16[16,3072]{1,0:T(8,128)(2,1)S(1)}, bf16[16,3072]{1,0:T(8,128)(2,1)S(1)}, u32[]{:S(2)}, u32[]{:S(2)}) %collective-permute-start.3) | collective-permute-done | bytes 98336 | tf_op jit(solution)/shard_map/ppermute | solution.py:203
  14.6 1.9 %collective-permute-start.4 = (bf16[16,3072]{1,0:T(8,128)(2,1)S(1)}, bf16[16,3072]{1,0:T(8,128)(2,1)S(1)}, u32[]{:S(2)}, u32[]{:S(2)}) collective-permute-start(bf16[16,3072]{1,0:T(8,128)(2,1)S(1)} %convert_element_type.33), channel_id=1, source_target_pairs={{0,5},{1,8},{2,11},{3,6},{4,13},{5,0},{6,3},{7,14},{8,1},{9,12},{1... | collective-permute-start | bytes 294920 | tf_op jit(solution)/shard_map/ppermute | solution.py:203
  16.5 3.0 %collective-permute-done.4 = bf16[16,3072]{1,0:T(8,128)(2,1)S(1)} collective-permute-done((bf16[16,3072]{1,0:T(8,128)(2,1)S(1)}, bf16[16,3072]{1,0:T(8,128)(2,1)S(1)}, u32[]{:S(2)}, u32[]{:S(2)}) %collective-permute-start.4) | collective-permute-done | bytes 98336 | tf_op jit(solution)/shard_map/ppermute | solution.py:203
  19.5 1.4 %collective-permute-start.6 = (bf16[16,3072]{1,0:T(8,128)(2,1)S(1)}, bf16[16,3072]{1,0:T(8,128)(2,1)S(1)}, u32[]{:S(2)}, u32[]{:S(2)}) collective-permute-start(bf16[16,3072]{1,0:T(8,128)(2,1)S(1)} %add_convert_fusion.refs_0_), channel_id=1, source_target_pairs={{0,2},{1,5},{2,6},{3,1},{4,0},{5,7},{6,4},{7,3},{8,12},{9,11},{10,... | collective-permute-start | bytes 294920 | tf_op jit(solution)/shard_map/ppermute | solution.py:203
  20.8 0.5 %collective-permute-start.5 = (bf16[16,3072]{1,0:T(8,128)(2,1)S(1)}, bf16[16,3072]{1,0:T(8,128)(2,1)S(1)}, u32[]{:S(2)}, u32[]{:S(2)}) collective-permute-start(bf16[16,3072]{1,0:T(8,128)(2,1)S(1)} %add_convert_fusion.refs_0_), channel_id=1, source_target_pairs={{0,1},{1,0},{2,3},{3,2},{4,5},{5,4},{6,7},{7,6},{8,9},{9,8},{10,11... | collective-permute-start | bytes 294920 | tf_op jit(solution)/shard_map/ppermute | solution.py:203
  21.3 1.6 %collective-permute-start.8 = (bf16[16,3072]{1,0:T(8,128)(2,1)S(1)}, bf16[16,3072]{1,0:T(8,128)(2,1)S(1)}, u32[]{:S(2)}, u32[]{:S(2)}) collective-permute-start(bf16[16,3072]{1,0:T(8,128)(2,1)S(1)} %add_convert_fusion.refs_0_), channel_id=1, source_target_pairs={{0,3},{1,4},{2,7},{3,0},{4,1},{5,6},{6,5},{7,2},{8,13},{9,10},{10,... | collective-permute-start | bytes 294920 | tf_op jit(solution)/shard_map/ppermute | solution.py:203
  22.9 1.3 %collective-permute-done.6.refs_2_ = bf16[16,3072]{1,0:T(8,128)(2,1)S(1)} collective-permute-done((bf16[16,3072]{1,0:T(8,128)(2,1)S(1)}, bf16[16,3072]{1,0:T(8,128)(2,1)S(1)}, u32[]{:S(2)}, u32[]{:S(2)}) %collective-permute-start.6) | collective-permute-done | bytes 98336 | tf_op jit(solution)/shard_map/ppermute | solution.py:203
  24.2 0.0 collective-permute-done.5.refs_1_
  24.2 0.6 %others.2 = bf16[3,48,384]{2,1,0:T(8,128)(2,1)S(1)} custom-call(bf16[2,16,3072]{2,1,0:T(8,128)(2,1)S(1)} %get-tuple-element.36.outside_ref, bf16[3072,384]{1,0:T(8,128)(2,1)S(1)} %turn.1.turned_ref, bf16[16,3072]{1,0:T(8,128)(2,1)S(1)} %add_convert_fusion.refs_0_, bf16[16,3072]{1,0:T(8,128)(2,1)S(1)} %collective-permute-done.5.refs_1_, ...), custom_call_target="tpu_custom_call" | custom-call | flops 301989888 | bytes 2359296 | tf_op jit(solution)/shard_map/others/pallas_call | solution.py:228
  24.8 1.5 %collective-permute-start.7 = (bf16[3,48,384]{2,1,0:T(8,128)(2,1)S(1)}, bf16[3,48,384]{2,1,0:T(8,128)(2,1)S(1)}, u32[]{:S(2)}, u32[]{:S(2)}) collective-permute-start(bf16[3,48,384]{2,1,0:T(8,128)(2,1)S(1)} %others.2), channel_id=1, source_target_pairs={{0,16},{16,0},{1,17},{17,1},{2,18},{18,2},{3,19},{19,3},{4,20},{20... | collective-permute-start | bytes 331784 | tf_op jit(solution)/shard_map/ppermute | solution.py:241
  26.3 0.0 collective-permute-done.8.refs_0_
  26.3 0.5 %others.3 = bf16[3,16,384]{2,1,0:T(8,128)(2,1)S(1)} custom-call(bf16[2,16,3072]{2,1,0:T(8,128)(2,1)S(1)} %get-tuple-element.36.outside_ref, bf16[3072,384]{1,0:T(8,128)(2,1)S(1)} %turn.1.turned_ref, bf16[16,3072]{1,0:T(8,128)(2,1)S(1)} %collective-permute-done.8.refs_0_), custom_call_target="tpu_custom_call" | custom-call | flops 301989888 | bytes 2359296 | tf_op jit(solution)/shard_map/others/pallas_call | solution.py:228
  26.8 0.6 %collective-permute-start.9 = (bf16[3,16,384]{2,1,0:T(8,128)(2,1)S(1)}, bf16[3,16,384]{2,1,0:T(8,128)(2,1)S(1)}, u32[]{:S(2)}, u32[]{:S(2)}) collective-permute-start(bf16[3,16,384]{2,1,0:T(8,128)(2,1)S(1)} %others.3), channel_id=1, source_target_pairs={{0,16},{16,0},{1,17},{17,1},{2,18},{18,2},{3,19},{19,3},{4,20},{20... | collective-permute-start | bytes 110600 | tf_op jit(solution)/shard_map/ppermute | solution.py:241
  27.4 0.5 %own.3.tail_ref = f32[4,16,384]{2,1,0:T(8,128)S(1)} custom-call(bf16[4,16,3072]{2,1,0:T(8,128)(2,1)S(1)} %get-tuple-element.31.outside_ref, bf16[3072,384]{1,0:T(8,128)(2,1)S(1)} %turn.1.turned_ref, bf16[16,3072]{1,0:T(8,128)(2,1)S(1)} %collective-permute-done.8.refs_0_), custom_call_target="tpu_custom_call" | custom-call | flops 301989888 | bytes 2359296 | tf_op jit(solution)/shard_map/own/pallas_call | solution.py:228
  27.9 0.8 %own.2.own_ref = f32[4,48,384]{2,1,0:T(8,128)S(1)} custom-call(bf16[4,16,3072]{2,1,0:T(8,128)(2,1)S(1)} %get-tuple-element.31.outside_ref, bf16[3072,384]{1,0:T(8,128)(2,1)S(1)} %turn.1.turned_ref, bf16[16,3072]{1,0:T(8,128)(2,1)S(1)} %add_convert_fusion.refs_0_, bf16[16,3072]{1,0:T(8,128)(2,1)S(1)} %collective-permute-done.5.refs_1_, ...), custom_call_target="tpu_custom_call" | custom-call | flops 301989888 | bytes 2359296 | tf_op jit(solution)/shard_map/own/pallas_call | solution.py:228
  28.7 1.4 %collective-permute-done.7.got_ref = bf16[3,48,384]{2,1,0:T(8,128)(2,1)S(1)} collective-permute-done((bf16[3,48,384]{2,1,0:T(8,128)(2,1)S(1)}, bf16[3,48,384]{2,1,0:T(8,128)(2,1)S(1)}, u32[]{:S(2)}, u32[]{:S(2)}) %collective-permute-start.7) | collective-permute-done | bytes 110624 | tf_op jit(solution)/shard_map/ppermute | solution.py:241
  30.2 0.6 %collective-permute-done.9.got_ref = bf16[3,16,384]{2,1,0:T(8,128)(2,1)S(1)} collective-permute-done((bf16[3,16,384]{2,1,0:T(8,128)(2,1)S(1)}, bf16[3,16,384]{2,1,0:T(8,128)(2,1)S(1)}, u32[]{:S(2)}, u32[]{:S(2)}) %collective-permute-start.9) | collective-permute-done | bytes 36896 | tf_op jit(solution)/shard_map/ppermute | solution.py:241
  30.8 0.8 %finish.1 = f32[4,64,384]{2,1,0:T(8,128)} custom-call(f32[4,16,384]{2,1,0:T(8,128)S(1)} %get-tuple-element.29.inverse_ref, f32[64,384]{1,0:T(8,128)S(1)} %get-tuple-element.30.ridged_ref, f32[4,48,384]{2,1,0:T(8,128)S(1)} %join.1.head_ref, f32[4,16,384]{2,1,0:T(8,128)S(1)} %own.3.tail_ref, bf16[3,16,384]{2,1,0:T(8,128)(2,1)S(1)} %collective-permute-done.9.got_ref), custom_call_target="tpu_custom_call" | custom-call | tf_op jit(solution)/shard_map/finish/pallas_call | solution.py:279
  (7 shorter events, 0.1 us)
Async XLA Ops:
  0.0 7.6 %copy-start = (f32[384,64]{0,1:T(8,128)S(1)}, f32[384,64]{0,1:T(8,128)}, u32[]{:S(2)}) copy-start(f32[384,64]{0,1:T(8,128)} %param.9) | copy-start | bytes 294916
  0.0 7.6 %copy-start.1 = (s32[8]{0:T(128)S(1)}, s32[8]{0:T(128)}, u32[]{:S(2)}) copy-start(s32[8]{0:T(128)} %widths_ref.1) | copy-start | bytes 100
  2.8 1.5 %collective-permute-start.1 = (bf16[16,3072]{1,0:T(8,128)(2,1)S(1)}, bf16[16,3072]{1,0:T(8,128)(2,1)S(1)}, u32[]{:S(2)}, u32[]{:S(2)}) collective-permute-start(bf16[16,3072]{1,0:T(8,128)(2,1)S(1)} %get-tuple-element.24), channel_id=1, source_target_pairs={{0,1},{1,0},{2,3},{3,2},{4,5},{5,4},{6,7},{7,6},{8,9},{9,8},{10,11... | collective-permute-start | bytes 294920 | tf_op jit(solution)/shard_map/ppermute | solution.py:203
  3.3 5.1 %collective-permute-start = (bf16[16,3072]{1,0:T(8,128)(2,1)S(1)}, bf16[16,3072]{1,0:T(8,128)(2,1)S(1)}, u32[]{:S(2)}, u32[]{:S(2)}) collective-permute-start(bf16[16,3072]{1,0:T(8,128)(2,1)S(1)} %get-tuple-element.22), channel_id=1, source_target_pairs={{0,1},{1,0},{2,3},{3,2},{4,5},{5,4},{6,7},{7,6},{8,9},{9,8},{10,11... | collective-permute-start | bytes 294920 | tf_op jit(solution)/shard_map/ppermute | solution.py:203
  4.3 5.0 %collective-permute-start.2 = (bf16[16,3072]{1,0:T(8,128)(2,1)S(1)}, bf16[16,3072]{1,0:T(8,128)(2,1)S(1)}, u32[]{:S(2)}, u32[]{:S(2)}) collective-permute-start(bf16[16,3072]{1,0:T(8,128)(2,1)S(1)} %add_convert_fusion.1), channel_id=1, source_target_pairs={{0,3},{1,4},{2,7},{3,0},{4,1},{5,6},{6,5},{7,2},{8,13},{9,10},{10,... | collective-permute-start | bytes 294920 | tf_op jit(solution)/shard_map/ppermute | solution.py:203
  9.3 5.2 %collective-permute-start.3 = (bf16[16,3072]{1,0:T(8,128)(2,1)S(1)}, bf16[16,3072]{1,0:T(8,128)(2,1)S(1)}, u32[]{:S(2)}, u32[]{:S(2)}) collective-permute-start(bf16[16,3072]{1,0:T(8,128)(2,1)S(1)} %convert_element_type.31), channel_id=1, source_target_pairs={{0,9},{1,2},{2,1},{3,10},{4,7},{5,12},{6,15},{7,4},{8,11},{9,0},{1... | collective-permute-start | bytes 294920 | tf_op jit(solution)/shard_map/ppermute | solution.py:203
  14.6 4.9 %collective-permute-start.4 = (bf16[16,3072]{1,0:T(8,128)(2,1)S(1)}, bf16[16,3072]{1,0:T(8,128)(2,1)S(1)}, u32[]{:S(2)}, u32[]{:S(2)}) collective-permute-start(bf16[16,3072]{1,0:T(8,128)(2,1)S(1)} %convert_element_type.33), channel_id=1, source_target_pairs={{0,5},{1,8},{2,11},{3,6},{4,13},{5,0},{6,3},{7,14},{8,1},{9,12},{1... | collective-permute-start | bytes 294920 | tf_op jit(solution)/shard_map/ppermute | solution.py:203
  19.5 4.7 %collective-permute-start.6 = (bf16[16,3072]{1,0:T(8,128)(2,1)S(1)}, bf16[16,3072]{1,0:T(8,128)(2,1)S(1)}, u32[]{:S(2)}, u32[]{:S(2)}) collective-permute-start(bf16[16,3072]{1,0:T(8,128)(2,1)S(1)} %add_convert_fusion.refs_0_), channel_id=1, source_target_pairs={{0,2},{1,5},{2,6},{3,1},{4,0},{5,7},{6,4},{7,3},{8,12},{9,11},{10,... | collective-permute-start | bytes 294920 | tf_op jit(solution)/shard_map/ppermute | solution.py:203
  20.8 3.3 %collective-permute-start.5 = (bf16[16,3072]{1,0:T(8,128)(2,1)S(1)}, bf16[16,3072]{1,0:T(8,128)(2,1)S(1)}, u32[]{:S(2)}, u32[]{:S(2)}) collective-permute-start(bf16[16,3072]{1,0:T(8,128)(2,1)S(1)} %add_convert_fusion.refs_0_), channel_id=1, source_target_pairs={{0,1},{1,0},{2,3},{3,2},{4,5},{5,4},{6,7},{7,6},{8,9},{9,8},{10,11... | collective-permute-start | bytes 294920 | tf_op jit(solution)/shard_map/ppermute | solution.py:203
  21.3 5.0 %collective-permute-start.8 = (bf16[16,3072]{1,0:T(8,128)(2,1)S(1)}, bf16[16,3072]{1,0:T(8,128)(2,1)S(1)}, u32[]{:S(2)}, u32[]{:S(2)}) collective-permute-start(bf16[16,3072]{1,0:T(8,128)(2,1)S(1)} %add_convert_fusion.refs_0_), channel_id=1, source_target_pairs={{0,3},{1,4},{2,7},{3,0},{4,1},{5,6},{6,5},{7,2},{8,13},{9,10},{10,... | collective-permute-start | bytes 294920 | tf_op jit(solution)/shard_map/ppermute | solution.py:203
  24.8 5.4 %collective-permute-start.7 = (bf16[3,48,384]{2,1,0:T(8,128)(2,1)S(1)}, bf16[3,48,384]{2,1,0:T(8,128)(2,1)S(1)}, u32[]{:S(2)}, u32[]{:S(2)}) collective-permute-start(bf16[3,48,384]{2,1,0:T(8,128)(2,1)S(1)} %others.2), channel_id=1, source_target_pairs={{0,16},{16,0},{1,17},{17,1},{2,18},{18,2},{3,19},{19,3},{4,20},{20... | collective-permute-start | bytes 331784 | tf_op jit(solution)/shard_map/ppermute | solution.py:241
  26.8 4.0 %collective-permute-start.9 = (bf16[3,16,384]{2,1,0:T(8,128)(2,1)S(1)}, bf16[3,16,384]{2,1,0:T(8,128)(2,1)S(1)}, u32[]{:S(2)}, u32[]{:S(2)}) collective-permute-start(bf16[3,16,384]{2,1,0:T(8,128)(2,1)S(1)} %others.3), channel_id=1, source_target_pairs={{0,16},{16,0},{1,17},{17,1},{2,18},{18,2},{3,19},{19,3},{4,20},{20... | collective-permute-start | bytes 110600 | tf_op jit(solution)/shard_map/ppermute | solution.py:241

commit v9 on v7

--- a/solution.py
+++ b/solution.py
@@ -112,7 +112,7 @@
 
 
 def section_kernel(near, outside_ref, turned_ref, *refs):
-    pieces, got_ref, out_ref = refs[:2], refs[2], refs[-1]
+    pieces, got_ref, out_ref = (refs[:-2] if near else refs[:-1]), refs[-2], refs[-1]
     count = outside_ref.shape[0]
     spread = [p[...] for p in pieces] if out_ref.shape[0] > count else []
     spread += [p[...] * outside_ref[c] for c in range(count) for p in pieces]
@@ -126,22 +126,20 @@
         out_ref[c] = product[c] + got_ref[received(c, 2 * count, near, side)].astype(jnp.float32)
 
 
-def finish_kernel(near, group, inverse_ref, ridged_ref, own_ref, *refs):
+def finish_kernel(near, group, inverse_ref, ridged_ref, own_ref, got_ref, *refs):
     out_hbm, done, sems = refs[-3:]
-    got = refs[:-3]
     per_device, rhs, _ = out_hbm.shape
     side = lax.axis_index("chrom")
     places = [received(c, 2 * per_device, near, side) if near else c for c in range(per_device)]
     quarter = rhs // 4
-    rows = piece_rows(rhs)[2 * group : 2 * group + 2]
+    own_pieces = ((0, 1, 3), (2,))[group]
     copies = []
-    for p, row in enumerate(rows):
+    for p, piece in enumerate(own_pieces):
+        row = piece_rows(rhs)[piece]
         here = pl.ds(p * quarter, quarter)
-        ridged = ridged_ref[pl.ds((2 * group + p) * quarter, quarter), :]
+        ridged = ridged_ref[pl.ds(piece * quarter, quarter), :]
         for c in range(per_device):
-            rest = own_ref[c, here, :]
-            if group == 1:
-                rest = rest + got[0][places[c], here, :].astype(jnp.float32)
+            rest = own_ref[c, here, :] + got_ref[places[c], here, :].astype(jnp.float32)
             done[p, c] = ridged + rest * inverse_ref[c]
         to = out_hbm.at[:, pl.ds(pl.multiple_of(row, quarter), quarter), :]
         copies.append(pltpu.make_async_copy(done.at[p], to, sems.at[p]))
@@ -228,8 +226,8 @@
     def products(outside, pieces, count, dtype, name, *got):
         return pl.pallas_call(
             functools.partial(section_kernel, near if got else 0),
-            out_shape=jax.ShapeDtypeStruct((count, half, rows), dtype),
-            in_specs=[vmem] * (4 + len(got)),
+            out_shape=jax.ShapeDtypeStruct((count, len(pieces) * quarter, rows), dtype),
+            in_specs=[vmem] * (2 + len(pieces) + len(got)),
             out_specs=vmem,
             compiler_params=params,
             cost_estimate=pl.CostEstimate(
@@ -243,15 +241,14 @@
 
     bit = n_chrom // 2
     for_others = lambda pieces: products(outside_others, pieces, near + 1, jnp.bfloat16, "others")
-    head = (first, swap(first, 1, 1))
+    late = (second, second_sibling)
+    head = (first, swap(first, 1, 1), late[1])
     products_head = for_others(head)
-    tail = (second, second_sibling)
+    tail = (late[0],)
     gots = [swap_chrom(products_head, bit), swap_chrom(for_others(tail), bit)]
     for_own = lambda pieces, *got: products(outside_own, pieces, sections // 2, jnp.float32, "own", *got)
-    if n_chrom == 2:
-        owns = [for_own(head, gots[0]), for_own(tail)]
-    else:
-        owns = [for_own(head), for_own(tail)]
+    owns = [for_own(head), for_own(tail)]
+    if bit > 1:
         side = (lax.axis_index("chrom") // bit) % 2
         places = [received(c, sections, near, side) for c in range(sections // 2)]
         gots = [jnp.stack([lax.dynamic_index_in_dim(got, p, 0, False) for p in places]) for got in gots]
@@ -264,25 +261,23 @@
             swap_chrom(lax.dynamic_slice_in_dim(s, (1 - side) * count, count, 0).astype(jnp.bfloat16), bit) for s in sums
         ]
         owns = [lax.dynamic_slice_in_dim(s, side * count, count, 0) for s in sums]
-    if n_chrom > 2:
-        owns[0] = owns[0] + gots[0]
 
     def finish(group, *operands):
         return pl.pallas_call(
             functools.partial(finish_kernel, near if n_chrom == 2 else 0, group),
             out_shape=jax.ShapeDtypeStruct((per_device, rhs, rows), jnp.float32),
-            in_specs=[vmem] * (3 + group) + [anywhere] * group,
+            in_specs=[vmem] * 4 + [anywhere] * group,
             out_specs=anywhere,
             scratch_shapes=[
-                pltpu.VMEM((2, per_device, quarter, rows), jnp.float32),
-                pltpu.SemaphoreType.DMA((2,)),
+                pltpu.VMEM((3 - 2 * group, per_device, quarter, rows), jnp.float32),
+                pltpu.SemaphoreType.DMA((3 - 2 * group,)),
             ],
             input_output_aliases={4: 0} if group else {},
             compiler_params=params,
             name="finish",
         )(inverse, ridged, *operands)
 
-    out = pltpu.with_memory_space_constraint(finish(0, owns[0]), pltpu.HBM)
+    out = pltpu.with_memory_space_constraint(finish(0, owns[0], gots[0]), pltpu.HBM)
     out = finish(1, owns[1], gots[1], out)
     return jnp.transpose(out, (0, 2, 1))
 

time: 31.8 us -> 31.8 us (level)
    ppermute x8, starting transfers between devices: 10.4 us -> 11.5 us  [swap(): lax.ppermute(x, 'samp', [(i, i ^ (high if i.bit_count() % 2 else low)) fo...]
    ppermute x2, starting transfers between devices: 3.26 us -> 2.16 us  [swap_chrom(): return lax.ppermute(x, 'chrom', [(i, i ^ bit) for i in range(n_chrom)])]
    ppermute x8, waiting for transfers between devices: 8.09 us -> 7.6 us  [swap(): lax.ppermute(x, 'samp', [(i, i ^ (high if i.bit_count() % 2 else low)) fo...]
    ppermute x2, waiting for transfers between devices: 1.08 us -> 1.43 us  [swap_chrom(): return lax.ppermute(x, 'chrom', [(i, i ^ bit) for i in range(n_chrom)])]
  transfers between devices with their start and end apart: 10 -> 10, of which waited for: 7 -> 6; matrix products, arithmetic and copies ran while one was open for 0% -> 0% of each run, Pallas kernels for 14% -> 14%
where the time goes in v9:
time: 31.8 us; the launch traced here: 31.6 us
  starting transfers between devices  13.7 us (43%)
  waiting for transfers between devices  9.03 us (28%)
  Pallas kernels  8.04 us (25%)
  between operations  0.77 us (2%)
    ppermute x8, starting transfers between devices, swap(): lax.ppermute(x, 'samp', [(i, i ^ (high if i.bit_count() % 2 else low)) fo...  11.5 us
    ppermute x8, waiting for transfers between devices, swap(): lax.ppermute(x, 'samp', [(i, i ^ (high if i.bit_count() % 2 else low)) fo...  7.6 us
    pallas_call x1, Pallas kernels, on_device(): pl.pallas_call(functools.partial(cross_kernel, blocks), out_shape=(jax.Sh...  2.79 us
    pallas_call x4, Pallas kernels, products(): pl.pallas_call(functools.partial(section_kernel, near if got else 0), out...  2.37 us
    ppermute x2, starting transfers between devices, swap_chrom(): return lax.ppermute(x, 'chrom', [(i, i ^ bit) for i in range(n_chrom)])  2.16 us
    pallas_call x2, Pallas kernels, finish(): pl.pallas_call(functools.partial(finish_kernel, near if n_chrom == 2 else...  1.46 us
    ppermute x2, waiting for transfers between devices, swap_chrom(): return lax.ppermute(x, 'chrom', [(i, i ^ bit) for i in range(n_chrom)])  1.43 us
    pallas_call x1, Pallas kernels, on_device(): pl.pallas_call(functools.partial(prepare_kernel, variants * n_chrom), out...  0.77 us
  transfers between devices with their start and end apart: 10, of which 6 were waited for; matrix products, arithmetic and copies ran while one was open for 0% of the time, Pallas kernels for 14%

profile of v9, /device:TPU:0, one launch (start us, length us, event | category | flops | bytes accessed | tf_op | source)
XLA Modules:
  0.0 31.6 jit_solution(11086217851353207258)
XLA Ops:
  0.0 0.0 copy-start
  0.0 2.8 %cross.1 = (bf16[384,3072]{1,0:T(8,128)(2,1)S(1)}, bf16[16,3072]{1,0:T(8,128)(2,1)S(1)}, bf16[16,3072]{1,0:T(8,128)(2,1)S(1)}, f32[16,3072]{1,0:T(8,128)S(1)}, f32[16,3072]{1,0:T(8,128)S(1)}) custom-call(s32[384,3072]{1,0:T(8,128)} %geno_hbm.1, f32[1,3072]{1,0:T(1,128)} %bitcast.5, f32[64,384]{1,0:T(8,128)} %bitcast.3), custom_call_target="tpu_custom_call" | custom-call | tf_op jit(solution)/shard_map/cross/pallas_call | solution.py:167
  2.8 0.5 %collective-permute-start.1 = (bf16[16,3072]{1,0:T(8,128)(2,1)S(1)}, bf16[16,3072]{1,0:T(8,128)(2,1)S(1)}, u32[]{:S(2)}, u32[]{:S(2)}) collective-permute-start(bf16[16,3072]{1,0:T(8,128)(2,1)S(1)} %get-tuple-element.24), channel_id=1, source_target_pairs={{0,1},{1,0},{2,3},{3,2},{4,5},{5,4},{6,7},{7,6},{8,9},{9,8},{10,11... | collective-permute-start | bytes 294920 | tf_op jit(solution)/shard_map/ppermute | solution.py:202
  3.3 0.1 collective-permute-start
  3.4 0.9 %collective-permute-done.1 = bf16[16,3072]{1,0:T(8,128)(2,1)S(1)} collective-permute-done((bf16[16,3072]{1,0:T(8,128)(2,1)S(1)}, bf16[16,3072]{1,0:T(8,128)(2,1)S(1)}, u32[]{:S(2)}, u32[]{:S(2)}) %collective-permute-start.1) | collective-permute-done | bytes 98336 | tf_op jit(solution)/shard_map/ppermute | solution.py:202
  4.3 2.7 %collective-permute-start.2 = (bf16[16,3072]{1,0:T(8,128)(2,1)S(1)}, bf16[16,3072]{1,0:T(8,128)(2,1)S(1)}, u32[]{:S(2)}, u32[]{:S(2)}) collective-permute-start(bf16[16,3072]{1,0:T(8,128)(2,1)S(1)} %add_convert_fusion.1), channel_id=1, source_target_pairs={{0,3},{1,4},{2,7},{3,0},{4,1},{5,6},{6,5},{7,2},{8,13},{9,10},{10,... | collective-permute-start | bytes 294920 | tf_op jit(solution)/shard_map/ppermute | solution.py:202
  7.6 0.0 copy-done
  7.6 0.0 copy-done.1
  7.7 0.8 %prepare.1 = (bf16[2,16,3072]{2,1,0:T(8,128)(2,1)S(1)}, bf16[4,16,3072]{2,1,0:T(8,128)(2,1)S(1)}, f32[4,16,384]{2,1,0:T(8,128)S(1)}, f32[64,384]{1,0:T(8,128)S(1)}) custom-call(s32[8]{0:T(128)S(1)} %copy-done.1, f32[1]{0:T(128)S(6)} %copy.8.ridge_ref, f32[64,384]{1,0:T(8,128)S(1)} %bitcast.4), custom_call_target="tpu_custom_call" | custom-call | tf_op jit(solution)/shard_map/prepare/pallas_call | solution.py:187
  8.4 0.0 collective-permute-done
  8.4 0.8 %collective-permute-done.2 = bf16[16,3072]{1,0:T(8,128)(2,1)S(1)} collective-permute-done((bf16[16,3072]{1,0:T(8,128)(2,1)S(1)}, bf16[16,3072]{1,0:T(8,128)(2,1)S(1)}, u32[]{:S(2)}, u32[]{:S(2)}) %collective-permute-start.2) | collective-permute-done | bytes 98336 | tf_op jit(solution)/shard_map/ppermute | solution.py:202
  9.3 2.9 %collective-permute-start.3 = (bf16[16,3072]{1,0:T(8,128)(2,1)S(1)}, bf16[16,3072]{1,0:T(8,128)(2,1)S(1)}, u32[]{:S(2)}, u32[]{:S(2)}) collective-permute-start(bf16[16,3072]{1,0:T(8,128)(2,1)S(1)} %convert_element_type.31), channel_id=1, source_target_pairs={{0,9},{1,2},{2,1},{3,10},{4,7},{5,12},{6,15},{7,4},{8,11},{9,0},{1... | collective-permute-start | bytes 294920 | tf_op jit(solution)/shard_map/ppermute | solution.py:202
  12.2 0.7 %turn.1.turned_ref = bf16[3072,384]{1,0:T(8,128)(2,1)S(1)} custom-call(bf16[384,3072]{1,0:T(8,128)(2,1)S(1)} %get-tuple-element.33.stand_ref), custom_call_target="tpu_custom_call" | custom-call | tf_op jit(solution)/shard_map/turn/pallas_call | solution.py:211
  12.9 1.6 %collective-permute-done.3 = bf16[16,3072]{1,0:T(8,128)(2,1)S(1)} collective-permute-done((bf16[16,3072]{1,0:T(8,128)(2,1)S(1)}, bf16[16,3072]{1,0:T(8,128)(2,1)S(1)}, u32[]{:S(2)}, u32[]{:S(2)}) %collective-permute-start.3) | collective-permute-done | bytes 98336 | tf_op jit(solution)/shard_map/ppermute | solution.py:202
  14.6 1.9 %collective-permute-start.4 = (bf16[16,3072]{1,0:T(8,128)(2,1)S(1)}, bf16[16,3072]{1,0:T(8,128)(2,1)S(1)}, u32[]{:S(2)}, u32[]{:S(2)}) collective-permute-start(bf16[16,3072]{1,0:T(8,128)(2,1)S(1)} %convert_element_type.33), channel_id=1, source_target_pairs={{0,5},{1,8},{2,11},{3,6},{4,13},{5,0},{6,3},{7,14},{8,1},{9,12},{1... | collective-permute-start | bytes 294920 | tf_op jit(solution)/shard_map/ppermute | solution.py:202
  16.5 3.0 %collective-permute-done.4 = bf16[16,3072]{1,0:T(8,128)(2,1)S(1)} collective-permute-done((bf16[16,3072]{1,0:T(8,128)(2,1)S(1)}, bf16[16,3072]{1,0:T(8,128)(2,1)S(1)}, u32[]{:S(2)}, u32[]{:S(2)}) %collective-permute-start.4) | collective-permute-done | bytes 98336 | tf_op jit(solution)/shard_map/ppermute | solution.py:202
  19.5 1.4 %collective-permute-start.8 = (bf16[16,3072]{1,0:T(8,128)(2,1)S(1)}, bf16[16,3072]{1,0:T(8,128)(2,1)S(1)}, u32[]{:S(2)}, u32[]{:S(2)}) collective-permute-start(bf16[16,3072]{1,0:T(8,128)(2,1)S(1)} %add_convert_fusion.refs_0_), channel_id=1, source_target_pairs={{0,2},{1,5},{2,6},{3,1},{4,0},{5,7},{6,4},{7,3},{8,12},{9,11},{10,... | collective-permute-start | bytes 294920 | tf_op jit(solution)/shard_map/ppermute | solution.py:202
  20.9 0.5 %collective-permute-start.7 = (bf16[16,3072]{1,0:T(8,128)(2,1)S(1)}, bf16[16,3072]{1,0:T(8,128)(2,1)S(1)}, u32[]{:S(2)}, u32[]{:S(2)}) collective-permute-start(bf16[16,3072]{1,0:T(8,128)(2,1)S(1)} %add_convert_fusion.refs_0_), channel_id=1, source_target_pairs={{0,1},{1,0},{2,3},{3,2},{4,5},{5,4},{6,7},{7,6},{8,9},{9,8},{10,11... | collective-permute-start | bytes 294920 | tf_op jit(solution)/shard_map/ppermute | solution.py:202
  21.3 1.6 %collective-permute-start.5 = (bf16[16,3072]{1,0:T(8,128)(2,1)S(1)}, bf16[16,3072]{1,0:T(8,128)(2,1)S(1)}, u32[]{:S(2)}, u32[]{:S(2)}) collective-permute-start(bf16[16,3072]{1,0:T(8,128)(2,1)S(1)} %add_convert_fusion.refs_0_), channel_id=1, source_target_pairs={{0,3},{1,4},{2,7},{3,0},{4,1},{5,6},{6,5},{7,2},{8,13},{9,10},{10,... | collective-permute-start | bytes 294920 | tf_op jit(solution)/shard_map/ppermute | solution.py:202
  22.9 1.3 %collective-permute-done.8.refs_2_ = bf16[16,3072]{1,0:T(8,128)(2,1)S(1)} collective-permute-done((bf16[16,3072]{1,0:T(8,128)(2,1)S(1)}, bf16[16,3072]{1,0:T(8,128)(2,1)S(1)}, u32[]{:S(2)}, u32[]{:S(2)}) %collective-permute-start.8) | collective-permute-done | bytes 98336 | tf_op jit(solution)/shard_map/ppermute | solution.py:202
  24.2 0.0 collective-permute-done.7.refs_1_
  24.2 0.6 %others.3 = bf16[3,48,384]{2,1,0:T(8,128)(2,1)S(1)} custom-call(bf16[2,16,3072]{2,1,0:T(8,128)(2,1)S(1)} %get-tuple-element.36.outside_ref, bf16[3072,384]{1,0:T(8,128)(2,1)S(1)} %turn.1.turned_ref, bf16[16,3072]{1,0:T(8,128)(2,1)S(1)} %add_convert_fusion.refs_0_, bf16[16,3072]{1,0:T(8,128)(2,1)S(1)} %collective-permute-done.7.refs_1_, ...), custom_call_target="tpu_custom_call" | custom-call | flops 301989888 | bytes 2359296 | tf_op jit(solution)/shard_map/others/pallas_call | solution.py:227
  24.8 1.5 %collective-permute-start.9 = (bf16[3,48,384]{2,1,0:T(8,128)(2,1)S(1)}, bf16[3,48,384]{2,1,0:T(8,128)(2,1)S(1)}, u32[]{:S(2)}, u32[]{:S(2)}) collective-permute-start(bf16[3,48,384]{2,1,0:T(8,128)(2,1)S(1)} %others.3), channel_id=1, source_target_pairs={{0,16},{16,0},{1,17},{17,1},{2,18},{18,2},{3,19},{19,3},{4,20},{20... | collective-permute-start | bytes 331784 | tf_op jit(solution)/shard_map/ppermute | solution.py:240
  26.3 0.0 collective-permute-done.5.refs_0_
  26.3 0.5 %others.2 = bf16[3,16,384]{2,1,0:T(8,128)(2,1)S(1)} custom-call(bf16[2,16,3072]{2,1,0:T(8,128)(2,1)S(1)} %get-tuple-element.36.outside_ref, bf16[3072,384]{1,0:T(8,128)(2,1)S(1)} %turn.1.turned_ref, bf16[16,3072]{1,0:T(8,128)(2,1)S(1)} %collective-permute-done.5.refs_0_), custom_call_target="tpu_custom_call" | custom-call | flops 301989888 | bytes 2359296 | tf_op jit(solution)/shard_map/others/pallas_call | solution.py:227
  26.8 0.6 %collective-permute-start.6 = (bf16[3,16,384]{2,1,0:T(8,128)(2,1)S(1)}, bf16[3,16,384]{2,1,0:T(8,128)(2,1)S(1)}, u32[]{:S(2)}, u32[]{:S(2)}) collective-permute-start(bf16[3,16,384]{2,1,0:T(8,128)(2,1)S(1)} %others.2), channel_id=1, source_target_pairs={{0,16},{16,0},{1,17},{17,1},{2,18},{18,2},{3,19},{19,3},{4,20},{20... | collective-permute-start | bytes 110600 | tf_op jit(solution)/shard_map/ppermute | solution.py:240
  27.4 0.8 %own.3.own_ref = f32[4,48,384]{2,1,0:T(8,128)S(1)} custom-call(bf16[4,16,3072]{2,1,0:T(8,128)(2,1)S(1)} %get-tuple-element.31.outside_ref, bf16[3072,384]{1,0:T(8,128)(2,1)S(1)} %turn.1.turned_ref, bf16[16,3072]{1,0:T(8,128)(2,1)S(1)} %add_convert_fusion.refs_0_, bf16[16,3072]{1,0:T(8,128)(2,1)S(1)} %collective-permute-done.7.refs_1_, ...), custom_call_target="tpu_custom_call" | custom-call | flops 301989888 | bytes 2359296 | tf_op jit(solution)/shard_map/own/pallas_call | solution.py:227
  28.2 0.5 %own.2.own_ref = f32[4,16,384]{2,1,0:T(8,128)S(1)} custom-call(bf16[4,16,3072]{2,1,0:T(8,128)(2,1)S(1)} %get-tuple-element.31.outside_ref, bf16[3072,384]{1,0:T(8,128)(2,1)S(1)} %turn.1.turned_ref, bf16[16,3072]{1,0:T(8,128)(2,1)S(1)} %collective-permute-done.5.refs_0_), custom_call_target="tpu_custom_call" | custom-call | flops 301989888 | bytes 2359296 | tf_op jit(solution)/shard_map/own/pallas_call | solution.py:227
  28.7 1.4 %collective-permute-done.9.got_ref = bf16[3,48,384]{2,1,0:T(8,128)(2,1)S(1)} collective-permute-done((bf16[3,48,384]{2,1,0:T(8,128)(2,1)S(1)}, bf16[3,48,384]{2,1,0:T(8,128)(2,1)S(1)}, u32[]{:S(2)}, u32[]{:S(2)}) %collective-permute-start.9) | collective-permute-done | bytes 110624 | tf_op jit(solution)/shard_map/ppermute | solution.py:240
  30.2 0.8 %finish.2.refs_0_ = f32[4,64,384]{2,1,0:T(8,128)} custom-call(f32[4,16,384]{2,1,0:T(8,128)S(1)} %get-tuple-element.29.inverse_ref, f32[64,384]{1,0:T(8,128)S(1)} %get-tuple-element.30.ridged_ref, f32[4,48,384]{2,1,0:T(8,128)S(1)} %own.3.own_ref, bf16[3,48,384]{2,1,0:T(8,128)(2,1)S(1)} %collective-permute-done.9.got_ref), custom_call_target="tpu_custom_call" | custom-call | tf_op jit(solution)/shard_map/finish/pallas_call | solution.py:266
  30.9 0.0 collective-permute-done.6.got_ref
  30.9 0.7 %finish.3 = f32[4,64,384]{2,1,0:T(8,128)} custom-call(f32[4,16,384]{2,1,0:T(8,128)S(1)} %get-tuple-element.29.inverse_ref, f32[64,384]{1,0:T(8,128)S(1)} %get-tuple-element.30.ridged_ref, f32[4,16,384]{2,1,0:T(8,128)S(1)} %own.2.own_ref, bf16[3,16,384]{2,1,0:T(8,128)(2,1)S(1)} %collective-permute-done.6.got_ref, ...), custom_call_target="tpu_custom_call", output_to_operand_aliasing={{}: (4, {})} | custom-call | tf_op jit(solution)/shard_map/finish/pallas_call | solution.py:266
  (7 shorter events, 0.1 us)
Async XLA Ops:
  0.0 7.6 %copy-start = (f32[384,64]{0,1:T(8,128)S(1)}, f32[384,64]{0,1:T(8,128)}, u32[]{:S(2)}) copy-start(f32[384,64]{0,1:T(8,128)} %param.9) | copy-start | bytes 294916
  0.0 7.6 %copy-start.1 = (s32[8]{0:T(128)S(1)}, s32[8]{0:T(128)}, u32[]{:S(2)}) copy-start(s32[8]{0:T(128)} %widths_ref.1) | copy-start | bytes 100
  2.8 1.5 %collective-permute-start.1 = (bf16[16,3072]{1,0:T(8,128)(2,1)S(1)}, bf16[16,3072]{1,0:T(8,128)(2,1)S(1)}, u32[]{:S(2)}, u32[]{:S(2)}) collective-permute-start(bf16[16,3072]{1,0:T(8,128)(2,1)S(1)} %get-tuple-element.24), channel_id=1, source_target_pairs={{0,1},{1,0},{2,3},{3,2},{4,5},{5,4},{6,7},{7,6},{8,9},{9,8},{10,11... | collective-permute-start | bytes 294920 | tf_op jit(solution)/shard_map/ppermute | solution.py:202
  3.3 5.1 %collective-permute-start = (bf16[16,3072]{1,0:T(8,128)(2,1)S(1)}, bf16[16,3072]{1,0:T(8,128)(2,1)S(1)}, u32[]{:S(2)}, u32[]{:S(2)}) collective-permute-start(bf16[16,3072]{1,0:T(8,128)(2,1)S(1)} %get-tuple-element.22), channel_id=1, source_target_pairs={{0,1},{1,0},{2,3},{3,2},{4,5},{5,4},{6,7},{7,6},{8,9},{9,8},{10,11... | collective-permute-start | bytes 294920 | tf_op jit(solution)/shard_map/ppermute | solution.py:202
  4.3 5.0 %collective-permute-start.2 = (bf16[16,3072]{1,0:T(8,128)(2,1)S(1)}, bf16[16,3072]{1,0:T(8,128)(2,1)S(1)}, u32[]{:S(2)}, u32[]{:S(2)}) collective-permute-start(bf16[16,3072]{1,0:T(8,128)(2,1)S(1)} %add_convert_fusion.1), channel_id=1, source_target_pairs={{0,3},{1,4},{2,7},{3,0},{4,1},{5,6},{6,5},{7,2},{8,13},{9,10},{10,... | collective-permute-start | bytes 294920 | tf_op jit(solution)/shard_map/ppermute | solution.py:202
  9.3 5.2 %collective-permute-start.3 = (bf16[16,3072]{1,0:T(8,128)(2,1)S(1)}, bf16[16,3072]{1,0:T(8,128)(2,1)S(1)}, u32[]{:S(2)}, u32[]{:S(2)}) collective-permute-start(bf16[16,3072]{1,0:T(8,128)(2,1)S(1)} %convert_element_type.31), channel_id=1, source_target_pairs={{0,9},{1,2},{2,1},{3,10},{4,7},{5,12},{6,15},{7,4},{8,11},{9,0},{1... | collective-permute-start | bytes 294920 | tf_op jit(solution)/shard_map/ppermute | solution.py:202
  14.6 4.9 %collective-permute-start.4 = (bf16[16,3072]{1,0:T(8,128)(2,1)S(1)}, bf16[16,3072]{1,0:T(8,128)(2,1)S(1)}, u32[]{:S(2)}, u32[]{:S(2)}) collective-permute-start(bf16[16,3072]{1,0:T(8,128)(2,1)S(1)} %convert_element_type.33), channel_id=1, source_target_pairs={{0,5},{1,8},{2,11},{3,6},{4,13},{5,0},{6,3},{7,14},{8,1},{9,12},{1... | collective-permute-start | bytes 294920 | tf_op jit(solution)/shard_map/ppermute | solution.py:202
  19.5 4.7 %collective-permute-start.8 = (bf16[16,3072]{1,0:T(8,128)(2,1)S(1)}, bf16[16,3072]{1,0:T(8,128)(2,1)S(1)}, u32[]{:S(2)}, u32[]{:S(2)}) collective-permute-start(bf16[16,3072]{1,0:T(8,128)(2,1)S(1)} %add_convert_fusion.refs_0_), channel_id=1, source_target_pairs={{0,2},{1,5},{2,6},{3,1},{4,0},{5,7},{6,4},{7,3},{8,12},{9,11},{10,... | collective-permute-start | bytes 294920 | tf_op jit(solution)/shard_map/ppermute | solution.py:202
  20.9 3.3 %collective-permute-start.7 = (bf16[16,3072]{1,0:T(8,128)(2,1)S(1)}, bf16[16,3072]{1,0:T(8,128)(2,1)S(1)}, u32[]{:S(2)}, u32[]{:S(2)}) collective-permute-start(bf16[16,3072]{1,0:T(8,128)(2,1)S(1)} %add_convert_fusion.refs_0_), channel_id=1, source_target_pairs={{0,1},{1,0},{2,3},{3,2},{4,5},{5,4},{6,7},{7,6},{8,9},{9,8},{10,11... | collective-permute-start | bytes 294920 | tf_op jit(solution)/shard_map/ppermute | solution.py:202
  21.3 5.0 %collective-permute-start.5 = (bf16[16,3072]{1,0:T(8,128)(2,1)S(1)}, bf16[16,3072]{1,0:T(8,128)(2,1)S(1)}, u32[]{:S(2)}, u32[]{:S(2)}) collective-permute-start(bf16[16,3072]{1,0:T(8,128)(2,1)S(1)} %add_convert_fusion.refs_0_), channel_id=1, source_target_pairs={{0,3},{1,4},{2,7},{3,0},{4,1},{5,6},{6,5},{7,2},{8,13},{9,10},{10,... | collective-permute-start | bytes 294920 | tf_op jit(solution)/shard_map/ppermute | solution.py:202
  24.8 5.4 %collective-permute-start.9 = (bf16[3,48,384]{2,1,0:T(8,128)(2,1)S(1)}, bf16[3,48,384]{2,1,0:T(8,128)(2,1)S(1)}, u32[]{:S(2)}, u32[]{:S(2)}) collective-permute-start(bf16[3,48,384]{2,1,0:T(8,128)(2,1)S(1)} %others.3), channel_id=1, source_target_pairs={{0,16},{16,0},{1,17},{17,1},{2,18},{18,2},{3,19},{19,3},{4,20},{20... | collective-permute-start | bytes 331784 | tf_op jit(solution)/shard_map/ppermute | solution.py:240
  26.8 4.1 %collective-permute-start.6 = (bf16[3,16,384]{2,1,0:T(8,128)(2,1)S(1)}, bf16[3,16,384]{2,1,0:T(8,128)(2,1)S(1)}, u32[]{:S(2)}, u32[]{:S(2)}) collective-permute-start(bf16[3,16,384]{2,1,0:T(8,128)(2,1)S(1)} %others.2), channel_id=1, source_target_pairs={{0,16},{16,0},{1,17},{17,1},{2,18},{18,2},{3,19},{19,3},{4,20},{20... | collective-permute-start | bytes 110600 | tf_op jit(solution)/shard_map/ppermute | solution.py:240

commit v10 on v9

--- a/solution.py
+++ b/solution.py
@@ -8,7 +8,7 @@
 from jax.sharding import PartitionSpec as P
 
 VMEM_LIMIT = 24 * 1024 * 1024
-BLOCK = 512
+BLOCK = 768
 
 
 def half_and_bits():

time: 31.8 us -> 31.8 us (level)
  no operation moved by 1% of the time
where the time goes in v10:
time: 31.8 us; the launch traced here: 31.7 us
  starting transfers between devices  13.7 us (43%)
  waiting for transfers between devices  9.03 us (28%)
  Pallas kernels  8.06 us (25%)
  between operations  0.77 us (2%)
    ppermute x8, starting transfers between devices, swap(): lax.ppermute(x, 'samp', [(i, i ^ (high if i.bit_count() % 2 else low)) fo...  11.5 us
    ppermute x8, waiting for transfers between devices, swap(): lax.ppermute(x, 'samp', [(i, i ^ (high if i.bit_count() % 2 else low)) fo...  7.6 us
    pallas_call x1, Pallas kernels, on_device(): pl.pallas_call(functools.partial(cross_kernel, blocks), out_shape=(jax.Sh...  2.8 us
    pallas_call x4, Pallas kernels, products(): pl.pallas_call(functools.partial(section_kernel, near if got else 0), out...  2.37 us
    ppermute x2, starting transfers between devices, swap_chrom(): return lax.ppermute(x, 'chrom', [(i, i ^ bit) for i in range(n_chrom)])  2.16 us
    pallas_call x2, Pallas kernels, finish(): pl.pallas_call(functools.partial(finish_kernel, near if n_chrom == 2 else...  1.46 us
    ppermute x2, waiting for transfers between devices, swap_chrom(): return lax.ppermute(x, 'chrom', [(i, i ^ bit) for i in range(n_chrom)])  1.43 us
    pallas_call x1, Pallas kernels, on_device(): pl.pallas_call(functools.partial(prepare_kernel, variants * n_chrom), out...  0.77 us
  transfers between devices with their start and end apart: 10, of which 6 were waited for; matrix products, arithmetic and copies ran while one was open for 0% of the time, Pallas kernels for 14%

profile of v10, /device:TPU:0, one launch (start us, length us, event | category | flops | bytes accessed | tf_op | source)
XLA Modules:
  0.0 31.7 jit_solution(6283620565326383721)
XLA Ops:
  0.0 0.0 copy-start
  0.0 2.8 %cross.1 = (bf16[384,3072]{1,0:T(8,128)(2,1)S(1)}, bf16[16,3072]{1,0:T(8,128)(2,1)S(1)}, bf16[16,3072]{1,0:T(8,128)(2,1)S(1)}, f32[16,3072]{1,0:T(8,128)S(1)}, f32[16,3072]{1,0:T(8,128)S(1)}) custom-call(s32[384,3072]{1,0:T(8,128)} %geno_hbm.1, f32[1,3072]{1,0:T(1,128)} %bitcast.5, f32[64,384]{1,0:T(8,128)} %bitcast.3), custom_call_target="tpu_custom_call" | custom-call | tf_op jit(solution)/shard_map/cross/pallas_call | solution.py:167
  2.8 0.5 %collective-permute-start.1 = (bf16[16,3072]{1,0:T(8,128)(2,1)S(1)}, bf16[16,3072]{1,0:T(8,128)(2,1)S(1)}, u32[]{:S(2)}, u32[]{:S(2)}) collective-permute-start(bf16[16,3072]{1,0:T(8,128)(2,1)S(1)} %get-tuple-element.24), channel_id=1, source_target_pairs={{0,1},{1,0},{2,3},{3,2},{4,5},{5,4},{6,7},{7,6},{8,9},{9,8},{10,11... | collective-permute-start | bytes 294920 | tf_op jit(solution)/shard_map/ppermute | solution.py:202
  3.3 0.1 collective-permute-start
  3.4 0.9 %collective-permute-done.1 = bf16[16,3072]{1,0:T(8,128)(2,1)S(1)} collective-permute-done((bf16[16,3072]{1,0:T(8,128)(2,1)S(1)}, bf16[16,3072]{1,0:T(8,128)(2,1)S(1)}, u32[]{:S(2)}, u32[]{:S(2)}) %collective-permute-start.1) | collective-permute-done | bytes 98336 | tf_op jit(solution)/shard_map/ppermute | solution.py:202
  4.3 2.7 %collective-permute-start.2 = (bf16[16,3072]{1,0:T(8,128)(2,1)S(1)}, bf16[16,3072]{1,0:T(8,128)(2,1)S(1)}, u32[]{:S(2)}, u32[]{:S(2)}) collective-permute-start(bf16[16,3072]{1,0:T(8,128)(2,1)S(1)} %add_convert_fusion.1), channel_id=1, source_target_pairs={{0,3},{1,4},{2,7},{3,0},{4,1},{5,6},{6,5},{7,2},{8,13},{9,10},{10,... | collective-permute-start | bytes 294920 | tf_op jit(solution)/shard_map/ppermute | solution.py:202
  7.6 0.0 copy-done
  7.7 0.0 copy-done.1
  7.7 0.8 %prepare.1 = (bf16[2,16,3072]{2,1,0:T(8,128)(2,1)S(1)}, bf16[4,16,3072]{2,1,0:T(8,128)(2,1)S(1)}, f32[4,16,384]{2,1,0:T(8,128)S(1)}, f32[64,384]{1,0:T(8,128)S(1)}) custom-call(s32[8]{0:T(128)S(1)} %copy-done.1, f32[1]{0:T(128)S(6)} %copy.8.ridge_ref, f32[64,384]{1,0:T(8,128)S(1)} %bitcast.4), custom_call_target="tpu_custom_call" | custom-call | tf_op jit(solution)/shard_map/prepare/pallas_call | solution.py:187
  8.4 0.0 collective-permute-done
  8.5 0.8 %collective-permute-done.2 = bf16[16,3072]{1,0:T(8,128)(2,1)S(1)} collective-permute-done((bf16[16,3072]{1,0:T(8,128)(2,1)S(1)}, bf16[16,3072]{1,0:T(8,128)(2,1)S(1)}, u32[]{:S(2)}, u32[]{:S(2)}) %collective-permute-start.2) | collective-permute-done | bytes 98336 | tf_op jit(solution)/shard_map/ppermute | solution.py:202
  9.4 2.9 %collective-permute-start.3 = (bf16[16,3072]{1,0:T(8,128)(2,1)S(1)}, bf16[16,3072]{1,0:T(8,128)(2,1)S(1)}, u32[]{:S(2)}, u32[]{:S(2)}) collective-permute-start(bf16[16,3072]{1,0:T(8,128)(2,1)S(1)} %convert_element_type.31), channel_id=1, source_target_pairs={{0,9},{1,2},{2,1},{3,10},{4,7},{5,12},{6,15},{7,4},{8,11},{9,0},{1... | collective-permute-start | bytes 294920 | tf_op jit(solution)/shard_map/ppermute | solution.py:202
  12.2 0.7 %turn.1.turned_ref = bf16[3072,384]{1,0:T(8,128)(2,1)S(1)} custom-call(bf16[384,3072]{1,0:T(8,128)(2,1)S(1)} %get-tuple-element.33.stand_ref), custom_call_target="tpu_custom_call" | custom-call | tf_op jit(solution)/shard_map/turn/pallas_call | solution.py:211
  12.9 1.6 %collective-permute-done.3 = bf16[16,3072]{1,0:T(8,128)(2,1)S(1)} collective-permute-done((bf16[16,3072]{1,0:T(8,128)(2,1)S(1)}, bf16[16,3072]{1,0:T(8,128)(2,1)S(1)}, u32[]{:S(2)}, u32[]{:S(2)}) %collective-permute-start.3) | collective-permute-done | bytes 98336 | tf_op jit(solution)/shard_map/ppermute | solution.py:202
  14.6 1.9 %collective-permute-start.4 = (bf16[16,3072]{1,0:T(8,128)(2,1)S(1)}, bf16[16,3072]{1,0:T(8,128)(2,1)S(1)}, u32[]{:S(2)}, u32[]{:S(2)}) collective-permute-start(bf16[16,3072]{1,0:T(8,128)(2,1)S(1)} %convert_element_type.33), channel_id=1, source_target_pairs={{0,5},{1,8},{2,11},{3,6},{4,13},{5,0},{6,3},{7,14},{8,1},{9,12},{1... | collective-permute-start | bytes 294920 | tf_op jit(solution)/shard_map/ppermute | solution.py:202
  16.5 3.0 %collective-permute-done.4 = bf16[16,3072]{1,0:T(8,128)(2,1)S(1)} collective-permute-done((bf16[16,3072]{1,0:T(8,128)(2,1)S(1)}, bf16[16,3072]{1,0:T(8,128)(2,1)S(1)}, u32[]{:S(2)}, u32[]{:S(2)}) %collective-permute-start.4) | collective-permute-done | bytes 98336 | tf_op jit(solution)/shard_map/ppermute | solution.py:202
  19.5 1.4 %collective-permute-start.8 = (bf16[16,3072]{1,0:T(8,128)(2,1)S(1)}, bf16[16,3072]{1,0:T(8,128)(2,1)S(1)}, u32[]{:S(2)}, u32[]{:S(2)}) collective-permute-start(bf16[16,3072]{1,0:T(8,128)(2,1)S(1)} %add_convert_fusion.refs_0_), channel_id=1, source_target_pairs={{0,2},{1,5},{2,6},{3,1},{4,0},{5,7},{6,4},{7,3},{8,12},{9,11},{10,... | collective-permute-start | bytes 294920 | tf_op jit(solution)/shard_map/ppermute | solution.py:202
  20.9 0.5 %collective-permute-start.7 = (bf16[16,3072]{1,0:T(8,128)(2,1)S(1)}, bf16[16,3072]{1,0:T(8,128)(2,1)S(1)}, u32[]{:S(2)}, u32[]{:S(2)}) collective-permute-start(bf16[16,3072]{1,0:T(8,128)(2,1)S(1)} %add_convert_fusion.refs_0_), channel_id=1, source_target_pairs={{0,1},{1,0},{2,3},{3,2},{4,5},{5,4},{6,7},{7,6},{8,9},{9,8},{10,11... | collective-permute-start | bytes 294920 | tf_op jit(solution)/shard_map/ppermute | solution.py:202
  21.3 1.6 %collective-permute-start.5 = (bf16[16,3072]{1,0:T(8,128)(2,1)S(1)}, bf16[16,3072]{1,0:T(8,128)(2,1)S(1)}, u32[]{:S(2)}, u32[]{:S(2)}) collective-permute-start(bf16[16,3072]{1,0:T(8,128)(2,1)S(1)} %add_convert_fusion.refs_0_), channel_id=1, source_target_pairs={{0,3},{1,4},{2,7},{3,0},{4,1},{5,6},{6,5},{7,2},{8,13},{9,10},{10,... | collective-permute-start | bytes 294920 | tf_op jit(solution)/shard_map/ppermute | solution.py:202
  22.9 1.3 %collective-permute-done.8.refs_2_ = bf16[16,3072]{1,0:T(8,128)(2,1)S(1)} collective-permute-done((bf16[16,3072]{1,0:T(8,128)(2,1)S(1)}, bf16[16,3072]{1,0:T(8,128)(2,1)S(1)}, u32[]{:S(2)}, u32[]{:S(2)}) %collective-permute-start.8) | collective-permute-done | bytes 98336 | tf_op jit(solution)/shard_map/ppermute | solution.py:202
  24.2 0.0 collective-permute-done.7.refs_1_
  24.2 0.6 %others.3 = bf16[3,48,384]{2,1,0:T(8,128)(2,1)S(1)} custom-call(bf16[2,16,3072]{2,1,0:T(8,128)(2,1)S(1)} %get-tuple-element.36.outside_ref, bf16[3072,384]{1,0:T(8,128)(2,1)S(1)} %turn.1.turned_ref, bf16[16,3072]{1,0:T(8,128)(2,1)S(1)} %add_convert_fusion.refs_0_, bf16[16,3072]{1,0:T(8,128)(2,1)S(1)} %collective-permute-done.7.refs_1_, ...), custom_call_target="tpu_custom_call" | custom-call | flops 301989888 | bytes 2359296 | tf_op jit(solution)/shard_map/others/pallas_call | solution.py:227
  24.8 1.5 %collective-permute-start.9 = (bf16[3,48,384]{2,1,0:T(8,128)(2,1)S(1)}, bf16[3,48,384]{2,1,0:T(8,128)(2,1)S(1)}, u32[]{:S(2)}, u32[]{:S(2)}) collective-permute-start(bf16[3,48,384]{2,1,0:T(8,128)(2,1)S(1)} %others.3), channel_id=1, source_target_pairs={{0,16},{16,0},{1,17},{17,1},{2,18},{18,2},{3,19},{19,3},{4,20},{20... | collective-permute-start | bytes 331784 | tf_op jit(solution)/shard_map/ppermute | solution.py:240
  26.4 0.0 collective-permute-done.5.refs_0_
  26.4 0.5 %others.2 = bf16[3,16,384]{2,1,0:T(8,128)(2,1)S(1)} custom-call(bf16[2,16,3072]{2,1,0:T(8,128)(2,1)S(1)} %get-tuple-element.36.outside_ref, bf16[3072,384]{1,0:T(8,128)(2,1)S(1)} %turn.1.turned_ref, bf16[16,3072]{1,0:T(8,128)(2,1)S(1)} %collective-permute-done.5.refs_0_), custom_call_target="tpu_custom_call" | custom-call | flops 301989888 | bytes 2359296 | tf_op jit(solution)/shard_map/others/pallas_call | solution.py:227
  26.8 0.6 %collective-permute-start.6 = (bf16[3,16,384]{2,1,0:T(8,128)(2,1)S(1)}, bf16[3,16,384]{2,1,0:T(8,128)(2,1)S(1)}, u32[]{:S(2)}, u32[]{:S(2)}) collective-permute-start(bf16[3,16,384]{2,1,0:T(8,128)(2,1)S(1)} %others.2), channel_id=1, source_target_pairs={{0,16},{16,0},{1,17},{17,1},{2,18},{18,2},{3,19},{19,3},{4,20},{20... | collective-permute-start | bytes 110600 | tf_op jit(solution)/shard_map/ppermute | solution.py:240
  27.5 0.8 %own.3.own_ref = f32[4,48,384]{2,1,0:T(8,128)S(1)} custom-call(bf16[4,16,3072]{2,1,0:T(8,128)(2,1)S(1)} %get-tuple-element.31.outside_ref, bf16[3072,384]{1,0:T(8,128)(2,1)S(1)} %turn.1.turned_ref, bf16[16,3072]{1,0:T(8,128)(2,1)S(1)} %add_convert_fusion.refs_0_, bf16[16,3072]{1,0:T(8,128)(2,1)S(1)} %collective-permute-done.7.refs_1_, ...), custom_call_target="tpu_custom_call" | custom-call | flops 301989888 | bytes 2359296 | tf_op jit(solution)/shard_map/own/pallas_call | solution.py:227
  28.2 0.5 %own.2.own_ref = f32[4,16,384]{2,1,0:T(8,128)S(1)} custom-call(bf16[4,16,3072]{2,1,0:T(8,128)(2,1)S(1)} %get-tuple-element.31.outside_ref, bf16[3072,384]{1,0:T(8,128)(2,1)S(1)} %turn.1.turned_ref, bf16[16,3072]{1,0:T(8,128)(2,1)S(1)} %collective-permute-done.5.refs_0_), custom_call_target="tpu_custom_call" | custom-call | flops 301989888 | bytes 2359296 | tf_op jit(solution)/shard_map/own/pallas_call | solution.py:227
  28.8 1.4 %collective-permute-done.9.got_ref = bf16[3,48,384]{2,1,0:T(8,128)(2,1)S(1)} collective-permute-done((bf16[3,48,384]{2,1,0:T(8,128)(2,1)S(1)}, bf16[3,48,384]{2,1,0:T(8,128)(2,1)S(1)}, u32[]{:S(2)}, u32[]{:S(2)}) %collective-permute-start.9) | collective-permute-done | bytes 110624 | tf_op jit(solution)/shard_map/ppermute | solution.py:240
  30.2 0.8 %finish.2.refs_0_ = f32[4,64,384]{2,1,0:T(8,128)} custom-call(f32[4,16,384]{2,1,0:T(8,128)S(1)} %get-tuple-element.29.inverse_ref, f32[64,384]{1,0:T(8,128)S(1)} %get-tuple-element.30.ridged_ref, f32[4,48,384]{2,1,0:T(8,128)S(1)} %own.3.own_ref, bf16[3,48,384]{2,1,0:T(8,128)(2,1)S(1)} %collective-permute-done.9.got_ref), custom_call_target="tpu_custom_call" | custom-call | tf_op jit(solution)/shard_map/finish/pallas_call | solution.py:266
  30.9 0.0 collective-permute-done.6.got_ref
  31.0 0.7 %finish.3 = f32[4,64,384]{2,1,0:T(8,128)} custom-call(f32[4,16,384]{2,1,0:T(8,128)S(1)} %get-tuple-element.29.inverse_ref, f32[64,384]{1,0:T(8,128)S(1)} %get-tuple-element.30.ridged_ref, f32[4,16,384]{2,1,0:T(8,128)S(1)} %own.2.own_ref, bf16[3,16,384]{2,1,0:T(8,128)(2,1)S(1)} %collective-permute-done.6.got_ref, ...), custom_call_target="tpu_custom_call", output_to_operand_aliasing={{}: (4, {})} | custom-call | tf_op jit(solution)/shard_map/finish/pallas_call | solution.py:266
  (7 shorter events, 0.1 us)
Async XLA Ops:
  0.0 7.7 %copy-start = (f32[384,64]{0,1:T(8,128)S(1)}, f32[384,64]{0,1:T(8,128)}, u32[]{:S(2)}) copy-start(f32[384,64]{0,1:T(8,128)} %param.9) | copy-start | bytes 294916
  0.0 7.7 %copy-start.1 = (s32[8]{0:T(128)S(1)}, s32[8]{0:T(128)}, u32[]{:S(2)}) copy-start(s32[8]{0:T(128)} %widths_ref.1) | copy-start | bytes 100
  2.8 1.5 %collective-permute-start.1 = (bf16[16,3072]{1,0:T(8,128)(2,1)S(1)}, bf16[16,3072]{1,0:T(8,128)(2,1)S(1)}, u32[]{:S(2)}, u32[]{:S(2)}) collective-permute-start(bf16[16,3072]{1,0:T(8,128)(2,1)S(1)} %get-tuple-element.24), channel_id=1, source_target_pairs={{0,1},{1,0},{2,3},{3,2},{4,5},{5,4},{6,7},{7,6},{8,9},{9,8},{10,11... | collective-permute-start | bytes 294920 | tf_op jit(solution)/shard_map/ppermute | solution.py:202
  3.3 5.1 %collective-permute-start = (bf16[16,3072]{1,0:T(8,128)(2,1)S(1)}, bf16[16,3072]{1,0:T(8,128)(2,1)S(1)}, u32[]{:S(2)}, u32[]{:S(2)}) collective-permute-start(bf16[16,3072]{1,0:T(8,128)(2,1)S(1)} %get-tuple-element.22), channel_id=1, source_target_pairs={{0,1},{1,0},{2,3},{3,2},{4,5},{5,4},{6,7},{7,6},{8,9},{9,8},{10,11... | collective-permute-start | bytes 294920 | tf_op jit(solution)/shard_map/ppermute | solution.py:202
  4.3 5.0 %collective-permute-start.2 = (bf16[16,3072]{1,0:T(8,128)(2,1)S(1)}, bf16[16,3072]{1,0:T(8,128)(2,1)S(1)}, u32[]{:S(2)}, u32[]{:S(2)}) collective-permute-start(bf16[16,3072]{1,0:T(8,128)(2,1)S(1)} %add_convert_fusion.1), channel_id=1, source_target_pairs={{0,3},{1,4},{2,7},{3,0},{4,1},{5,6},{6,5},{7,2},{8,13},{9,10},{10,... | collective-permute-start | bytes 294920 | tf_op jit(solution)/shard_map/ppermute | solution.py:202
  9.4 5.2 %collective-permute-start.3 = (bf16[16,3072]{1,0:T(8,128)(2,1)S(1)}, bf16[16,3072]{1,0:T(8,128)(2,1)S(1)}, u32[]{:S(2)}, u32[]{:S(2)}) collective-permute-start(bf16[16,3072]{1,0:T(8,128)(2,1)S(1)} %convert_element_type.31), channel_id=1, source_target_pairs={{0,9},{1,2},{2,1},{3,10},{4,7},{5,12},{6,15},{7,4},{8,11},{9,0},{1... | collective-permute-start | bytes 294920 | tf_op jit(solution)/shard_map/ppermute | solution.py:202
  14.6 4.9 %collective-permute-start.4 = (bf16[16,3072]{1,0:T(8,128)(2,1)S(1)}, bf16[16,3072]{1,0:T(8,128)(2,1)S(1)}, u32[]{:S(2)}, u32[]{:S(2)}) collective-permute-start(bf16[16,3072]{1,0:T(8,128)(2,1)S(1)} %convert_element_type.33), channel_id=1, source_target_pairs={{0,5},{1,8},{2,11},{3,6},{4,13},{5,0},{6,3},{7,14},{8,1},{9,12},{1... | collective-permute-start | bytes 294920 | tf_op jit(solution)/shard_map/ppermute | solution.py:202
  19.5 4.7 %collective-permute-start.8 = (bf16[16,3072]{1,0:T(8,128)(2,1)S(1)}, bf16[16,3072]{1,0:T(8,128)(2,1)S(1)}, u32[]{:S(2)}, u32[]{:S(2)}) collective-permute-start(bf16[16,3072]{1,0:T(8,128)(2,1)S(1)} %add_convert_fusion.refs_0_), channel_id=1, source_target_pairs={{0,2},{1,5},{2,6},{3,1},{4,0},{5,7},{6,4},{7,3},{8,12},{9,11},{10,... | collective-permute-start | bytes 294920 | tf_op jit(solution)/shard_map/ppermute | solution.py:202
  20.9 3.3 %collective-permute-start.7 = (bf16[16,3072]{1,0:T(8,128)(2,1)S(1)}, bf16[16,3072]{1,0:T(8,128)(2,1)S(1)}, u32[]{:S(2)}, u32[]{:S(2)}) collective-permute-start(bf16[16,3072]{1,0:T(8,128)(2,1)S(1)} %add_convert_fusion.refs_0_), channel_id=1, source_target_pairs={{0,1},{1,0},{2,3},{3,2},{4,5},{5,4},{6,7},{7,6},{8,9},{9,8},{10,11... | collective-permute-start | bytes 294920 | tf_op jit(solution)/shard_map/ppermute | solution.py:202
  21.3 5.0 %collective-permute-start.5 = (bf16[16,3072]{1,0:T(8,128)(2,1)S(1)}, bf16[16,3072]{1,0:T(8,128)(2,1)S(1)}, u32[]{:S(2)}, u32[]{:S(2)}) collective-permute-start(bf16[16,3072]{1,0:T(8,128)(2,1)S(1)} %add_convert_fusion.refs_0_), channel_id=1, source_target_pairs={{0,3},{1,4},{2,7},{3,0},{4,1},{5,6},{6,5},{7,2},{8,13},{9,10},{10,... | collective-permute-start | bytes 294920 | tf_op jit(solution)/shard_map/ppermute | solution.py:202
  24.8 5.4 %collective-permute-start.9 = (bf16[3,48,384]{2,1,0:T(8,128)(2,1)S(1)}, bf16[3,48,384]{2,1,0:T(8,128)(2,1)S(1)}, u32[]{:S(2)}, u32[]{:S(2)}) collective-permute-start(bf16[3,48,384]{2,1,0:T(8,128)(2,1)S(1)} %others.3), channel_id=1, source_target_pairs={{0,16},{16,0},{1,17},{17,1},{2,18},{18,2},{3,19},{19,3},{4,20},{20... | collective-permute-start | bytes 331784 | tf_op jit(solution)/shard_map/ppermute | solution.py:240
  26.8 4.1 %collective-permute-start.6 = (bf16[3,16,384]{2,1,0:T(8,128)(2,1)S(1)}, bf16[3,16,384]{2,1,0:T(8,128)(2,1)S(1)}, u32[]{:S(2)}, u32[]{:S(2)}) collective-permute-start(bf16[3,16,384]{2,1,0:T(8,128)(2,1)S(1)} %others.2), channel_id=1, source_target_pairs={{0,16},{16,0},{1,17},{17,1},{2,18},{18,2},{3,19},{19,3},{4,20},{20... | collective-permute-start | bytes 110600 | tf_op jit(solution)/shard_map/ppermute | solution.py:240
